TPU v7x, 768 devices: a whole 4x8x12 slice. The times are simulated.
768 devices in a mesh: gx: 12 (over z_lo, x), gy: 64 (over z_hi, y, core).
Axes of the slice: x: 4, y: 8, z: 12 (z_hi: 4, z_lo: 3; z = z_hi * 3 + z_lo), core: 2. Of those that a mesh axis runs over, the one named last changes fastest.
Arguments:
- density: float32 [192, 512, 256], P('gx', 'gy'), may hold values from 0.05 to 1
- force: float32 [3, 192, 512, 256], P(None, 'gx', 'gy'), may hold values from -40 to 40
- brick_ids: int32 [12, 64, 512], P('gx', 'gy'), may hold values from 0 to 512, as said below
- offsets: int32 [14, 3], replicated, may hold values from -1 to 1, as said below
Outputs:
- displacement: float32 [3, 192, 512, 256], P(None, 'gx', 'gy')
- sensitivity: float32 [192, 512, 256], P('gx', 'gy')
Inputs may be any that keep to these rules, and one draw needn't show every extreme that they name: `brick_ids`: each device's row lists the numbers of the solid bricks of its block, distinct and ascending, followed by the padding value 512 in the remaining slots; at least half of a block's bricks are solid and at least one slot is padding. `offsets`: 14 distinct rows (dx, dy, dz); the first row is (0, 0, 0).
All inputs are finite; a program needn't handle non-finite values.
Results may differ from a plain program's by a relative error of at most 0.0065.
Values sent between devices are 32-bit elements; how exact they have to be, the bound alone decides.
No kernel may reach another device: no remote copies, remote signals or barrier semaphores. Data moves between devices by JAX's collectives and lax.ppermute only.
A program may use at most 32 MiB of HBM per device.

v0:
```python
import jax
import jax.numpy as jnp
import numpy as np
from jax import lax
from jax.sharding import PartitionSpec as P

ITERS = 2


CUBE = np.array([[i // 9 - 1, i // 3 % 3 - 1, i % 3 - 1] for i in range(27)], dtype=np.int32)
REACH = np.sqrt((CUBE**2).sum(axis=1)).astype(np.float32)
GAINS = np.where(np.eye(3) > 0, 2.0, 1.0).astype(np.float32)
EMIN = 0.001
RADIUS = 2.0


def padded_2(block, sides, width):
    for axis, dim in sides:
        count = lax.axis_size(axis)
        forward = [(i, i + 1) for i in range(count - 1)]
        backward = [(target, source) for source, target in forward]
        low = lax.ppermute(
            lax.slice_in_dim(block, block.shape[dim] - width, None, axis=dim), axis, forward
        )
        high = lax.ppermute(lax.slice_in_dim(block, 0, width, axis=dim), axis, backward)
        block = jnp.concatenate([low, block, high], axis=dim)
    return block


def stencil_weights(offsets):
    match = jnp.all(offsets[None, :, :] == jnp.asarray(CUBE)[:, None, :], axis=2)
    chosen = jnp.any(match, axis=1)
    return jnp.where(chosen, RADIUS - jnp.asarray(REACH), 0.0).astype(jnp.float32)


def apply_filter(padded, weights, sign):
    sizes = [padded.shape[a] - 2 for a in range(3)]
    total = jnp.zeros(sizes, padded.dtype)
    for index in range(27):
        begin = [1 + int(CUBE[index, a]) * sign for a in range(3)]
        piece = padded[
            begin[0] : begin[0] + sizes[0],
            begin[1] : begin[1] + sizes[1],
            begin[2] : begin[2] + sizes[2],
        ]
        total = total + weights[index] * piece
    return total


def interior(padded):
    return padded[..., 1:-1, 1:-1, 1:-1]


def neighbours(padded):
    return [
        (padded[..., 2:, 1:-1, 1:-1], padded[..., :-2, 1:-1, 1:-1]),
        (padded[..., 1:-1, 2:, 1:-1], padded[..., 1:-1, :-2, 1:-1]),
        (padded[..., 1:-1, 1:-1, 2:], padded[..., 1:-1, 1:-1, :-2]),
    ]


def face_couplings(stiff_pad):
    centre = interior(stiff_pad)
    return [
        (0.5 * (centre + upper), 0.5 * (centre + lower)) for upper, lower in neighbours(stiff_pad)
    ]


def apply_operator(padded, couplings):
    centre = interior(padded)
    total = jnp.zeros_like(centre)
    for index, pair in enumerate(neighbours(padded)):
        gain = jnp.asarray(GAINS[:, index]).reshape(3, 1, 1, 1)
        upper_c, lower_c = couplings[index]
        total = total + gain * (upper_c * (centre - pair[0]) + lower_c * (centre - pair[1]))
    return total


def strain_energy(padded):
    centre = interior(padded)
    total = jnp.zeros_like(centre)
    for index, pair in enumerate(neighbours(padded)):
        gain = jnp.asarray(GAINS[:, index]).reshape(3, 1, 1, 1)
        total = total + gain * ((centre - pair[0]) ** 2 + (centre - pair[1]) ** 2)
    return 0.5 * jnp.sum(total, axis=0)


def device_mask(brick_ids, rows_x, rows_y, depth):
    slots = brick_ids.shape[2]
    flags = jnp.zeros((slots + 1,), jnp.float32).at[brick_ids.reshape(slots)].set(1.0)[:slots]
    flags = flags.reshape(rows_x // 4, 1, rows_y // 4, 1, depth // 4, 1)
    cells = jnp.broadcast_to(flags, (rows_x // 4, 4, rows_y // 4, 4, depth // 4, 4))
    return cells.reshape(rows_x, rows_y, depth)


def inside_cells(rows_x, rows_y, depth, width):
    shape = (rows_x + 2 * width, rows_y + 2 * width, depth + 2)
    plane_x = lax.broadcasted_iota(jnp.int32, shape, 0)
    plane_y = lax.broadcasted_iota(jnp.int32, shape, 1)
    plane_z = lax.broadcasted_iota(jnp.int32, shape, 2)
    where_x = lax.axis_index("gx")
    where_y = lax.axis_index("gy")
    inside = ((plane_x >= width) | (where_x > 0)) & (
        (plane_x < rows_x + width) | (where_x < lax.axis_size("gx") - 1)
    )
    inside = (
        inside
        & ((plane_y >= width) | (where_y > 0))
        & ((plane_y < rows_y + width) | (where_y < lax.axis_size("gy") - 1))
    )
    inside = inside & (plane_z > 0) & (plane_z < depth + 1)
    return inside.astype(jnp.float32)


def rim_scalar(field):
    widened = padded_2(field, (("gx", 0), ("gy", 1)), 1)
    return jnp.pad(widened, ((0, 0), (0, 0), (1, 1)))


def rim_motion(field):
    widened = padded_2(field, (("gx", 1), ("gy", 2)), 1)
    return jnp.pad(widened, ((0, 0), (0, 0), (0, 0), (1, 1)))


def squared_norm(residual):
    return lax.psum(jnp.sum(residual * residual), ("gx", "gy"))


def body(density, force, brick_ids, offsets):
    rows_x, rows_y, depth = density.shape
    weights = stencil_weights(offsets)
    solid_mask = device_mask(brick_ids, rows_x, rows_y, depth)
    weight_total = apply_filter(inside_cells(rows_x, rows_y, depth, 1), weights, 1)
    smooth = apply_filter(rim_scalar(density), weights, 1) / weight_total
    stiffness = EMIN + solid_mask * smooth**3 * (1.0 - EMIN)
    couplings = face_couplings(rim_scalar(stiffness))
    motion = jnp.zeros_like(force)
    residual = force
    direction = force
    norm_now = squared_norm(residual)
    for step in range(ITERS):
        image = apply_operator(rim_motion(direction), couplings)
        step_size = norm_now / lax.psum(jnp.sum(direction * image), ("gx", "gy"))
        motion = motion + step_size * direction
        residual = residual - step_size * image
        if step + 1 < ITERS:
            norm_next = squared_norm(residual)
            direction = residual + norm_next / norm_now * direction
            norm_now = norm_next
    motion_rim = rim_motion(motion)
    energy = strain_energy(motion_rim)
    share_term = -3.0 * (1.0 - EMIN) * solid_mask * smooth**2 * energy / weight_total
    widened = padded_2(share_term, (("gx", 0), ("gy", 1)), 1)
    sensitivity = apply_filter(jnp.pad(widened, ((0, 0), (0, 0), (1, 1))), weights, -1)
    return (motion, sensitivity)


def solution(mesh):
    return jax.shard_map(
        body,
        mesh=mesh,
        in_specs=(P("gx", "gy", None), P(None, "gx", "gy", None), P("gx", "gy", None), P()),
        out_specs=(P(None, "gx", "gy", None), P("gx", "gy", None)),
        check_vma=False,
    )
```

profile of v0, /device:TPU:63, one launch (start us, length us, event | category | flops | bytes accessed | tf_op | source)
XLA Modules:
  0.0 531.9 jit_solution(12858641658603077345)
XLA Ops:
  0.6 0.7 fusion.179
  1.3 3.9 collective-permute-start
  5.3 1.9 collective-permute-start.1
  7.2 0.8 fusion.175
  8.0 5.5 %collective-permute-start.7 = (f32[3,1,8,256]{3,2,1,0:T(8,128)S(1)}, f32[3,1,8,256]{3,2,1,0:T(8,128)S(1)}, u32[]{:S(2)}, u32[]{:S(2)}) collective-permute-start(f32[3,1,8,256]{3,2,1,0:T(8,128)S(1)} %get-tuple-element.23), channel_id=1, source_target_pairs={{0,64},{64,128},{128,192},{192,256},{256,320},{320,384},{384,448},... | collective-permute-start | bytes 73736 | tf_op jit(solution)/shard_map/ppermute | solution.py:22
  13.4 1.9 collective-permute-start.5
  15.4 0.8 compare_reduce_fusion
  16.2 0.7 broadcast_select_fusion
  16.8 0.7 fusion.180
  17.6 0.7 compare_select_fusion
  18.3 0.1 and_convert_fusion
  18.4 0.7 fusion.181
  19.1 2.4 scatter_custom_fusion
  21.6 0.1 broadcast_in_dim.14
  21.7 2.5 broadcast_in_dim.15
  24.2 5.0 reshape.67
  29.3 10.6 %collective-permute-start.2 = (f32[18,1,256]{2,1,0:T(1,128)S(1)}, f32[18,1,256]{2,1,0:T(1,128)S(1)}, u32[]{:S(2)}, u32[]{:S(2)}) collective-permute-start(f32[18,1,256]{2,1,0:T(1,128)S(1)} %get-tuple-element.32), channel_id=1, source_target_pairs={{0,1},{1,2},{2,3},{3,4},{4,5},{5,6},{6,7},{7,8},{8,9},{9,10},{10,1... | collective-permute-start | bytes 55304 | tf_op jit(solution)/shard_map/ppermute | solution.py:22
  39.9 1.9 collective-permute-start.3
  42.0 7.0 %collective-permute-done.3 = f32[18,1,256]{2,1,0:T(1,128)S(1)} collective-permute-done((f32[18,1,256]{2,1,0:T(1,128)S(1)}, f32[18,1,256]{2,1,0:T(1,128)S(1)}, u32[]{:S(2)}, u32[]{:S(2)}) %collective-permute-start.3) | collective-permute-done | bytes 18464 | tf_op jit(solution)/shard_map/ppermute | solution.py:25
  48.9 0.3 select_maximum_fusion.18
  49.2 18.0 %fusion.61 = (f32[16,8,256]{2,1,0:T(8,128)S(1)}, f32[16,8,256]{2,1,0:T(8,128)S(1)}, f32[16,8,256]{2,1,0:T(8,128)S(1)}) fusion(f32[16,8,256]{2,1,0:T(8,128)S(1)} %reshape.67, f32[18,10,258]{2,1,0:T(8,128)S(1)} %select_maximum_fusion.18, f32[]{:T(128)} %bitcast.28, f32[18,1,256]{2,1,0:T(1,128)S(1)} %collective-permute-done.3, ...), kind=kLoop, calls=%fused_computation.131 | loop fusion | flops 3932160 | bytes 6754412 | tf_op jit(solution)/shard_map/add | solution.py:135
  67.2 1.9 collective-permute-start.4
  69.2 8.2 %collective-permute-start.6 = (f32[1,8,256]{2,1,0:T(8,128)S(1)}, f32[1,8,256]{2,1,0:T(8,128)S(1)}, u32[]{:S(2)}, u32[]{:S(2)}) collective-permute-start(f32[1,8,256]{2,1,0:T(8,128)S(1)} %get-tuple-element.40), channel_id=1, source_target_pairs={{0,64},{64,128},{128,192},{192,256},{256,320},{320,384},{384,448},... | collective-permute-start | bytes 24584 | tf_op jit(solution)/shard_map/ppermute | solution.py:22
  77.4 0.7 collective-permute-done.6
  78.2 2.8 collective-permute-start.10
  80.9 1.9 collective-permute-start.8
  83.0 7.5 %collective-permute-start.11 = (f32[3,18,1,256]{3,2,1,0:T(1,128)S(1)}, f32[3,18,1,256]{3,2,1,0:T(1,128)S(1)}, u32[]{:S(2)}, u32[]{:S(2)}) collective-permute-start(f32[3,18,1,256]{3,2,1,0:T(1,128)S(1)} %get-tuple-element.16), channel_id=1, source_target_pairs={{0,1},{1,2},{2,3},{3,4},{4,5},{5,6},{6,7},{7,8},{8,9},{9,10},{10,1... | collective-permute-start | bytes 165896 | tf_op jit(solution)/shard_map/ppermute | solution.py:22
  90.5 1.9 collective-permute-start.9
  92.5 0.3 select_maximum_fusion.14
  92.8 0.1 fusion.132
  92.9 7.5 %collective-permute-done.9 = f32[3,18,1,256]{3,2,1,0:T(1,128)S(1)} collective-permute-done((f32[3,18,1,256]{3,2,1,0:T(1,128)S(1)}, f32[3,18,1,256]{3,2,1,0:T(1,128)S(1)}, u32[]{:S(2)}, u32[]{:S(2)}) %collective-permute-start.9) | collective-permute-done | bytes 55328 | tf_op jit(solution)/shard_map/ppermute | solution.py:25
  100.5 0.8 select_maximum_fusion.8
  101.4 1.1 multiply_reduce_fusion.1
  102.5 111.2 %all-reduce.6 = (f32[]{:T(128)}, f32[]{:T(128)}) all-reduce(f32[]{:T(128)} %get-tuple-element.3, f32[]{:T(128)} %get-tuple-element.2), channel_id=1, replica_groups=mesh['gx'=12,'gy'=64] {'gx','gy'}, use_global_device_ids=true, to_apply=%region_1.0 | all-reduce | flops 2 | bytes 16 | tf_op jit(solution)/shard_map/psum | solution.py:126
  215.0 0.7 multiply_reduce_fusion
  215.7 103.7 %psum.30 = f32[]{:T(128)} all-reduce(f32[]{:T(128)} %multiply_reduce_fusion), channel_id=1, replica_groups=mesh['gx'=12,'gy'=64] {'gx','gy'}, use_global_device_ids=true, to_apply=%region_8.9 | all-reduce | flops 1 | bytes 8 | tf_op jit(solution)/shard_map/psum | solution.py:126
  320.8 1.9 collective-permute-start.12
  322.7 5.5 %collective-permute-start.13 = (f32[3,1,8,256]{3,2,1,0:T(8,128)S(1)}, f32[3,1,8,256]{3,2,1,0:T(8,128)S(1)}, u32[]{:S(2)}, u32[]{:S(2)}) collective-permute-start(f32[3,1,8,256]{3,2,1,0:T(8,128)S(1)} %get-tuple-element.20), channel_id=1, source_target_pairs={{0,64},{64,128},{128,192},{192,256},{256,320},{320,384},{384,448},... | collective-permute-start | bytes 73736 | tf_op jit(solution)/shard_map/ppermute | solution.py:22
  328.2 0.9 collective-permute-done.13
  329.2 2.9 collective-permute-start.14
  332.2 9.7 %collective-permute-start.15 = (f32[3,18,1,256]{3,2,1,0:T(1,128)S(1)}, f32[3,18,1,256]{3,2,1,0:T(1,128)S(1)}, u32[]{:S(2)}, u32[]{:S(2)}) collective-permute-start(f32[3,18,1,256]{3,2,1,0:T(1,128)S(1)} %get-tuple-element.14), channel_id=1, source_target_pairs={{0,1},{1,2},{2,3},{3,4},{4,5},{5,6},{6,7},{7,8},{8,9},{9,10},{10,1... | collective-permute-start | bytes 165896 | tf_op jit(solution)/shard_map/ppermute | solution.py:22
  341.9 0.6 collective-permute-done.14
  342.5 0.6 collective-permute-done.15
  343.1 0.8 select_maximum_fusion.4
  343.9 1.1 fusion.26
  345.0 107.8 %psum.31 = f32[]{:T(128)} all-reduce(f32[]{:T(128)} %fusion.26), channel_id=1, replica_groups=mesh['gx'=12,'gy'=64] {'gx','gy'}, use_global_device_ids=true, to_apply=%region_10.11 | all-reduce | flops 1 | bytes 8 | tf_op jit(solution)/shard_map/psum | solution.py:143
  454.3 1.9 collective-permute-start.16
  456.2 5.5 %collective-permute-start.17 = (f32[3,1,8,256]{3,2,1,0:T(8,128)S(1)}, f32[3,1,8,256]{3,2,1,0:T(8,128)S(1)}, u32[]{:S(2)}, u32[]{:S(2)}) collective-permute-start(f32[3,1,8,256]{3,2,1,0:T(8,128)S(1)} %get-tuple-element.18), channel_id=1, source_target_pairs={{0,64},{64,128},{128,192},{192,256},{256,320},{320,384},{384,448},... | collective-permute-start | bytes 73736 | tf_op jit(solution)/shard_map/ppermute | solution.py:22
  461.7 0.9 collective-permute-done.17
  462.6 0.1 pad_maximum_fusion.35
  462.7 2.9 collective-permute-start.18
  465.7 10.5 %collective-permute-start.19 = (f32[3,18,1,256]{3,2,1,0:T(1,128)S(1)}, f32[3,18,1,256]{3,2,1,0:T(1,128)S(1)}, u32[]{:S(2)}, u32[]{:S(2)}) collective-permute-start(f32[3,18,1,256]{3,2,1,0:T(1,128)S(1)} %get-tuple-element.12), channel_id=1, source_target_pairs={{0,1},{1,2},{2,3},{3,4},{4,5},{5,6},{6,7},{7,8},{8,9},{9,10},{10,1... | collective-permute-start | bytes 165896 | tf_op jit(solution)/shard_map/ppermute | solution.py:22
  476.1 0.3 collective-permute-done.18
  476.5 0.7 collective-permute-done.19
  477.2 0.8 select_maximum_fusion
  478.0 0.5 fusion.6
  478.6 7.3 %collective-permute-start.20 = (f32[1,8,256]{2,1,0:T(8,128)S(1)}, f32[1,8,256]{2,1,0:T(8,128)S(1)}, u32[]{:S(2)}, u32[]{:S(2)}) collective-permute-start(f32[1,8,256]{2,1,0:T(8,128)S(1)} %get-tuple-element.38), channel_id=1, source_target_pairs={{0,64},{64,128},{128,192},{192,256},{256,320},{320,384},{384,448},... | collective-permute-start | bytes 24584 | tf_op jit(solution)/shard_map/ppermute | solution.py:22
  485.8 1.9 collective-permute-start.21
  487.8 4.6 collective-permute-done.21
  492.4 12.0 %collective-permute-start.22 = (f32[18,1,256]{2,1,0:T(1,128)S(1)}, f32[18,1,256]{2,1,0:T(1,128)S(1)}, u32[]{:S(2)}, u32[]{:S(2)}) collective-permute-start(f32[18,1,256]{2,1,0:T(1,128)S(1)} %get-tuple-element.26), channel_id=1, source_target_pairs={{0,1},{1,2},{2,3},{3,4},{4,5},{5,6},{6,7},{7,8},{8,9},{9,10},{10,1... | collective-permute-start | bytes 55304 | tf_op jit(solution)/shard_map/ppermute | solution.py:22
  504.4 1.9 collective-permute-start.23
  506.3 7.0 %collective-permute-done.23 = f32[18,1,256]{2,1,0:T(1,128)S(1)} collective-permute-done((f32[18,1,256]{2,1,0:T(1,128)S(1)}, f32[18,1,256]{2,1,0:T(1,128)S(1)}, u32[]{:S(2)}, u32[]{:S(2)}) %collective-permute-start.23) | collective-permute-done | bytes 18464 | tf_op jit(solution)/shard_map/ppermute | solution.py:25
  513.5 0.3 select_maximum_fusion.10
  513.8 18.1 %fusion.99 = f32[16,8,256]{2,1,0:T(8,128)} fusion(f32[18,10,258]{2,1,0:T(8,128)S(1)} %select_maximum_fusion.10, f32[18,9,256]{2,1,0:T(8,128)S(1)} %get-tuple-element.25, f32[16,8,256]{2,1,0:T(8,128)S(1)} %fusion.63, f32[1,8,256]{2,1,0:T(8,128)S(1)} %collective-permute-done.20, f32[18,9,256]{2,1,0:T(8,128)S(1)} %get-tuple-element.24, ...), kind=kLoop, calls=%fused_computation.170 | loop fusion | flops 1802240 | bytes 3424364 | tf_op jit(solution)/shard_map/add | solution.py:46
  (50 shorter events, 0.6 us)
Async XLA Ops:
  1.3 27.8 %collective-permute-start = (f32[1,8,256]{2,1,0:T(8,128)S(1)}, f32[1,8,256]{2,1,0:T(8,128)S(1)}, u32[]{:S(2)}, u32[]{:S(2)}) collective-permute-start(f32[1,8,256]{2,1,0:T(8,128)S(1)} %get-tuple-element.43), channel_id=1, source_target_pairs={{0,64},{64,128},{128,192},{192,256},{256,320},{320,384},{384,448},... | collective-permute-start | bytes 24584 | tf_op jit(solution)/shard_map/ppermute | solution.py:22
  5.3 24.0 %collective-permute-start.1 = (f32[1,8,256]{2,1,0:T(8,128)S(1)}, f32[1,8,256]{2,1,0:T(8,128)S(1)}, u32[]{:S(2)}, u32[]{:S(2)}) collective-permute-start(f32[1,8,256]{2,1,0:T(8,128)S(1)} %get-tuple-element.42), channel_id=1, source_target_pairs={{64,0},{128,64},{192,128},{256,192},{320,256},{384,320},{448,384},... | collective-permute-start | bytes 24584 | tf_op jit(solution)/shard_map/ppermute | solution.py:25
  8.0 33.9 %collective-permute-start.7 = (f32[3,1,8,256]{3,2,1,0:T(8,128)S(1)}, f32[3,1,8,256]{3,2,1,0:T(8,128)S(1)}, u32[]{:S(2)}, u32[]{:S(2)}) collective-permute-start(f32[3,1,8,256]{3,2,1,0:T(8,128)S(1)} %get-tuple-element.23), channel_id=1, source_target_pairs={{0,64},{64,128},{128,192},{192,256},{256,320},{320,384},{384,448},... | collective-permute-start | bytes 73736 | tf_op jit(solution)/shard_map/ppermute | solution.py:22
  13.4 63.9 %collective-permute-start.5 = (f32[3,1,8,256]{3,2,1,0:T(8,128)S(1)}, f32[3,1,8,256]{3,2,1,0:T(8,128)S(1)}, u32[]{:S(2)}, u32[]{:S(2)}) collective-permute-start(f32[3,1,8,256]{3,2,1,0:T(8,128)S(1)} %get-tuple-element.22), channel_id=1, source_target_pairs={{64,0},{128,64},{192,128},{256,192},{320,256},{384,320},{448,384},... | collective-permute-start | bytes 73736 | tf_op jit(solution)/shard_map/ppermute | solution.py:25
  24.2 5.0 copy-start.2
  24.2 17.7 %copy-start = (f32[3,16,8,256]{3,2,1,0:T(8,128)S(1)}, f32[3,16,8,256]{3,2,1,0:T(8,128)}, u32[]{:S(2)}) copy-start(f32[3,16,8,256]{3,2,1,0:T(8,128)} %param.16) | copy-start | bytes 1179652
  29.3 12.7 %collective-permute-start.2 = (f32[18,1,256]{2,1,0:T(1,128)S(1)}, f32[18,1,256]{2,1,0:T(1,128)S(1)}, u32[]{:S(2)}, u32[]{:S(2)}) collective-permute-start(f32[18,1,256]{2,1,0:T(1,128)S(1)} %get-tuple-element.32), channel_id=1, source_target_pairs={{0,1},{1,2},{2,3},{3,4},{4,5},{5,6},{6,7},{7,8},{8,9},{9,10},{10,1... | collective-permute-start | bytes 55304 | tf_op jit(solution)/shard_map/ppermute | solution.py:22
  39.9 9.0 %collective-permute-start.3 = (f32[18,1,256]{2,1,0:T(1,128)S(1)}, f32[18,1,256]{2,1,0:T(1,128)S(1)}, u32[]{:S(2)}, u32[]{:S(2)}) collective-permute-start(f32[18,1,256]{2,1,0:T(1,128)S(1)} %get-tuple-element.33), channel_id=1, source_target_pairs={{1,0},{2,1},{3,2},{4,3},{5,4},{6,5},{7,6},{8,7},{9,8},{10,9},{11,1... | collective-permute-start | bytes 55304 | tf_op jit(solution)/shard_map/ppermute | solution.py:25
  67.2 10.1 %collective-permute-start.4 = (f32[1,8,256]{2,1,0:T(8,128)S(1)}, f32[1,8,256]{2,1,0:T(8,128)S(1)}, u32[]{:S(2)}, u32[]{:S(2)}) collective-permute-start(f32[1,8,256]{2,1,0:T(8,128)S(1)} %get-tuple-element.41), channel_id=1, source_target_pairs={{64,0},{128,64},{192,128},{256,192},{320,256},{384,320},{448,384},... | collective-permute-start | bytes 24584 | tf_op jit(solution)/shard_map/ppermute | solution.py:25
  69.2 9.0 %collective-permute-start.6 = (f32[1,8,256]{2,1,0:T(8,128)S(1)}, f32[1,8,256]{2,1,0:T(8,128)S(1)}, u32[]{:S(2)}, u32[]{:S(2)}) collective-permute-start(f32[1,8,256]{2,1,0:T(8,128)S(1)} %get-tuple-element.40), channel_id=1, source_target_pairs={{0,64},{64,128},{128,192},{192,256},{256,320},{320,384},{384,448},... | collective-permute-start | bytes 24584 | tf_op jit(solution)/shard_map/ppermute | solution.py:22
  78.2 14.3 %collective-permute-start.10 = (f32[18,1,256]{2,1,0:T(1,128)S(1)}, f32[18,1,256]{2,1,0:T(1,128)S(1)}, u32[]{:S(2)}, u32[]{:S(2)}) collective-permute-start(f32[18,1,256]{2,1,0:T(1,128)S(1)} %get-tuple-element.30), channel_id=1, source_target_pairs={{0,1},{1,2},{2,3},{3,4},{4,5},{5,6},{6,7},{7,8},{8,9},{9,10},{10,1... | collective-permute-start | bytes 55304 | tf_op jit(solution)/shard_map/ppermute | solution.py:22
  80.9 11.5 %collective-permute-start.8 = (f32[18,1,256]{2,1,0:T(1,128)S(1)}, f32[18,1,256]{2,1,0:T(1,128)S(1)}, u32[]{:S(2)}, u32[]{:S(2)}) collective-permute-start(f32[18,1,256]{2,1,0:T(1,128)S(1)} %get-tuple-element.31), channel_id=1, source_target_pairs={{1,0},{2,1},{3,2},{4,3},{5,4},{6,5},{7,6},{8,7},{9,8},{10,9},{11,1... | collective-permute-start | bytes 55304 | tf_op jit(solution)/shard_map/ppermute | solution.py:25
  83.0 10.0 %collective-permute-start.11 = (f32[3,18,1,256]{3,2,1,0:T(1,128)S(1)}, f32[3,18,1,256]{3,2,1,0:T(1,128)S(1)}, u32[]{:S(2)}, u32[]{:S(2)}) collective-permute-start(f32[3,18,1,256]{3,2,1,0:T(1,128)S(1)} %get-tuple-element.16), channel_id=1, source_target_pairs={{0,1},{1,2},{2,3},{3,4},{4,5},{5,6},{6,7},{7,8},{8,9},{9,10},{10,1... | collective-permute-start | bytes 165896 | tf_op jit(solution)/shard_map/ppermute | solution.py:22
  90.5 10.0 %collective-permute-start.9 = (f32[3,18,1,256]{3,2,1,0:T(1,128)S(1)}, f32[3,18,1,256]{3,2,1,0:T(1,128)S(1)}, u32[]{:S(2)}, u32[]{:S(2)}) collective-permute-start(f32[3,18,1,256]{3,2,1,0:T(1,128)S(1)} %get-tuple-element.17), channel_id=1, source_target_pairs={{1,0},{2,1},{3,2},{4,3},{5,4},{6,5},{7,6},{8,7},{9,8},{10,9},{11,1... | collective-permute-start | bytes 165896 | tf_op jit(solution)/shard_map/ppermute | solution.py:25
  92.8 8.6 %copy-start.3 = (f32[3]{0:T(128)S(1)}, f32[3]{0:T(128)}, u32[]{:S(2)}) copy-start(f32[3]{0:T(128)} %constant.58.clone) | copy-start | bytes 40
  92.8 8.6 %copy-start.4 = (f32[3]{0:T(128)S(1)}, f32[3]{0:T(128)}, u32[]{:S(2)}) copy-start(f32[3]{0:T(128)} %constant.59.clone) | copy-start | bytes 40
  92.8 8.6 %copy-start.5 = (f32[3]{0:T(128)S(1)}, f32[3]{0:T(128)}, u32[]{:S(2)}) copy-start(f32[3]{0:T(128)} %constant.60.clone) | copy-start | bytes 40
  320.8 7.4 %collective-permute-start.12 = (f32[3,1,8,256]{3,2,1,0:T(8,128)S(1)}, f32[3,1,8,256]{3,2,1,0:T(8,128)S(1)}, u32[]{:S(2)}, u32[]{:S(2)}) collective-permute-start(f32[3,1,8,256]{3,2,1,0:T(8,128)S(1)} %get-tuple-element.21), channel_id=1, source_target_pairs={{64,0},{128,64},{192,128},{256,192},{320,256},{384,320},{448,384},... | collective-permute-start | bytes 73736 | tf_op jit(solution)/shard_map/ppermute | solution.py:25
  322.7 6.4 %collective-permute-start.13 = (f32[3,1,8,256]{3,2,1,0:T(8,128)S(1)}, f32[3,1,8,256]{3,2,1,0:T(8,128)S(1)}, u32[]{:S(2)}, u32[]{:S(2)}) collective-permute-start(f32[3,1,8,256]{3,2,1,0:T(8,128)S(1)} %get-tuple-element.20), channel_id=1, source_target_pairs={{0,64},{64,128},{128,192},{192,256},{256,320},{320,384},{384,448},... | collective-permute-start | bytes 73736 | tf_op jit(solution)/shard_map/ppermute | solution.py:22
  329.2 13.2 %collective-permute-start.14 = (f32[3,18,1,256]{3,2,1,0:T(1,128)S(1)}, f32[3,18,1,256]{3,2,1,0:T(1,128)S(1)}, u32[]{:S(2)}, u32[]{:S(2)}) collective-permute-start(f32[3,18,1,256]{3,2,1,0:T(1,128)S(1)} %get-tuple-element.15), channel_id=1, source_target_pairs={{1,0},{2,1},{3,2},{4,3},{5,4},{6,5},{7,6},{8,7},{9,8},{10,9},{11,1... | collective-permute-start | bytes 165896 | tf_op jit(solution)/shard_map/ppermute | solution.py:25
  332.2 10.9 %collective-permute-start.15 = (f32[3,18,1,256]{3,2,1,0:T(1,128)S(1)}, f32[3,18,1,256]{3,2,1,0:T(1,128)S(1)}, u32[]{:S(2)}, u32[]{:S(2)}) collective-permute-start(f32[3,18,1,256]{3,2,1,0:T(1,128)S(1)} %get-tuple-element.14), channel_id=1, source_target_pairs={{0,1},{1,2},{2,3},{3,4},{4,5},{5,6},{6,7},{7,8},{8,9},{9,10},{10,1... | collective-permute-start | bytes 165896 | tf_op jit(solution)/shard_map/ppermute | solution.py:22
  454.3 24.2 %copy-start.1 = (f32[3,16,8,256]{3,2,1,0:T(8,128)}, f32[3,16,8,256]{3,2,1,0:T(8,128)S(1)}, u32[]{:S(2)}) copy-start(f32[3,16,8,256]{3,2,1,0:T(8,128)S(1)} %multiply_add_fusion) | copy-start | bytes 1179652
  454.3 7.4 %collective-permute-start.16 = (f32[3,1,8,256]{3,2,1,0:T(8,128)S(1)}, f32[3,1,8,256]{3,2,1,0:T(8,128)S(1)}, u32[]{:S(2)}, u32[]{:S(2)}) collective-permute-start(f32[3,1,8,256]{3,2,1,0:T(8,128)S(1)} %get-tuple-element.19), channel_id=1, source_target_pairs={{64,0},{128,64},{192,128},{256,192},{320,256},{384,320},{448,384},... | collective-permute-start | bytes 73736 | tf_op jit(solution)/shard_map/ppermute | solution.py:25
  456.2 6.4 %collective-permute-start.17 = (f32[3,1,8,256]{3,2,1,0:T(8,128)S(1)}, f32[3,1,8,256]{3,2,1,0:T(8,128)S(1)}, u32[]{:S(2)}, u32[]{:S(2)}) collective-permute-start(f32[3,1,8,256]{3,2,1,0:T(8,128)S(1)} %get-tuple-element.18), channel_id=1, source_target_pairs={{0,64},{64,128},{128,192},{192,256},{256,320},{320,384},{384,448},... | collective-permute-start | bytes 73736 | tf_op jit(solution)/shard_map/ppermute | solution.py:22
  462.7 13.8 %collective-permute-start.18 = (f32[3,18,1,256]{3,2,1,0:T(1,128)S(1)}, f32[3,18,1,256]{3,2,1,0:T(1,128)S(1)}, u32[]{:S(2)}, u32[]{:S(2)}) collective-permute-start(f32[3,18,1,256]{3,2,1,0:T(1,128)S(1)} %get-tuple-element.13), channel_id=1, source_target_pairs={{1,0},{2,1},{3,2},{4,3},{5,4},{6,5},{7,6},{8,7},{9,8},{10,9},{11,1... | collective-permute-start | bytes 165896 | tf_op jit(solution)/shard_map/ppermute | solution.py:25
  465.7 11.5 %collective-permute-start.19 = (f32[3,18,1,256]{3,2,1,0:T(1,128)S(1)}, f32[3,18,1,256]{3,2,1,0:T(1,128)S(1)}, u32[]{:S(2)}, u32[]{:S(2)}) collective-permute-start(f32[3,18,1,256]{3,2,1,0:T(1,128)S(1)} %get-tuple-element.12), channel_id=1, source_target_pairs={{0,1},{1,2},{2,3},{3,4},{4,5},{5,6},{6,7},{7,8},{8,9},{9,10},{10,1... | collective-permute-start | bytes 165896 | tf_op jit(solution)/shard_map/ppermute | solution.py:22
  478.6 9.2 %collective-permute-start.20 = (f32[1,8,256]{2,1,0:T(8,128)S(1)}, f32[1,8,256]{2,1,0:T(8,128)S(1)}, u32[]{:S(2)}, u32[]{:S(2)}) collective-permute-start(f32[1,8,256]{2,1,0:T(8,128)S(1)} %get-tuple-element.38), channel_id=1, source_target_pairs={{0,64},{64,128},{128,192},{192,256},{256,320},{320,384},{384,448},... | collective-permute-start | bytes 24584 | tf_op jit(solution)/shard_map/ppermute | solution.py:22
  485.8 6.5 %collective-permute-start.21 = (f32[1,8,256]{2,1,0:T(8,128)S(1)}, f32[1,8,256]{2,1,0:T(8,128)S(1)}, u32[]{:S(2)}, u32[]{:S(2)}) collective-permute-start(f32[1,8,256]{2,1,0:T(8,128)S(1)} %get-tuple-element.39), channel_id=1, source_target_pairs={{64,0},{128,64},{192,128},{256,192},{320,256},{384,320},{448,384},... | collective-permute-start | bytes 24584 | tf_op jit(solution)/shard_map/ppermute | solution.py:25
  492.4 14.0 %collective-permute-start.22 = (f32[18,1,256]{2,1,0:T(1,128)S(1)}, f32[18,1,256]{2,1,0:T(1,128)S(1)}, u32[]{:S(2)}, u32[]{:S(2)}) collective-permute-start(f32[18,1,256]{2,1,0:T(1,128)S(1)} %get-tuple-element.26), channel_id=1, source_target_pairs={{0,1},{1,2},{2,3},{3,4},{4,5},{5,6},{6,7},{7,8},{8,9},{9,10},{10,1... | collective-permute-start | bytes 55304 | tf_op jit(solution)/shard_map/ppermute | solution.py:22
  504.4 9.0 %collective-permute-start.23 = (f32[18,1,256]{2,1,0:T(1,128)S(1)}, f32[18,1,256]{2,1,0:T(1,128)S(1)}, u32[]{:S(2)}, u32[]{:S(2)}) collective-permute-start(f32[18,1,256]{2,1,0:T(1,128)S(1)} %get-tuple-element.27), channel_id=1, source_target_pairs={{1,0},{2,1},{3,2},{4,3},{5,4},{6,5},{7,6},{8,7},{9,8},{10,9},{11,1... | collective-permute-start | bytes 55304 | tf_op jit(solution)/shard_map/ppermute | solution.py:25
where the time goes:
time: 533 us; the launch traced here: 532 us
  blocking collectives  323 us (61%)
  starting transfers between devices  114 us (21%)
  other arithmetic  45.8 us (9%)
  waiting for transfers between devices  31 us (6%)
  local copies, waits for them, and re-layouts  13.1 us (2%)
    psum x2, blocking collectives, squared_norm(): return lax.psum(jnp.sum(residual * residual), ('gx', 'gy'))  215 us
    psum x1, blocking collectives, body(): step_size = norm_now / lax.psum(jnp.sum(direction * image), ('gx', 'gy'))  108 us
    ppermute x12, starting transfers between devices, padded_2(): lax.ppermute(lax.slice_in_dim(block, block.shape[dim] - width, None, axis...  88.9 us
    ppermute x12, waiting for transfers between devices, padded_2(): lax.ppermute(lax.slice_in_dim(block, 0, width, axis=dim), axis, backward)  27.1 us
    ppermute x12, starting transfers between devices, padded_2(): lax.ppermute(lax.slice_in_dim(block, 0, width, axis=dim), axis, backward)  25.1 us
    add x1, other arithmetic, apply_filter(): total = total + weights[index] * piece  18.1 us
    add x1, other arithmetic, body(): stiffness = EMIN + solid_mask * smooth ** 3 * (1.0 - EMIN)  18 us
  transfers between devices with their start and end apart: 24, of which 11 were waited for; matrix products, arithmetic and copies ran while one was open for 6% of the time, Pallas kernels for 0%

commit v1 on v0

v1 whole, which is shorter than its diff:
```python
import functools

import jax
import jax.numpy as jnp
import numpy as np
from jax import lax
from jax.experimental import pallas as pl
from jax.experimental.pallas import tpu as pltpu
from jax.sharding import Mesh
from jax.sharding import PartitionSpec as P

EMIN = 0.001
RADIUS = 2.0
REACH = [float(np.float32(RADIUS) - np.float32(np.sqrt(np.float32(s)))) for s in range(4)]

CX, CY, CZ = 16, 8, 256
NX, NY = 192, 512
ROWS = 16
F32 = jnp.float32


def sub_iota(rows):
    return lax.broadcasted_iota(jnp.int32, (rows, CZ), 0)


def lane_iota(rows):
    return lax.broadcasted_iota(jnp.int32, (rows, CZ), 1)


def roll(v, shift, axis):
    return pltpu.roll(v, shift % v.shape[axis], axis)


def yp(v):
    return roll(v, -1, 0)


def ym(v):
    return roll(v, 1, 0)


def zp(v, lane, fill=0.0):
    return jnp.where(lane == CZ - 1, fill, roll(v, -1, 1))


def zm(v, lane, fill=0.0):
    return jnp.where(lane == 0, fill, roll(v, 1, 1))


def pack_y_kernel(den_ref, f_ref, ids_ref, lo_ref, hi_ref, m_ref):
    ids = ids_ref[...]
    row = lax.shift_right_logical(ids, 6)
    col = lax.bitwise_and(ids, 63)
    p = (lax.broadcasted_iota(jnp.int32, (8, 512), 0) == row).astype(jnp.bfloat16)
    q = (
        lax.shift_right_logical(lax.broadcasted_iota(jnp.int32, (CZ, 512), 0), 2) == col
    ).astype(jnp.bfloat16)
    m_ref[...] = lax.dot_general(p, q, (((1,), (1,)), ((), ())), preferred_element_type=F32)
    sub = sub_iota(8)
    low = sub < 4

    def step(x, _):
        base = lax.shift_right_logical(x, 2) * 2
        den, f0, f1, f2 = den_ref[x], f_ref[0, x], f_ref[1, x], f_ref[2, x]
        f0r, f2r = roll(f0, 4, 0), roll(f2, 4, 0)
        lo_ref[x, 0:8] = jnp.where(sub == 7, m_ref[pl.ds(base, 1)], jnp.where(low, den, f0r))
        lo_ref[x, 8:16] = jnp.where(low, f1, f2r)
        hi_ref[x, 0:8] = jnp.where(sub == 0, m_ref[pl.ds(base + 1, 1)], jnp.where(low, f0r, den))
        hi_ref[x, 8:16] = jnp.where(low, f2r, f1)
        return 0

    lax.fori_loop(0, CX, step, 0, unroll=2)


def pack_x_kernel(den_ref, f_ref, m_ref, up_ref, dn_ref, bd_ref, bf_ref, lo_ref, hi_ref):
    sub = sub_iota(8)
    low = sub < 4

    def step(x, _):
        base = lax.shift_right_logical(x, 2) * 2
        u0, u1 = up_ref[x, 0:8], up_ref[x, 8:16]
        d0, d1 = dn_ref[x, 0:8], dn_ref[x, 8:16]
        bd_ref[x] = jnp.where(low, u0, d0)
        bf_ref[0, x] = roll(jnp.where(low, d0, u0), 4, 0)
        f1 = jnp.where(low, u1, d1)
        f1 = jnp.where(sub == 3, m_ref[pl.ds(base, 1)], f1)
        bf_ref[1, x] = jnp.where(sub == 4, m_ref[pl.ds(base + 1, 1)], f1)
        bf_ref[2, x] = roll(jnp.where(low, d1, u1), 4, 0)
        return 0

    lax.fori_loop(0, CX, step, 0, unroll=2)
    for slab, dx0, fx0 in ((lo_ref, 0, 0), (hi_ref, 12, 13)):
        for j in range(4):
            slab[j, 0:8] = den_ref[dx0 + j]
            slab[j, 8:16] = bd_ref[dx0 + j]
        for c in range(3):
            for j in range(3):
                slab[4 + 3 * c + j, 0:8] = f_ref[c, fx0 + j]
                slab[4 + 3 * c + j, 8:16] = bf_ref[c, fx0 + j]


def load_weights(off_ref, w_ref):
    for i in range(27):
        w_ref[i] = jnp.float32(0.0)
    for j in range(off_ref.shape[0]):
        dx, dy, dz = off_ref[j, 0], off_ref[j, 1], off_ref[j, 2]
        s = dx * dx + dy * dy + dz * dz
        w = jnp.where(
            s == 0,
            jnp.float32(REACH[0]),
            jnp.where(
                s == 1, jnp.float32(REACH[1]), jnp.where(s == 2, jnp.float32(REACH[2]), jnp.float32(REACH[3]))
            ),
        )
        w_ref[(dx + 1) * 9 + (dy + 1) * 3 + dz + 1] = w


def filter_plane(planes, w_ref, lane, sign):
    out = None
    for dz in (-1, 0, 1):
        acc = None
        for dy in (-1, 0, 1):
            t = None
            for dx in (-1, 0, 1):
                w = w_ref[(sign * dx + 1) * 9 + (sign * dy + 1) * 3 + sign * dz + 1]
                term = planes[dx + 1] * w
                t = term if t is None else t + term
            if dy == 1:
                t = yp(t)
            elif dy == -1:
                t = ym(t)
            acc = t if acc is None else acc + t
        if dz == 1:
            acc = zp(acc, lane)
        elif dz == -1:
            acc = zm(acc, lane)
        out = acc if out is None else out + acc
    return out


def image_plane(load, s_m, s_0, s_p, lane):
    px, mx = 0.5 * (s_0 + s_p), 0.5 * (s_0 + s_m)
    py = 0.5 * (s_0 + yp(s_0))
    pz = 0.5 * (s_0 + zp(s_0, lane))
    half = -0.5 * s_0
    outs = []
    for c in range(3):
        v = load(c, 0)
        fx = px * (v - load(c, 1)) + mx * (v - load(c, -1))
        fy = py * (v - yp(v))
        fy = fy - ym(fy)
        fz = pz * (v - zp(v, lane))
        fz = fz - zm(fz, lane, half * v)
        outs.append(fx + fy + fz + (fx, fy, fz)[c])
    return outs


def main_kernel(
    pos_ref, off_ref, den_ref, f_ref, bd_ref, bf_ref, xu_ref, xd_ref, ext_ref, g_ref, coef_ref, mom_ref,
    dext_ref, s_ref, rwt_ref, w_ref,
):
    gx, gy = pos_ref[0], pos_ref[1]
    load_weights(off_ref, w_ref)
    sub, lane = sub_iota(ROWS), lane_iota(ROWS)
    y = jnp.where(sub < 12, sub, sub - 16) + gy * CY

    def in_y(at):
        return ((at >= 0) & (at < NY)).astype(F32)

    iy = {dy: in_y(y + dy) for dy in (-1, 0, 1)}
    iz = {dz: ((lane + dz >= 0) & (lane + dz < CZ)).astype(F32) for dz in (-1, 0, 1)}

    for case, dxs in enumerate(((0, 1), (-1, 0, 1), (-1, 0))):
        total = jnp.zeros((ROWS, CZ), F32)
        for dy in (-1, 0, 1):
            part = jnp.zeros((ROWS, CZ), F32)
            for dz in (-1, 0, 1):
                w = w_ref[(dxs[0] + 1) * 9 + (dy + 1) * 3 + dz + 1]
                for dx in dxs[1:]:
                    w = w + w_ref[(dx + 1) * 9 + (dy + 1) * 3 + dz + 1]
                part = part + w * iz[dz]
            total = total + part * iy[dy]
        rwt_ref[case] = jnp.where(total > 0.0, iy[0] / jnp.where(total > 0.0, total, 1.0), 0.0)

    for j in range(4):
        dext_ref[j] = xd_ref[j]
        dext_ref[20 + j] = xu_ref[j]
    for c in range(3):
        for j in range(3):
            ext_ref[c, j] = xd_ref[4 + 3 * c + j]
            ext_ref[c, 19 + j] = xu_ref[4 + 3 * c + j]

    def spread(x, _):
        dext_ref[x + 4, 0:8] = den_ref[x]
        dext_ref[x + 4, 8:16] = bd_ref[x]
        for c in range(3):
            ext_ref[c, x + 3, 0:8] = f_ref[c, x]
            ext_ref[c, x + 3, 8:16] = bf_ref[c, x]
        return 0

    lax.fori_loop(0, CX, spread, 0, unroll=2)

    low_half = (sub_iota(8) < 4)

    def smooth_step(p, _):
        x = gx * CX + p - 3
        planes = [dext_ref[p], dext_ref[p + 1], dext_ref[p + 2]]
        num = filter_plane(planes, w_ref, lane, 1)
        case = jnp.where(x == 0, 0, jnp.where(x == NX - 1, 2, 1))
        in_x = jnp.where((x >= 0) & (x < NX), jnp.float32(1.0), jnp.float32(0.0))
        rwt = rwt_ref[case] * in_x
        smooth = num * rwt
        mask = jnp.concatenate(
            [
                jnp.where(low_half, ext_ref[1, p, 11:12], ext_ref[1, p, 12:13]),
                jnp.where(low_half, ext_ref[0, p, 11:12], ext_ref[0, p, 12:13]),
            ],
            axis=0,
        )
        sq = mask * (smooth * smooth)
        s_ref[p] = (iy[0] * in_x) * (EMIN + (sq * smooth) * (1.0 - EMIN))
        coef_ref[p] = (-3.0 * (1.0 - EMIN)) * sq * rwt
        return 0

    lax.fori_loop(0, CX + 6, smooth_step, 0)

    def image_step(q, _):
        x = gx * CX + q - 2
        in_x = jnp.where((x >= 0) & (x < NX), jnp.float32(1.0), jnp.float32(0.0))
        inside = iy[0] * in_x
        outs = image_plane(
            lambda c, k: ext_ref[c, q + 1 + k], s_ref[q], s_ref[q + 1], s_ref[q + 2], lane
        )
        for c in range(3):
            g_ref[c, q] = outs[c] * inside
        return 0

    lax.fori_loop(0, CX + 4, image_step, 0)

    def moment_step(x, sums):
        outs = image_plane(
            lambda c, k: g_ref[c, x + 2 + k], s_ref[x + 2], s_ref[x + 3], s_ref[x + 4], lane
        )
        m0, m1, m2, m3 = sums
        for c in range(3):
            f, g = f_ref[c, x], g_ref[c, x + 2, 0:8]
            m0, m1, m2, m3 = m0 + f * f, m1 + f * g, m2 + g * g, m3 + g * outs[c][0:8]
        return m0, m1, m2, m3

    zero = jnp.zeros((8, CZ), F32)
    sums = lax.fori_loop(0, CX, moment_step, (zero, zero, zero, zero))
    at = lax.broadcasted_iota(jnp.int32, (1, 128), 1)
    line = jnp.zeros((1, 128), F32)
    for k in range(4):
        total = jnp.sum(jnp.sum(sums[k], axis=0, keepdims=True), axis=1, keepdims=True)
        line = jnp.where(at == k, total, line)
    mom_ref[...] = line


def last_kernel(off_ref, ext_ref, g_ref, coef_ref, mom_ref, u_out, sens_out, u_ref, sh_ref, w_ref):
    load_weights(off_ref, w_ref)
    lane = lane_iota(ROWS)
    line = jnp.sum(mom_ref[...], axis=0, keepdims=True)
    at = lax.broadcasted_iota(jnp.int32, (1, 128), 1)
    m0, m1, m2, m3 = (
        jnp.sum(jnp.where(at == k, line, 0.0), axis=1, keepdims=True) for k in range(4)
    )
    s1 = m0 / m1
    rr = m0 - 2.0 * s1 * m1 + s1 * s1 * m2
    grow = 1.0 + rr / m0
    s2 = rr / (grow * grow * m1 - 2.0 * grow * s1 * m2 + s1 * s1 * m3)
    alpha = jnp.broadcast_to(s1 + s2 * grow, (ROWS, CZ))
    beta = jnp.broadcast_to(-s1 * s2, (ROWS, CZ))

    def u_step(q, _):
        for c in range(3):
            u_ref[c, q] = alpha * ext_ref[c, q + 1] + beta * g_ref[c, q]
        return 0

    lax.fori_loop(0, CX + 4, u_step, 0)

    def share_step(r, _):
        ex = ey = ez = e0 = None
        for c in range(3):
            v = u_ref[c, r + 1]
            ax, bx = v - u_ref[c, r + 2], v - u_ref[c, r]
            ay, az = v - yp(v), v - zp(v, lane)
            tx, ty, tz, t0 = ax * ax + bx * bx, ay * ay, az * az, v * v
            if c == 0:
                tx = tx + tx
            elif c == 1:
                ty = ty + ty
            else:
                tz, t0 = tz + tz, t0 + t0
            ex = tx if ex is None else ex + tx
            ey = ty if ey is None else ey + ty
            ez = tz if ez is None else ez + tz
            e0 = t0 if e0 is None else e0 + t0
        energy = 0.5 * (ex + (ey + ym(ey)) + (ez + zm(ez, lane, e0)))
        sh_ref[r] = coef_ref[r + 2] * energy
        return 0

    lax.fori_loop(0, CX + 2, share_step, 0)

    def out_step(x, _):
        planes = [sh_ref[x], sh_ref[x + 1], sh_ref[x + 2]]
        sens_out[x] = filter_plane(planes, w_ref, lane, -1)[0:8]
        for c in range(3):
            u_out[c, x] = u_ref[c, x + 2, 0:8]
        return 0

    lax.fori_loop(0, CX, out_step, 0)


VMEM = pl.BlockSpec(memory_space=pltpu.VMEM)
SMEM = pl.BlockSpec(memory_space=pltpu.SMEM)


def f32(*shape):
    return jax.ShapeDtypeStruct(shape, F32)


def call(kernel, outs, ins, scratch=()):
    return pl.pallas_call(
        kernel,
        out_shape=outs,
        in_specs=ins,
        out_specs=jax.tree.map(lambda _: VMEM, outs),
        scratch_shapes=list(scratch),
        compiler_params=pltpu.CompilerParams(vmem_limit_bytes=40 * 1024 * 1024),
    )


def swap(lo, hi, axes, count):
    up = lax.ppermute(lo, axes, [(i + 1, i) for i in range(count - 1)])
    down = lax.ppermute(hi, axes, [(i, i + 1) for i in range(count - 1)])
    return up, down


def spread_sum(line, axes, count):
    lines = jnp.broadcast_to(line, (count, 128))
    return lax.all_to_all(lines, axes, 0, 0, tiled=True)


def body(density, force, brick_ids, offsets):
    gx, gy = ("zl", "x"), ("zh", "y", "c")
    pos = jnp.stack([lax.axis_index(gx), lax.axis_index(gy)]).astype(jnp.int32)
    ids = brick_ids.reshape(1, 512)
    slab_y = f32(CX, ROWS, CZ)
    lo, hi, mask = call(pack_y_kernel, (slab_y, slab_y, f32(8, CZ)), [VMEM] * 3)(density, force, ids)
    up, down = swap(lo, hi, gy, 64)
    slab_x = f32(13, ROWS, CZ)
    bd, bf, lo, hi = call(
        pack_x_kernel, (f32(CX, 8, CZ), f32(3, CX, 8, CZ), slab_x, slab_x), [VMEM] * 5
    )(density, force, mask, up, down)
    up, down = swap(lo, hi, gx, 12)
    ext, image, coef, line = call(
        main_kernel,
        (f32(3, CX + 6, ROWS, CZ), f32(3, CX + 4, ROWS, CZ), f32(CX + 6, ROWS, CZ), f32(1, 128)),
        [SMEM, SMEM] + [VMEM] * 6,
        [
            pltpu.VMEM((CX + 8, ROWS, CZ), F32),
            pltpu.VMEM((CX + 6, ROWS, CZ), F32),
            pltpu.VMEM((3, ROWS, CZ), F32),
            pltpu.SMEM((27,), F32),
        ],
    )(pos, offsets, density, force, bd, bf, up, down)
    lines = spread_sum(line, ("x", "y"), 32)
    lines = spread_sum(jnp.sum(lines, axis=0, keepdims=True), ("zl", "zh", "c"), 24)
    return call(
        last_kernel,
        (f32(3, CX, CY, CZ), f32(CX, CY, CZ)),
        [SMEM] + [VMEM] * 4,
        [
            pltpu.VMEM((3, CX + 4, ROWS, CZ), F32),
            pltpu.VMEM((CX + 2, ROWS, CZ), F32),
            pltpu.SMEM((27,), F32),
        ],
    )(offsets, ext, image, coef, lines)


def solution(mesh):
    fine = Mesh(mesh.devices.reshape(3, 4, 4, 8, 2), ("zl", "x", "zh", "y", "c"))
    gx, gy = ("zl", "x"), ("zh", "y", "c")
    return jax.shard_map(
        body,
        mesh=fine,
        in_specs=(P(gx, gy, None), P(None, gx, gy, None), P(gx, gy, None), P()),
        out_specs=(P(None, gx, gy, None), P(gx, gy, None)),
        check_vma=False,
    )
```

time: 533 us -> 99.1 us (0.19)
  the two profiles are of different devices: /device:TPU:63 before, /device:TPU:1 now
where the time goes in v1:
time: 99.1 us; the launch traced here: 98.6 us
  blocking collectives  48 us (48%)
  starting transfers between devices  19.6 us (20%)
  Pallas kernels  15.7 us (16%)
  local copies, waits for them, and re-layouts  7.85 us (8%)
  waiting for transfers between devices  6.63 us (7%)
    all_to_all x2, blocking collectives, spread_sum(): return lax.all_to_all(lines, axes, 0, 0, tiled=True)  48 us
    ppermute x2, starting transfers between devices, swap(): up = lax.ppermute(lo, axes, [(i + 1, i) for i in range(count - 1)])  13.7 us
    pallas_call x1, Pallas kernels, body(): call(main_kernel, (f32(3, CX + 6, ROWS, CZ), f32(3, CX + 4, ROWS, CZ), f3...  9.23 us
    unnamed x25, local copies, waits for them, and re-layouts  7.83 us
    pallas_call x1, Pallas kernels, body(): call(last_kernel, (f32(3, CX, CY, CZ), f32(CX, CY, CZ)), [SMEM] + [VMEM]...  6.05 us
    ppermute x2, starting transfers between devices, swap(): down = lax.ppermute(hi, axes, [(i, i + 1) for i in range(count - 1)])  5.92 us
    ppermute x2, waiting for transfers between devices, swap(): down = lax.ppermute(hi, axes, [(i, i + 1) for i in range(count - 1)])  5.04 us
  transfers between devices with their start and end apart: 4, of which 3 were waited for; matrix products, arithmetic and copies ran while one was open for 1% of the time, Pallas kernels for 0%

profile of v1, /device:TPU:1, one launch (start us, length us, event | category | flops | bytes accessed | tf_op | source)
XLA Modules:
  0.0 98.6 jit_solution(6688600974577328937)
XLA Ops:
  0.6 0.0 copy-start
  0.6 1.0 %copy-done = f32[3,16,8,256]{3,2,1,0:T(8,128)S(1)} copy-done((f32[3,16,8,256]{3,2,1,0:T(8,128)S(1)}, f32[3,16,8,256]{3,2,1,0:T(8,128)}, u32[]{:S(2)}) %copy-start) | copy-done | bytes 393240
  1.6 0.0 copy-start.2
  1.6 0.9 copy-done.2
  2.5 0.0 copy-start.10
  2.5 0.7 copy-done.10
  3.2 0.0 copy-start.11
  3.2 0.0 copy-start.1
  3.2 0.0 copy-start.3
  3.2 0.3 shard_map.59
  3.5 12.4 %collective-permute-start = (f32[16,16,256]{2,1,0:T(8,128)S(1)}, f32[16,16,256]{2,1,0:T(8,128)S(1)}, u32[]{:S(2)}, u32[]{:S(2)}) collective-permute-start(f32[16,16,256]{2,1,0:T(8,128)S(1)} %get-tuple-element.14), channel_id=1, source_target_pairs={{1,0},{2,1},{3,2},{4,3},{5,4},{6,5},{7,6},{8,7},{9,8},{10,9},{11,1... | collective-permute-start | bytes 786440 | tf_op jit(solution)/shard_map/ppermute | solution.py:335
  16.0 1.9 %collective-permute-start.1 = (f32[16,16,256]{2,1,0:T(8,128)S(1)}, f32[16,16,256]{2,1,0:T(8,128)S(1)}, u32[]{:S(2)}, u32[]{:S(2)}) collective-permute-start(f32[16,16,256]{2,1,0:T(8,128)S(1)} %get-tuple-element.15), channel_id=1, source_target_pairs={{0,1},{1,2},{2,3},{3,4},{4,5},{5,6},{6,7},{7,8},{8,9},{9,10},{10,1... | collective-permute-start | bytes 786440 | tf_op jit(solution)/shard_map/ppermute | solution.py:336
  17.9 0.0 collective-permute-done.up_ref
  17.9 3.3 %collective-permute-done.1.dn_ref = f32[16,16,256]{2,1,0:T(8,128)S(1)} collective-permute-done((f32[16,16,256]{2,1,0:T(8,128)S(1)}, f32[16,16,256]{2,1,0:T(8,128)S(1)}, u32[]{:S(2)}, u32[]{:S(2)}) %collective-permute-start.1) | collective-permute-done | bytes 262176 | tf_op jit(solution)/shard_map/ppermute | solution.py:336
  21.2 0.1 shard_map.60
  21.3 0.0 copy-start.6
  21.3 0.6 copy-done.6
  22.0 1.3 %collective-permute-start.2 = (f32[13,16,256]{2,1,0:T(8,128)S(1)}, f32[13,16,256]{2,1,0:T(8,128)S(1)}, u32[]{:S(2)}, u32[]{:S(2)}) collective-permute-start(f32[13,16,256]{2,1,0:T(8,128)S(1)} %get-tuple-element.18), channel_id=1, source_target_pairs={{64,0},{128,64},{192,128},{256,192},{320,256},{384,320},{448,384},... | collective-permute-start | bytes 638984 | tf_op jit(solution)/shard_map/ppermute | solution.py:335
  23.3 4.0 %collective-permute-start.3 = (f32[13,16,256]{2,1,0:T(8,128)S(1)}, f32[13,16,256]{2,1,0:T(8,128)S(1)}, u32[]{:S(2)}, u32[]{:S(2)}) collective-permute-start(f32[13,16,256]{2,1,0:T(8,128)S(1)} %get-tuple-element.19), channel_id=1, source_target_pairs={{0,64},{64,128},{128,192},{192,256},{256,320},{320,384},{384,448},... | collective-permute-start | bytes 638984 | tf_op jit(solution)/shard_map/ppermute | solution.py:336
  27.3 0.0 copy-done.11
  27.3 0.7 copy.14.off_ref
  28.0 0.1 pad_add_fusion.pos_ref
  28.1 1.6 %collective-permute-done.2.xu_ref = f32[13,16,256]{2,1,0:T(8,128)S(1)} collective-permute-done((f32[13,16,256]{2,1,0:T(8,128)S(1)}, f32[13,16,256]{2,1,0:T(8,128)S(1)}, u32[]{:S(2)}, u32[]{:S(2)}) %collective-permute-start.2) | collective-permute-done | bytes 213024 | tf_op jit(solution)/shard_map/ppermute | solution.py:335
  29.6 1.8 %collective-permute-done.3.xd_ref = f32[13,16,256]{2,1,0:T(8,128)S(1)} collective-permute-done((f32[13,16,256]{2,1,0:T(8,128)S(1)}, f32[13,16,256]{2,1,0:T(8,128)S(1)}, u32[]{:S(2)}, u32[]{:S(2)}) %collective-permute-start.3) | collective-permute-done | bytes 213024 | tf_op jit(solution)/shard_map/ppermute | solution.py:336
  31.4 0.0 copy-start.4
  31.4 0.7 copy-done.4
  32.1 0.0 copy-done.1
  32.1 0.0 copy-done.3
  32.1 0.0 copy-start.5
  32.1 0.9 copy-done.5
  33.0 0.0 copy-start.7
  33.0 0.9 copy-done.7
  33.9 0.0 copy-start.8
  33.9 0.7 copy-done.8
  34.6 9.2 %shard_map.61 = (f32[3,22,16,256]{3,2,1,0:T(8,128)S(1)}, f32[3,20,16,256]{3,2,1,0:T(8,128)S(1)}, f32[22,16,256]{2,1,0:T(8,128)S(1)}, f32[1,128]{1,0:T(1,128)S(1)}) custom-call(s32[2]{0:T(128)S(1)} %pad_add_fusion.pos_ref, s32[14,3]{1,0:T(8,128)S(1)} %copy-done.8, f32[16,8,256]{2,1,0:T(8,128)S(1)} %copy-done.3, f32[3,16,8,256]{3,2,1,0:T(8,128)S(1)} %copy-done.1, ...), custom_call_target="tpu_custom_call" | custom-call | tf_op jit(solution)/shard_map/pallas_call | solution.py:357
  43.9 14.5 %all_to_all.14 = f32[32,1,128]{2,1,0:T(1,128)S(1)} all-to-all(f32[32,1,128]{2,1,0:T(1,128)S(1)} %broadcast_in_dim.4), channel_id=1, replica_groups=mesh['zl'=3,'x'=4,'zh'=4,'y'=8,'c'=2] {'x','y'}, dimensions={0} | all-to-all | bytes 32768 | tf_op jit(solution)/shard_map/all_to_all | solution.py:342
  58.4 33.5 %all_to_all.15 = f32[24,1,128]{2,1,0:T(1,128)S(1)} all-to-all(f32[24,1,128]{2,1,0:T(1,128)S(1)} %broadcast_in_dim.5), channel_id=1, replica_groups=mesh['zl'=3,'x'=4,'zh'=4,'y'=8,'c'=2] {'zl','zh','c'}, dimensions={0} | all-to-all | bytes 24576 | tf_op jit(solution)/shard_map/all_to_all | solution.py:342
  91.9 0.0 copy-start.9
  91.9 0.7 copy-done.9
  92.6 6.0 %shard_map.62 = (f32[3,16,8,256]{3,2,1,0:T(8,128)}, f32[16,8,256]{2,1,0:T(8,128)}) custom-call(s32[14,3]{1,0:T(8,128)S(1)} %copy-done.9, f32[3,22,16,256]{3,2,1,0:T(8,128)S(1)} %get-tuple-element.20.ext_ref, f32[3,20,16,256]{3,2,1,0:T(8,128)S(1)} %get-tuple-element.21.g_ref, f32[22,16,256]{2,1,0:T(8,128)S(1)} %get-tuple-element.22.coef_ref, ...), custom_call_target="tpu_custom_call" | custom-call | tf_op jit(solution)/shard_map/pallas_call | solution.py:370
  (3 shorter events, 0.0 us)
Async XLA Ops:
  0.6 1.0 %copy-start = (f32[3,16,8,256]{3,2,1,0:T(8,128)S(1)}, f32[3,16,8,256]{3,2,1,0:T(8,128)}, u32[]{:S(2)}) copy-start(f32[3,16,8,256]{3,2,1,0:T(8,128)} %f_ref.5) | copy-start | bytes 1179652
  1.6 0.9 copy-start.2
  2.5 0.7 copy-start.10
  3.2 24.1 %copy-start.11 = (s32[14,3]{0,1:T(4,128)S(1)}, s32[14,3]{0,1:T(4,128)}, u32[]{:S(2)}) copy-start(s32[14,3]{0,1:T(4,128)} %param.7) | copy-start | bytes 508
  3.2 28.9 %copy-start.1 = (f32[3,16,8,256]{3,2,1,0:T(8,128)S(1)}, f32[3,16,8,256]{3,2,1,0:T(8,128)}, u32[]{:S(2)}) copy-start(f32[3,16,8,256]{3,2,1,0:T(8,128)} %f_ref.5) | copy-start | bytes 1179652
  3.2 28.9 %copy-start.3 = (f32[16,8,256]{2,1,0:T(8,128)S(1)}, f32[16,8,256]{2,1,0:T(8,128)}, u32[]{:S(2)}) copy-start(f32[16,8,256]{2,1,0:T(8,128)} %den_ref.5) | copy-start | bytes 393220
  3.5 14.4 %collective-permute-start = (f32[16,16,256]{2,1,0:T(8,128)S(1)}, f32[16,16,256]{2,1,0:T(8,128)S(1)}, u32[]{:S(2)}, u32[]{:S(2)}) collective-permute-start(f32[16,16,256]{2,1,0:T(8,128)S(1)} %get-tuple-element.14), channel_id=1, source_target_pairs={{1,0},{2,1},{3,2},{4,3},{5,4},{6,5},{7,6},{8,7},{9,8},{10,9},{11,1... | collective-permute-start | bytes 786440 | tf_op jit(solution)/shard_map/ppermute | solution.py:335
  16.0 5.2 %collective-permute-start.1 = (f32[16,16,256]{2,1,0:T(8,128)S(1)}, f32[16,16,256]{2,1,0:T(8,128)S(1)}, u32[]{:S(2)}, u32[]{:S(2)}) collective-permute-start(f32[16,16,256]{2,1,0:T(8,128)S(1)} %get-tuple-element.15), channel_id=1, source_target_pairs={{0,1},{1,2},{2,3},{3,4},{4,5},{5,6},{6,7},{7,8},{8,9},{9,10},{10,1... | collective-permute-start | bytes 786440 | tf_op jit(solution)/shard_map/ppermute | solution.py:336
  21.3 0.7 copy-start.6
  22.0 7.7 %collective-permute-start.2 = (f32[13,16,256]{2,1,0:T(8,128)S(1)}, f32[13,16,256]{2,1,0:T(8,128)S(1)}, u32[]{:S(2)}, u32[]{:S(2)}) collective-permute-start(f32[13,16,256]{2,1,0:T(8,128)S(1)} %get-tuple-element.18), channel_id=1, source_target_pairs={{64,0},{128,64},{192,128},{256,192},{320,256},{384,320},{448,384},... | collective-permute-start | bytes 638984 | tf_op jit(solution)/shard_map/ppermute | solution.py:335
  23.3 8.1 %collective-permute-start.3 = (f32[13,16,256]{2,1,0:T(8,128)S(1)}, f32[13,16,256]{2,1,0:T(8,128)S(1)}, u32[]{:S(2)}, u32[]{:S(2)}) collective-permute-start(f32[13,16,256]{2,1,0:T(8,128)S(1)} %get-tuple-element.19), channel_id=1, source_target_pairs={{0,64},{64,128},{128,192},{192,256},{256,320},{320,384},{384,448},... | collective-permute-start | bytes 638984 | tf_op jit(solution)/shard_map/ppermute | solution.py:336
  31.4 0.7 copy-start.4
  32.1 0.9 copy-start.5
  33.0 0.9 copy-start.7
  33.9 0.7 copy-start.8
  91.9 0.7 copy-start.9

commit v2 on v1

v2 whole, which is shorter than its diff:
```python
import functools

import jax
import jax.numpy as jnp
import numpy as np
from jax import lax
from jax.experimental import pallas as pl
from jax.experimental.pallas import tpu as pltpu
from jax.sharding import Mesh
from jax.sharding import PartitionSpec as P

EMIN = 0.001
RADIUS = 2.0
REACH = [float(np.float32(RADIUS) - np.float32(np.sqrt(np.float32(s)))) for s in range(4)]

CX, CY, CZ = 16, 8, 256
NX, NY = 192, 512
DEV_X, DEV_Y = 12, 64
ROWS = 16
F32 = jnp.float32
UNROLL = (11, 4, 4, 6, 4)


def sub_iota(rows):
    return lax.broadcasted_iota(jnp.int32, (rows, CZ), 0)


def lane_iota(rows):
    return lax.broadcasted_iota(jnp.int32, (rows, CZ), 1)


def roll(v, shift, axis):
    return pltpu.roll(v, shift % v.shape[axis], axis)


def yp(v):
    return roll(v, -1, 0)


def ym(v):
    return roll(v, 1, 0)


def zp(v, lane, fill=0.0):
    return jnp.where(lane == CZ - 1, fill, roll(v, -1, 1))


def zm(v, lane, fill=0.0):
    return jnp.where(lane == 0, fill, roll(v, 1, 1))


def store_weights(off_ref, w_ref):
    for i in range(27):
        w_ref[i] = jnp.float32(0.0)
    for j in range(off_ref.shape[1]):
        dx, dy, dz = off_ref[0, j], off_ref[1, j], off_ref[2, j]
        s = dx * dx + dy * dy + dz * dz
        w = jnp.where(
            s == 0,
            jnp.float32(REACH[0]),
            jnp.where(
                s == 1,
                jnp.float32(REACH[1]),
                jnp.where(s == 2, jnp.float32(REACH[2]), jnp.float32(REACH[3])),
            ),
        )
        w_ref[(dx + 1) * 9 + (dy + 1) * 3 + dz + 1] = w


def pack_kernel(
    off_ref, den_hbm, f_hbm, ids_hbm,
    den_ref, f_ref, m_ref, w_ref, ylo_ref, yhi_ref, xlo_ref, xhi_ref, ll_ref, lh_ref, hl_ref, hh_ref,
    ids_ref, sem,
):
    copies = [
        pltpu.make_async_copy(src, dst, sem.at[i])
        for i, (src, dst) in enumerate(((ids_hbm, ids_ref), (den_hbm, den_ref), (f_hbm, f_ref)))
    ]
    for copy in copies:
        copy.start()
    store_weights(off_ref, w_ref)
    copies[0].wait()
    ids = ids_ref[...]
    row = lax.shift_right_logical(ids, 6)
    col = lax.bitwise_and(ids, 63)
    p = (lax.broadcasted_iota(jnp.int32, (8, 512), 0) == row).astype(jnp.bfloat16)
    q = (
        lax.shift_right_logical(lax.broadcasted_iota(jnp.int32, (CZ, 512), 0), 2) == col
    ).astype(jnp.bfloat16)
    m_ref[...] = lax.dot_general(p, q, (((1,), (1,)), ((), ())), preferred_element_type=F32)
    sub = sub_iota(8)
    low = sub < 4
    copies[1].wait()
    copies[2].wait()

    for x in range(CX):
        base = x // 4 * 2
        m_lo, m_hi = m_ref[base : base + 1], m_ref[base + 1 : base + 2]
        den, f0, f1, f2 = den_ref[x], f_ref[0, x], f_ref[1, x], f_ref[2, x]
        f0r, f2r = roll(f0, 4, 0), roll(f2, 4, 0)
        lo0 = jnp.where(sub == 7, m_lo, jnp.where(low, den, f0r))
        lo1 = jnp.where(low, f1, f2r)
        hi0 = jnp.where(sub == 0, m_hi, jnp.where(low, f0r, den))
        hi1 = jnp.where(low, f2r, f1)
        for ref, t0, t1 in ((ylo_ref, lo0, lo1), (yhi_ref, hi0, hi1)):
            ref[x, 0:8] = t0
            ref[x, 8:16] = t1
        if x < 4 or x >= 12:
            for ref, t0, t1 in (
                ((ll_ref, lo0, lo1), (lh_ref, hi0, hi1))
                if x < 4
                else ((hl_ref, lo0, lo1), (hh_ref, hi0, hi1))
            ):
                ref[x % 4, 0:8] = t0
                ref[x % 4, 8:16] = t1
            slab = xlo_ref if x < 4 else xhi_ref
            slab[x % 4] = den
            at = x if x < 4 else x - 13
            if 0 <= at < 3:
                for c, f in enumerate((f0, f1, f2)):
                    slab[4 + 3 * c + at] = f
            if x == 0 or x == 12:
                slab[13] = jnp.where(low, m_lo, m_hi)


def filter_plane(planes, w_ref, lane, sign):
    out = None
    for dz in (-1, 0, 1):
        acc = None
        for dy in (-1, 0, 1):
            t = None
            for dx in (-1, 0, 1):
                w = w_ref[(sign * dx + 1) * 9 + (sign * dy + 1) * 3 + sign * dz + 1]
                term = planes[dx + 1] * w
                t = term if t is None else t + term
            if dy == 1:
                t = yp(t)
            elif dy == -1:
                t = ym(t)
            acc = t if acc is None else acc + t
        if dz == 1:
            acc = zp(acc, lane)
        elif dz == -1:
            acc = zm(acc, lane)
        out = acc if out is None else out + acc
    return out


def image_plane(load, s_m, s_0, s_p, lane):
    px, mx = 0.5 * (s_0 + s_p), 0.5 * (s_0 + s_m)
    py = 0.5 * (s_0 + yp(s_0))
    pz = 0.5 * (s_0 + zp(s_0, lane))
    half = -0.5 * s_0
    outs = []
    for c in range(3):
        v = load(c, 0)
        fx = px * (v - load(c, 1)) + mx * (v - load(c, -1))
        fy = py * (v - yp(v))
        fy = fy - ym(fy)
        fz = pz * (v - zp(v, lane))
        fz = fz - zm(fz, lane, half * v)
        outs.append(fx + fy + fz + (fx, fy, fz)[c])
    return outs


def main_kernel(
    pos_ref, w_ref, den_ref, f_ref, m_ref, yu_ref, yd_ref, xu_ref, xd_ref, uu_ref, ud_ref, du_ref, dd_ref,
    ext_ref, g_ref, coef_ref, mom_ref,
    dext_ref, s_ref, rwt_ref, mask_ref,
):
    gx, gy = pos_ref[0], pos_ref[1]
    sub, lane = sub_iota(ROWS), lane_iota(ROWS)
    y = jnp.where(sub < 12, sub, sub - 16) + gy * CY

    def in_y(at):
        return ((at >= 0) & (at < NY)).astype(F32)

    iy = {dy: in_y(y + dy) for dy in (-1, 0, 1)}
    iz = {dz: ((lane + dz >= 0) & (lane + dz < CZ)).astype(F32) for dz in (-1, 0, 1)}

    for case, dxs in enumerate(((0, 1), (-1, 0, 1), (-1, 0))):
        total = jnp.zeros((ROWS, CZ), F32)
        for dy in (-1, 0, 1):
            part = jnp.zeros((ROWS, CZ), F32)
            for dz in (-1, 0, 1):
                w = w_ref[(dxs[0] + 1) * 9 + (dy + 1) * 3 + dz + 1]
                for dx in dxs[1:]:
                    w = w + w_ref[(dx + 1) * 9 + (dy + 1) * 3 + dz + 1]
                part = part + w * iz[dz]
            total = total + part * iy[dy]
        rwt_ref[case] = jnp.where(total > 0.0, iy[0] / jnp.where(total > 0.0, total, 1.0), 0.0)

    sub8 = sub_iota(8)
    low = sub8 < 4
    for layer in range(6):
        if layer == 0:
            own, up, down = xd_ref[13], du_ref[0, 7:8], dd_ref[0, 0:1]
        elif layer == 5:
            own, up, down = xu_ref[13], uu_ref[0, 7:8], ud_ref[0, 0:1]
        else:
            k, x = 2 * (layer - 1), 4 * (layer - 1)
            own = jnp.where(low, m_ref[k : k + 1], m_ref[k + 1 : k + 2])
            up, down = yu_ref[x, 7:8], yd_ref[x, 0:1]
        mask_ref[layer, 0:8] = own
        mask_ref[layer, 8:16] = jnp.where(low, up, down)

    def spread(j, den, fs, u0, u1, d0, d1):
        dext_ref[j, 0:8] = den
        dext_ref[j, 8:16] = jnp.where(low, u0, d0)
        if fs is None:
            return
        halo = (
            roll(jnp.where(low, d0, u0), 4, 0),
            jnp.where(low, u1, d1),
            roll(jnp.where(low, d1, u1), 4, 0),
        )
        for c in range(3):
            ext_ref[c, j - 1, 0:8] = fs[c]
            ext_ref[c, j - 1, 8:16] = halo[c]

    for i in range(4):
        for at, first, side, up, down in ((i, 1, xd_ref, du_ref, dd_ref), (20 + i, 0, xu_ref, uu_ref, ud_ref)):
            k = i - first
            fs = [side[4 + 3 * c + k] for c in range(3)] if 0 <= k < 3 else None
            spread(at, side[i], fs, up[i, 0:8], up[i, 8:16], down[i, 0:8], down[i, 8:16])

    def spread_own(x, _):
        fs = [f_ref[c, x] for c in range(3)]
        spread(x + 4, den_ref[x], fs, yu_ref[x, 0:8], yu_ref[x, 8:16], yd_ref[x, 0:8], yd_ref[x, 8:16])
        return 0

    lax.fori_loop(0, CX, spread_own, 0, unroll=4)

    def smooth_step(p, _):
        x = gx * CX + p - 3
        planes = [dext_ref[p], dext_ref[p + 1], dext_ref[p + 2]]
        num = filter_plane(planes, w_ref, lane, 1)
        case = jnp.where(x == 0, 0, jnp.where(x == NX - 1, 2, 1))
        in_x = jnp.where((x >= 0) & (x < NX), jnp.float32(1.0), jnp.float32(0.0))
        rwt = rwt_ref[case] * in_x
        smooth = num * rwt
        mask = mask_ref[lax.shift_right_logical(p + 1, 2)]
        sq = mask * (smooth * smooth)
        s_ref[p] = (iy[0] * in_x) * (EMIN + (sq * smooth) * (1.0 - EMIN))
        coef_ref[p] = (-3.0 * (1.0 - EMIN)) * sq * rwt
        return 0

    lax.fori_loop(0, CX + 6, smooth_step, 0, unroll=UNROLL[0])

    def image_step(q, _):
        x = gx * CX + q - 2
        in_x = jnp.where((x >= 0) & (x < NX), jnp.float32(1.0), jnp.float32(0.0))
        inside = iy[0] * in_x
        outs = image_plane(
            lambda c, k: ext_ref[c, q + 1 + k], s_ref[q], s_ref[q + 1], s_ref[q + 2], lane
        )
        for c in range(3):
            g_ref[c, q] = outs[c] * inside
        return 0

    lax.fori_loop(0, CX + 4, image_step, 0, unroll=UNROLL[1])

    def moment_step(x, sums):
        outs = image_plane(
            lambda c, k: g_ref[c, x + 2 + k], s_ref[x + 2], s_ref[x + 3], s_ref[x + 4], lane
        )
        m0, m1, m2, m3 = sums
        for c in range(3):
            f, g = f_ref[c, x], g_ref[c, x + 2, 0:8]
            m0, m1, m2, m3 = m0 + f * f, m1 + f * g, m2 + g * g, m3 + g * outs[c][0:8]
        return m0, m1, m2, m3

    zero = jnp.zeros((8, CZ), F32)
    sums = lax.fori_loop(0, CX, moment_step, (zero, zero, zero, zero), unroll=UNROLL[2])
    at = lax.broadcasted_iota(jnp.int32, (1, 128), 1)
    line = jnp.zeros((1, 128), F32)
    for k in range(4):
        total = jnp.sum(jnp.sum(sums[k], axis=0, keepdims=True), axis=1, keepdims=True)
        line = jnp.where(at == k, total, line)
    mom_ref[...] = line


def last_kernel(
    w_ref, ext_ref, g_ref, coef_ref, mom_ref, u_hbm, sens_hbm, u_ref, sh_ref, own_ref, sens_ref, sem
):
    lane = lane_iota(ROWS)
    line = jnp.sum(mom_ref[...], axis=0, keepdims=True)
    at = lax.broadcasted_iota(jnp.int32, (1, 128), 1)
    m0, m1, m2, m3 = (
        jnp.sum(jnp.where(at == k, line, 0.0), axis=1, keepdims=True) for k in range(4)
    )
    s1 = m0 / m1
    rr = m0 - 2.0 * s1 * m1 + s1 * s1 * m2
    grow = 1.0 + rr / m0
    s2 = rr / (grow * grow * m1 - 2.0 * grow * s1 * m2 + s1 * s1 * m3)
    alpha = jnp.broadcast_to(s1 + s2 * grow, (ROWS, CZ))
    beta = jnp.broadcast_to(-s1 * s2, (ROWS, CZ))

    def u_plane(q):
        us = [alpha * ext_ref[c, q + 1] + beta * g_ref[c, q] for c in range(3)]
        for c in range(3):
            u_ref[c, q] = us[c]
        return us

    def u_step(x, _):
        us = u_plane(x + 2)
        for c in range(3):
            own_ref[c, x] = us[c][0:8]
        return 0

    lax.fori_loop(0, CX, u_step, 0, unroll=4)
    u_copy = pltpu.make_async_copy(own_ref, u_hbm, sem.at[0])
    u_copy.start()
    for q in (0, 1, CX + 2, CX + 3):
        u_plane(q)

    def share_step(r, _):
        ex = ey = ez = e0 = None
        for c in range(3):
            v = u_ref[c, r + 1]
            ax, bx = v - u_ref[c, r + 2], v - u_ref[c, r]
            ay, az = v - yp(v), v - zp(v, lane)
            tx, ty, tz, t0 = ax * ax + bx * bx, ay * ay, az * az, v * v
            if c == 0:
                tx = tx + tx
            elif c == 1:
                ty = ty + ty
            else:
                tz, t0 = tz + tz, t0 + t0
            ex = tx if ex is None else ex + tx
            ey = ty if ey is None else ey + ty
            ez = tz if ez is None else ez + tz
            e0 = t0 if e0 is None else e0 + t0
        energy = 0.5 * (ex + (ey + ym(ey)) + (ez + zm(ez, lane, e0)))
        sh_ref[r] = coef_ref[r + 2] * energy
        return 0

    lax.fori_loop(0, CX + 2, share_step, 0, unroll=UNROLL[3])

    def out_step(x, _):
        planes = [sh_ref[x], sh_ref[x + 1], sh_ref[x + 2]]
        sens_ref[x] = filter_plane(planes, w_ref, lane, -1)[0:8]
        return 0

    half = CX // 2
    copies = [u_copy]
    for k in range(2):
        lax.fori_loop(k * half, (k + 1) * half, out_step, 0, unroll=UNROLL[4])
        part = pl.ds(k * half, half)
        copies.append(pltpu.make_async_copy(sens_ref.at[part], sens_hbm.at[part], sem.at[1 + k]))
        copies[-1].start()
    for copy in copies:
        copy.wait()


VMEM = pl.BlockSpec(memory_space=pltpu.VMEM)
SMEM = pl.BlockSpec(memory_space=pltpu.SMEM)


def f32(*shape):
    return jax.ShapeDtypeStruct(shape, F32)


HBM = pl.BlockSpec(memory_space=pltpu.HBM)


def call(kernel, outs, ins, out_specs, scratch):
    return pl.pallas_call(
        kernel,
        out_shape=outs,
        in_specs=ins,
        out_specs=out_specs,
        scratch_shapes=scratch,
        compiler_params=pltpu.CompilerParams(vmem_limit_bytes=24 * 1024 * 1024),
    )


def shift(slab, dx, dy):
    pairs = [
        (i * DEV_Y + j, (i + dx) * DEV_Y + j + dy)
        for i in range(DEV_X)
        for j in range(DEV_Y)
        if 0 <= i + dx < DEV_X and 0 <= j + dy < DEV_Y
    ]
    return lax.ppermute(slab, ("zl", "x", "zh", "y", "c"), pairs)


def spread_sum(line, axes, count):
    lines = jnp.broadcast_to(line, (count, 128))
    return lax.all_to_all(lines, axes, 0, 0, tiled=True)


def body(density, force, brick_ids, offsets):
    gx, gy = ("zl", "x"), ("zh", "y", "c")
    pos = jnp.stack([lax.axis_index(gx), lax.axis_index(gy)]).astype(jnp.int32)
    ids = brick_ids.reshape(1, 512)
    slab_y, slab_x, corner = f32(CX, ROWS, CZ), f32(14, 8, CZ), f32(4, ROWS, CZ)
    den, f, mask, w, ylo, yhi, xlo, xhi, ll, lh, hl, hh = call(
        pack_kernel,
        (f32(CX, CY, CZ), f32(3, CX, CY, CZ), f32(8, CZ), f32(27), slab_y, slab_y, slab_x, slab_x)
        + (corner,) * 4,
        [SMEM, HBM, HBM, HBM],
        (VMEM, VMEM, VMEM, SMEM) + (VMEM,) * 8,
        [pltpu.VMEM((1, 512), jnp.int32), pltpu.SemaphoreType.DMA((3,))],
    )(*(pltpu.with_memory_space_constraint(a, pltpu.HBM) for a in (offsets.T, density, force, ids)))
    yu, yd = shift(ylo, 0, -1), shift(yhi, 0, 1)
    xu, xd = shift(xlo, -1, 0), shift(xhi, 1, 0)
    uu, ud, du, dd = shift(ll, -1, -1), shift(lh, -1, 1), shift(hl, 1, -1), shift(hh, 1, 1)
    ext, image, coef, line = call(
        main_kernel,
        (f32(3, CX + 6, ROWS, CZ), f32(3, CX + 4, ROWS, CZ), f32(CX + 6, ROWS, CZ), f32(1, 128)),
        [SMEM, SMEM] + [VMEM] * 11,
        (VMEM,) * 4,
        [
            pltpu.VMEM((CX + 8, ROWS, CZ), F32),
            pltpu.VMEM((CX + 6, ROWS, CZ), F32),
            pltpu.VMEM((3, ROWS, CZ), F32),
            pltpu.VMEM((6, ROWS, CZ), F32),
        ],
    )(pos, w, den, f, mask, yu, yd, xu, xd, uu, ud, du, dd)
    lines = spread_sum(line, ("x", "y"), 32)
    lines = spread_sum(jnp.sum(lines, axis=0, keepdims=True), ("zl", "zh", "c"), 24)
    return call(
        last_kernel,
        (f32(3, CX, CY, CZ), f32(CX, CY, CZ)),
        [SMEM] + [VMEM] * 4,
        (HBM, HBM),
        [
            pltpu.VMEM((3, CX + 4, ROWS, CZ), F32),
            pltpu.VMEM((CX + 2, ROWS, CZ), F32),
            pltpu.VMEM((3, CX, CY, CZ), F32),
            pltpu.VMEM((CX, CY, CZ), F32),
            pltpu.SemaphoreType.DMA((3,)),
        ],
    )(w, ext, image, coef, lines)


def solution(mesh):
    fine = Mesh(mesh.devices.reshape(3, 4, 4, 8, 2), ("zl", "x", "zh", "y", "c"))
    gx, gy = ("zl", "x"), ("zh", "y", "c")
    return jax.shard_map(
        body,
        mesh=fine,
        in_specs=(P(gx, gy, None), P(None, gx, gy, None), P(gx, gy, None), P()),
        out_specs=(P(None, gx, gy, None), P(gx, gy, None)),
        check_vma=False,
    )
```

time: 99.1 us -> 103 us (1.039)
  starting transfers between devices: 19.6 us -> 33.1 us
  Pallas kernels: 15.7 us -> 9.05 us
  waiting for transfers between devices: 6.63 us -> 1.25 us
  blocking collectives: 48 us -> 52.5 us
  local copies, waits for them, and re-layouts: 7.85 us -> 6.02 us
    ppermute x4 -> x8, starting transfers between devices: 19.6 us -> 33.1 us  [shift(): return lax.ppermute(slab, ('zl', 'x', 'zh', 'y', 'c'), pairs)]
    ppermute x4 -> x8, waiting for transfers between devices: 6.63 us -> 1.25 us  [shift(): return lax.ppermute(slab, ('zl', 'x', 'zh', 'y', 'c'), pairs)]
    pallas_call x1, Pallas kernels: 9.23 us -> 3.86 us  [body(): call(main_kernel, (f32(3, CX + 6, ROWS, CZ), f32(3, CX + 4, ROWS, CZ), f3...]
    all_to_all x2, blocking collectives: 48 us -> 52.5 us  [spread_sum(): return lax.all_to_all(lines, axes, 0, 0, tiled=True)]
    pallas_call x1, Pallas kernels: 6.05 us -> 2.8 us  [body(): call(last_kernel, (f32(3, CX, CY, CZ), f32(CX, CY, CZ)), [SMEM] + [VMEM]...]
    pallas_call x2 -> x1, Pallas kernels: 0.43 us -> 2.39 us  [body(): call(pack_kernel, (f32(CX, CY, CZ), f32(3, CX, CY, CZ), f32(8, CZ), f32(2...]
    unnamed x25 -> x16, local copies, waits for them, and re-layouts: 7.83 us -> 5.99 us
  transfers between devices with their start and end apart: 4 -> 8, of which waited for: 3 -> 1; matrix products, arithmetic and copies ran while one was open for 1% -> 0% of each run, Pallas kernels for 0% -> 0%
where the time goes in v2:
time: 103 us
  blocking collectives  52.5 us (51%)
  starting transfers between devices  33.1 us (32%)
  Pallas kernels  9.05 us (9%)
  local copies, waits for them, and re-layouts  6.02 us (6%)
  waiting for transfers between devices  1.25 us (1%)
    all_to_all x2, blocking collectives, spread_sum(): return lax.all_to_all(lines, axes, 0, 0, tiled=True)  52.5 us
    ppermute x8, starting transfers between devices, shift(): return lax.ppermute(slab, ('zl', 'x', 'zh', 'y', 'c'), pairs)  33.1 us
    unnamed x16, local copies, waits for them, and re-layouts  5.99 us
    pallas_call x1, Pallas kernels, body(): call(main_kernel, (f32(3, CX + 6, ROWS, CZ), f32(3, CX + 4, ROWS, CZ), f3...  3.86 us
    pallas_call x1, Pallas kernels, body(): call(last_kernel, (f32(3, CX, CY, CZ), f32(CX, CY, CZ)), [SMEM] + [VMEM]...  2.8 us
    pallas_call x1, Pallas kernels, body(): call(pack_kernel, (f32(CX, CY, CZ), f32(3, CX, CY, CZ), f32(8, CZ), f32(2...  2.39 us
  transfers between devices with their start and end apart: 8, of which 1 were waited for; matrix products, arithmetic and copies ran while one was open for 0% of the time, Pallas kernels for 0%

profile of v2, /device:TPU:1, one launch (start us, length us, event | category | flops | bytes accessed | tf_op | source)
XLA Modules:
  0.0 102.8 jit_solution(15876530597308771905)
XLA Ops:
  0.6 2.4 %shard_map.59 = (f32[16,8,256]{2,1,0:T(8,128)S(1)}, f32[3,16,8,256]{3,2,1,0:T(8,128)S(1)}, f32[8,256]{1,0:T(8,128)S(1)}, f32[27]{0:T(128)S(1)}, f32[16,16,256]{2...) custom-call(s32[3,14]{1,0:T(4,128)} %bitcast.10, ...), custom_call_target="tpu_custom_call" | custom-call | tf_op jit(solution)/shard_map/pallas_call | solution.py:398
  3.0 12.4 %collective-permute-start = (f32[16,16,256]{2,1,0:T(8,128)S(1)}, f32[16,16,256]{2,1,0:T(8,128)S(1)}, u32[]{:S(2)}, u32[]{:S(2)}) collective-permute-start(f32[16,16,256]{2,1,0:T(8,128)S(1)} %get-tuple-element.22), channel_id=1, source_target_pairs={{1,0},{2,1},{3,2},{4,3},{5,4},{6,5},{7,6},{8,7},{9,8},{10,9},{11,1... | collective-permute-start | bytes 786440 | tf_op jit(solution)/shard_map/ppermute | solution.py:385
  15.5 1.9 %collective-permute-start.1 = (f32[16,16,256]{2,1,0:T(8,128)S(1)}, f32[16,16,256]{2,1,0:T(8,128)S(1)}, u32[]{:S(2)}, u32[]{:S(2)}) collective-permute-start(f32[16,16,256]{2,1,0:T(8,128)S(1)} %get-tuple-element.23), channel_id=1, source_target_pairs={{0,1},{1,2},{2,3},{3,4},{4,5},{5,6},{6,7},{7,8},{8,9},{9,10},{10,1... | collective-permute-start | bytes 786440 | tf_op jit(solution)/shard_map/ppermute | solution.py:385
  17.4 1.3 %collective-permute-start.4 = (f32[4,16,256]{2,1,0:T(8,128)S(1)}, f32[4,16,256]{2,1,0:T(8,128)S(1)}, u32[]{:S(2)}, u32[]{:S(2)}) collective-permute-start(f32[4,16,256]{2,1,0:T(8,128)S(1)} %get-tuple-element.26), channel_id=1, source_target_pairs={{65,0},{66,1},{67,2},{68,3},{69,4},{70,5},{71,6},{72,7},{73,8},{74... | collective-permute-start | bytes 196616 | tf_op jit(solution)/shard_map/ppermute | solution.py:385
  18.7 1.3 %collective-permute-start.5 = (f32[4,16,256]{2,1,0:T(8,128)S(1)}, f32[4,16,256]{2,1,0:T(8,128)S(1)}, u32[]{:S(2)}, u32[]{:S(2)}) collective-permute-start(f32[4,16,256]{2,1,0:T(8,128)S(1)} %get-tuple-element.27), channel_id=1, source_target_pairs={{64,1},{65,2},{66,3},{67,4},{68,5},{69,6},{70,7},{71,8},{72,9},{73... | collective-permute-start | bytes 196616 | tf_op jit(solution)/shard_map/ppermute | solution.py:385
  20.0 4.3 %collective-permute-start.6 = (f32[4,16,256]{2,1,0:T(8,128)S(1)}, f32[4,16,256]{2,1,0:T(8,128)S(1)}, u32[]{:S(2)}, u32[]{:S(2)}) collective-permute-start(f32[4,16,256]{2,1,0:T(8,128)S(1)} %get-tuple-element.28), channel_id=1, source_target_pairs={{1,64},{2,65},{3,66},{4,67},{5,68},{6,69},{7,70},{8,71},{9,72},{10... | collective-permute-start | bytes 196616 | tf_op jit(solution)/shard_map/ppermute | solution.py:385
  24.3 0.0 collective-permute-done.4.uu_ref
  24.3 1.3 %collective-permute-start.2 = (f32[14,8,256]{2,1,0:T(8,128)S(1)}, f32[14,8,256]{2,1,0:T(8,128)S(1)}, u32[]{:S(2)}, u32[]{:S(2)}) collective-permute-start(f32[14,8,256]{2,1,0:T(8,128)S(1)} %get-tuple-element.24), channel_id=1, source_target_pairs={{64,0},{65,1},{66,2},{67,3},{68,4},{69,5},{70,6},{71,7},{72,8},{73... | collective-permute-start | bytes 344072 | tf_op jit(solution)/shard_map/ppermute | solution.py:385
  25.6 0.0 collective-permute-done.5.ud_ref
  25.6 0.0 copy-start.4
  25.6 0.6 copy-done.4
  26.2 5.0 %collective-permute-start.3 = (f32[14,8,256]{2,1,0:T(8,128)S(1)}, f32[14,8,256]{2,1,0:T(8,128)S(1)}, u32[]{:S(2)}, u32[]{:S(2)}) collective-permute-start(f32[14,8,256]{2,1,0:T(8,128)S(1)} %get-tuple-element.25), channel_id=1, source_target_pairs={{0,64},{1,65},{2,66},{3,67},{4,68},{5,69},{6,70},{7,71},{8,72},{9,... | collective-permute-start | bytes 344072 | tf_op jit(solution)/shard_map/ppermute | solution.py:385
  31.2 0.0 collective-permute-done.6.du_ref
  31.2 0.0 copy-start.6
  31.3 0.6 copy-done.6
  31.9 5.6 %collective-permute-start.7 = (f32[4,16,256]{2,1,0:T(8,128)S(1)}, f32[4,16,256]{2,1,0:T(8,128)S(1)}, u32[]{:S(2)}, u32[]{:S(2)}) collective-permute-start(f32[4,16,256]{2,1,0:T(8,128)S(1)} %get-tuple-element.29), channel_id=1, source_target_pairs={{0,65},{1,66},{2,67},{3,68},{4,69},{5,70},{6,71},{7,72},{8,73},{9,... | collective-permute-start | bytes 196616 | tf_op jit(solution)/shard_map/ppermute | solution.py:385
  37.5 0.1 pad_add_fusion.pos_ref
  37.5 1.2 %collective-permute-done.7.dd_ref = f32[4,16,256]{2,1,0:T(8,128)S(1)} collective-permute-done((f32[4,16,256]{2,1,0:T(8,128)S(1)}, f32[4,16,256]{2,1,0:T(8,128)S(1)}, u32[]{:S(2)}, u32[]{:S(2)}) %collective-permute-start.7) | collective-permute-done | bytes 65568 | tf_op jit(solution)/shard_map/ppermute | solution.py:385
  38.8 0.0 collective-permute-done.2.xu_ref
  38.8 0.0 copy-start
  38.8 0.6 copy-done
  39.4 0.0 collective-permute-done.3.xd_ref
  39.4 0.0 copy-start.2
  39.4 0.6 copy-done.2
  40.1 0.0 collective-permute-done.yu_ref
  40.1 0.0 collective-permute-done.1.yd_ref
  40.1 0.0 copy-start.1
  40.1 0.9 copy-done.1
  41.0 0.0 copy-start.3
  41.0 0.9 copy-done.3
  41.9 0.0 copy-start.5
  41.9 0.8 copy-done.5
  42.7 0.0 copy-start.7
  42.7 0.8 copy-done.7
  43.6 3.9 %shard_map.60 = (f32[3,22,16,256]{3,2,1,0:T(8,128)S(1)}, f32[3,20,16,256]{3,2,1,0:T(8,128)S(1)}, f32[22,16,256]{2,1,0:T(8,128)S(1)}, f32[1,128]{1,0:T(1,128)S(1)}) custom-call(s32[2]{0:T(128)S(1)} %pad_add_fusion.pos_ref, f32[27]{0:T(128)S(1)} %get-tuple-element.18.w_ref, f32[16,8,256]{2,1,0:T(8,128)S(1)} %get-tuple-element.19.den_ref, ...), custom_call_target="tpu_custom_call" | custom-call | tf_op jit(solution)/shard_map/pallas_call | solution.py:409
  47.5 23.8 %all_to_all.14 = f32[32,1,128]{2,1,0:T(1,128)S(1)} all-to-all(f32[32,1,128]{2,1,0:T(1,128)S(1)} %broadcast_in_dim.4), channel_id=1, replica_groups=mesh['zl'=3,'x'=4,'zh'=4,'y'=8,'c'=2] {'x','y'}, dimensions={0} | all-to-all | bytes 32768 | tf_op jit(solution)/shard_map/all_to_all | solution.py:390
  71.3 28.7 %all_to_all.15 = f32[24,1,128]{2,1,0:T(1,128)S(1)} all-to-all(f32[24,1,128]{2,1,0:T(1,128)S(1)} %broadcast_in_dim.5), channel_id=1, replica_groups=mesh['zl'=3,'x'=4,'zh'=4,'y'=8,'c'=2] {'zl','zh','c'}, dimensions={0} | all-to-all | bytes 24576 | tf_op jit(solution)/shard_map/all_to_all | solution.py:390
  100.0 2.8 %shard_map.61 = (f32[3,16,8,256]{3,2,1,0:T(8,128)}, f32[16,8,256]{2,1,0:T(8,128)}) custom-call(f32[27]{0:T(128)S(1)} %get-tuple-element.18.w_ref, f32[3,22,16,256]{3,2,1,0:T(8,128)S(1)} %get-tuple-element.30.ext_ref, f32[3,20,16,256]{3,2,1,0:T(8,128)S(1)} %get-tuple-element.31.g_ref, f32[22,16,256]{2,1,0:T(8,128)S(1)} %get-tuple-element.32.coef_ref, ...), custom_call_target="tpu_custom_call" | custom-call | tf_op jit(solution)/shard_map/pallas_call | solution.py:423
  (3 shorter events, 0.0 us)
Async XLA Ops:
  3.0 37.1 %collective-permute-start = (f32[16,16,256]{2,1,0:T(8,128)S(1)}, f32[16,16,256]{2,1,0:T(8,128)S(1)}, u32[]{:S(2)}, u32[]{:S(2)}) collective-permute-start(f32[16,16,256]{2,1,0:T(8,128)S(1)} %get-tuple-element.22), channel_id=1, source_target_pairs={{1,0},{2,1},{3,2},{4,3},{5,4},{6,5},{7,6},{8,7},{9,8},{10,9},{11,1... | collective-permute-start | bytes 786440 | tf_op jit(solution)/shard_map/ppermute | solution.py:385
  15.5 24.6 %collective-permute-start.1 = (f32[16,16,256]{2,1,0:T(8,128)S(1)}, f32[16,16,256]{2,1,0:T(8,128)S(1)}, u32[]{:S(2)}, u32[]{:S(2)}) collective-permute-start(f32[16,16,256]{2,1,0:T(8,128)S(1)} %get-tuple-element.23), channel_id=1, source_target_pairs={{0,1},{1,2},{2,3},{3,4},{4,5},{5,6},{6,7},{7,8},{8,9},{9,10},{10,1... | collective-permute-start | bytes 786440 | tf_op jit(solution)/shard_map/ppermute | solution.py:385
  17.4 6.9 %collective-permute-start.4 = (f32[4,16,256]{2,1,0:T(8,128)S(1)}, f32[4,16,256]{2,1,0:T(8,128)S(1)}, u32[]{:S(2)}, u32[]{:S(2)}) collective-permute-start(f32[4,16,256]{2,1,0:T(8,128)S(1)} %get-tuple-element.26), channel_id=1, source_target_pairs={{65,0},{66,1},{67,2},{68,3},{69,4},{70,5},{71,6},{72,7},{73,8},{74... | collective-permute-start | bytes 196616 | tf_op jit(solution)/shard_map/ppermute | solution.py:385
  18.7 6.9 %collective-permute-start.5 = (f32[4,16,256]{2,1,0:T(8,128)S(1)}, f32[4,16,256]{2,1,0:T(8,128)S(1)}, u32[]{:S(2)}, u32[]{:S(2)}) collective-permute-start(f32[4,16,256]{2,1,0:T(8,128)S(1)} %get-tuple-element.27), channel_id=1, source_target_pairs={{64,1},{65,2},{66,3},{67,4},{68,5},{69,6},{70,7},{71,8},{72,9},{73... | collective-permute-start | bytes 196616 | tf_op jit(solution)/shard_map/ppermute | solution.py:385
  20.0 11.2 %collective-permute-start.6 = (f32[4,16,256]{2,1,0:T(8,128)S(1)}, f32[4,16,256]{2,1,0:T(8,128)S(1)}, u32[]{:S(2)}, u32[]{:S(2)}) collective-permute-start(f32[4,16,256]{2,1,0:T(8,128)S(1)} %get-tuple-element.28), channel_id=1, source_target_pairs={{1,64},{2,65},{3,66},{4,67},{5,68},{6,69},{7,70},{8,71},{9,72},{10... | collective-permute-start | bytes 196616 | tf_op jit(solution)/shard_map/ppermute | solution.py:385
  24.3 14.5 %collective-permute-start.2 = (f32[14,8,256]{2,1,0:T(8,128)S(1)}, f32[14,8,256]{2,1,0:T(8,128)S(1)}, u32[]{:S(2)}, u32[]{:S(2)}) collective-permute-start(f32[14,8,256]{2,1,0:T(8,128)S(1)} %get-tuple-element.24), channel_id=1, source_target_pairs={{64,0},{65,1},{66,2},{67,3},{68,4},{69,5},{70,6},{71,7},{72,8},{73... | collective-permute-start | bytes 344072 | tf_op jit(solution)/shard_map/ppermute | solution.py:385
  25.6 0.6 copy-start.4
  26.2 13.2 %collective-permute-start.3 = (f32[14,8,256]{2,1,0:T(8,128)S(1)}, f32[14,8,256]{2,1,0:T(8,128)S(1)}, u32[]{:S(2)}, u32[]{:S(2)}) collective-permute-start(f32[14,8,256]{2,1,0:T(8,128)S(1)} %get-tuple-element.25), channel_id=1, source_target_pairs={{0,64},{1,65},{2,66},{3,67},{4,68},{5,69},{6,70},{7,71},{8,72},{9,... | collective-permute-start | bytes 344072 | tf_op jit(solution)/shard_map/ppermute | solution.py:385
  31.2 0.6 copy-start.6
  31.9 6.9 %collective-permute-start.7 = (f32[4,16,256]{2,1,0:T(8,128)S(1)}, f32[4,16,256]{2,1,0:T(8,128)S(1)}, u32[]{:S(2)}, u32[]{:S(2)}) collective-permute-start(f32[4,16,256]{2,1,0:T(8,128)S(1)} %get-tuple-element.29), channel_id=1, source_target_pairs={{0,65},{1,66},{2,67},{3,68},{4,69},{5,70},{6,71},{7,72},{8,73},{9,... | collective-permute-start | bytes 196616 | tf_op jit(solution)/shard_map/ppermute | solution.py:385
  38.8 0.6 copy-start
  39.4 0.6 copy-start.2
  40.1 0.9 copy-start.1
  41.0 0.9 copy-start.3
  41.9 0.8 copy-start.5
  42.7 0.8 copy-start.7

commit v3 on v2

v3 whole, which is shorter than its diff:
```python
import functools

import jax
import jax.numpy as jnp
import numpy as np
from jax import lax
from jax.experimental import pallas as pl
from jax.experimental.pallas import tpu as pltpu
from jax.sharding import Mesh
from jax.sharding import PartitionSpec as P

EMIN = 0.001
RADIUS = 2.0
REACH = [float(np.float32(RADIUS) - np.float32(np.sqrt(np.float32(s)))) for s in range(4)]

CX, CY, CZ = 16, 8, 256
NX, NY = 192, 512
DEV_X, DEV_Y = 12, 64
ROWS = 16
F32 = jnp.float32
UNROLL = (7, 4, 5, 8, 4, 1, 6, 4)


def sub_iota(rows):
    return lax.broadcasted_iota(jnp.int32, (rows, CZ), 0)


def lane_iota(rows):
    return lax.broadcasted_iota(jnp.int32, (rows, CZ), 1)


def roll(v, shift, axis):
    return pltpu.roll(v, shift % v.shape[axis], axis)


def yp(v):
    return roll(v, -1, 0)


def ym(v):
    return roll(v, 1, 0)


def zp(v, lane, fill=0.0):
    return jnp.where(lane == CZ - 1, fill, roll(v, -1, 1))


def zm(v, lane, fill=0.0):
    return jnp.where(lane == 0, fill, roll(v, 1, 1))


def store_weights(off_ref, w_ref):
    for i in range(27):
        w_ref[i] = jnp.float32(0.0)
    for j in range(off_ref.shape[1]):
        dx, dy, dz = off_ref[0, j], off_ref[1, j], off_ref[2, j]
        s = dx * dx + dy * dy + dz * dz
        w = jnp.where(
            s == 0,
            jnp.float32(REACH[0]),
            jnp.where(
                s == 1,
                jnp.float32(REACH[1]),
                jnp.where(s == 2, jnp.float32(REACH[2]), jnp.float32(REACH[3])),
            ),
        )
        w_ref[(dx + 1) * 9 + (dy + 1) * 3 + dz + 1] = w


def pack_y_kernel(
    off_ref, den_hbm, f_hbm, ids_hbm, den_ref, f_ref, m_ref, w_ref, lo_ref, hi_ref, ids_ref, sem
):
    copies = [
        pltpu.make_async_copy(src, dst, sem.at[i])
        for i, (src, dst) in enumerate(((ids_hbm, ids_ref), (den_hbm, den_ref), (f_hbm, f_ref)))
    ]
    for copy in copies:
        copy.start()
    store_weights(off_ref, w_ref)
    copies[0].wait()
    ids = ids_ref[...]
    row = lax.shift_right_logical(ids, 6)
    col = lax.bitwise_and(ids, 63)
    p = (lax.broadcasted_iota(jnp.int32, (8, 512), 0) == row).astype(jnp.bfloat16)
    q = (
        lax.shift_right_logical(lax.broadcasted_iota(jnp.int32, (CZ, 512), 0), 2) == col
    ).astype(jnp.bfloat16)
    flags = lax.dot_general(p, q, (((1,), (1,)), ((), ())), preferred_element_type=F32)
    m_ref[...] = flags
    lo_ref[208:216] = flags
    hi_ref[208:216] = flags
    copies[1].wait()
    den = jnp.swapaxes(den_ref[...], 0, 1)
    for j in range(4):
        lo_ref[16 * j : 16 * j + 16] = den[j]
        hi_ref[16 * j : 16 * j + 16] = den[4 + j]
    copies[2].wait()
    for c in range(3):
        f = jnp.swapaxes(f_ref[c], 0, 1)
        for j in range(3):
            at = 64 + 16 * (3 * c + j)
            lo_ref[at : at + 16] = f[j]
            hi_ref[at : at + 16] = f[5 + j]


def pack_x_kernel(den_ref, f_ref, m_ref, up_ref, dn_ref, dext_ref, fext_ref, lo_ref, hi_ref):
    def spread_flags(ref, first, by):
        rows = [ref[first + 2 * bx + by : first + 2 * bx + by + 1] for bx in range(4)]
        return jnp.concatenate([jnp.broadcast_to(r, (4, CZ)) for r in rows], axis=0)

    def halo_rows(planes):
        return jnp.swapaxes(jnp.stack(planes), 0, 1)

    dext_ref[:, 0:8] = den_ref[...]
    dext_ref[:, 8:16] = halo_rows(
        [up_ref[16 * j : 16 * j + 16] for j in range(4)] + [dn_ref[16 * j : 16 * j + 16] for j in range(4)]
    )
    flags = (
        [spread_flags(up_ref, 208, 0), spread_flags(dn_ref, 208, 1)],
        [spread_flags(m_ref, 0, 0), spread_flags(m_ref, 0, 1)],
        [jnp.zeros((CX, CZ), F32)] * 2,
    )
    for c in range(3):
        at = [64 + 16 * (3 * c + j) for j in range(3)]
        fext_ref[c, :, 0:8] = f_ref[c]
        fext_ref[c, :, 8:16] = halo_rows(
            [up_ref[i : i + 16] for i in at] + flags[c] + [dn_ref[i : i + 16] for i in at]
        )
    for slab, dx0, fx0 in ((lo_ref, 0, 0), (hi_ref, 12, 13)):
        slab[0:4] = dext_ref[dx0 : dx0 + 4]
        for c in range(3):
            slab[4 + 3 * c : 7 + 3 * c] = fext_ref[c, fx0 : fx0 + 3]


def filter_plane(planes, w_ref, lane, sign):
    out = None
    for dz in (-1, 0, 1):
        acc = None
        for dy in (-1, 0, 1):
            t = None
            for dx in (-1, 0, 1):
                w = w_ref[(sign * dx + 1) * 9 + (sign * dy + 1) * 3 + sign * dz + 1]
                term = planes[dx + 1] * w
                t = term if t is None else t + term
            if dy == 1:
                t = yp(t)
            elif dy == -1:
                t = ym(t)
            acc = t if acc is None else acc + t
        if dz == 1:
            acc = zp(acc, lane)
        elif dz == -1:
            acc = zm(acc, lane)
        out = acc if out is None else out + acc
    return out


def image_plane(load, s_m, s_0, s_p, lane):
    px, mx = 0.5 * (s_0 + s_p), 0.5 * (s_0 + s_m)
    py = 0.5 * (s_0 + yp(s_0))
    pz = 0.5 * (s_0 + zp(s_0, lane))
    half = -0.5 * s_0
    outs = []
    for c in range(3):
        v = load(c, 0)
        fx = px * (v - load(c, 1)) + mx * (v - load(c, -1))
        fy = py * (v - yp(v))
        fy = fy - ym(fy)
        fz = pz * (v - zp(v, lane))
        fz = fz - zm(fz, lane, half * v)
        outs.append(fx + fy + fz + (fx, fy, fz)[c])
    return outs


def grid_y(gy):
    sub = sub_iota(ROWS)
    y = jnp.where(sub < 12, sub, sub - 16) + gy * CY
    return {dy: ((y + dy >= 0) & (y + dy < NY)).astype(F32) for dy in (-1, 0, 1)}


def store_reciprocals(rwt_ref, w_ref, iy):
    lane = lane_iota(ROWS)
    iz = {dz: ((lane + dz >= 0) & (lane + dz < CZ)).astype(F32) for dz in (-1, 0, 1)}
    for case, dxs in enumerate(((0, 1), (-1, 0, 1), (-1, 0))):
        total = jnp.zeros((ROWS, CZ), F32)
        for dy in (-1, 0, 1):
            part = jnp.zeros((ROWS, CZ), F32)
            for dz in (-1, 0, 1):
                w = w_ref[(dxs[0] + 1) * 9 + (dy + 1) * 3 + dz + 1]
                for dx in dxs[1:]:
                    w = w + w_ref[(dx + 1) * 9 + (dy + 1) * 3 + dz + 1]
                part = part + w * iz[dz]
            total = total + part * iy[dy]
        rwt_ref[case] = jnp.where(total > 0.0, iy[0] / jnp.where(total > 0.0, total, 1.0), 0.0)


def on_grid(x):
    return jnp.where((x >= 0) & (x < NX), jnp.float32(1.0), jnp.float32(0.0))


def brick_flags(f1_rows, f0_rows):
    low = sub_iota(8) < 4
    halves = [jnp.where(low, rows[0:1], rows[1:2]) for rows in (f1_rows, f0_rows)]
    return jnp.concatenate(halves, axis=0)


def stiffness_plane(planes, flags, x, inside_y, rwt_ref, w_ref, lane):
    num = filter_plane(planes, w_ref, lane, 1)
    inside = on_grid(x)
    rwt = rwt_ref[jnp.where(x == 0, 0, jnp.where(x == NX - 1, 2, 1))] * inside
    smooth = num * rwt
    sq = flags * (smooth * smooth)
    stiff = (inside_y * inside) * (EMIN + (sq * smooth) * (1.0 - EMIN))
    return stiff, (-3.0 * (1.0 - EMIN)) * sq * rwt


def add_moments(sums, fs, gs, outs):
    m0, m1, m2, m3 = sums
    for f, g, out in zip(fs, gs, outs):
        f, g, out = f[0:8], g[0:8], out[0:8]
        m0, m1, m2, m3 = m0 + f * f, m1 + f * g, m2 + g * g, m3 + g * out
    return m0, m1, m2, m3


def inner_kernel(
    pos_ref, w_ref, dext_ref, fext_ref, s_ref, coef_ref, g_ref, sums_ref, rwt_ref
):
    gx, gy = pos_ref[0], pos_ref[1]
    lane = lane_iota(ROWS)
    iy = grid_y(gy)
    store_reciprocals(rwt_ref, w_ref, iy)

    def smooth_step(p, _):
        x = p + 1
        planes = [dext_ref[p], dext_ref[p + 1], dext_ref[p + 2]]
        flags = brick_flags(fext_ref[1, x, 11:13], fext_ref[0, x, 11:13])
        s_ref[p], coef_ref[p] = stiffness_plane(
            planes, flags, gx * CX + x, iy[0], rwt_ref, w_ref, lane
        )
        return 0

    lax.fori_loop(0, CX - 2, smooth_step, 0, unroll=UNROLL[0])

    def image_step(q, _):
        outs = image_plane(
            lambda c, k: fext_ref[c, q + 2 + k], s_ref[q], s_ref[q + 1], s_ref[q + 2], lane
        )
        for c in range(3):
            g_ref[c, q] = outs[c] * iy[0]
        return 0

    lax.fori_loop(0, CX - 4, image_step, 0, unroll=UNROLL[1])

    def moment_step(t, sums):
        outs = image_plane(
            lambda c, k: g_ref[c, t + 1 + k], s_ref[t + 1], s_ref[t + 2], s_ref[t + 3], lane
        )
        fs = [fext_ref[c, t + 3] for c in range(3)]
        return add_moments(sums, fs, [g_ref[c, t + 1] for c in range(3)], outs)

    zero = jnp.zeros((8, CZ), F32)
    sums = lax.fori_loop(0, CX - 6, moment_step, (zero,) * 4, unroll=UNROLL[2])
    for k in range(4):
        sums_ref[k] = sums[k]


def rim_kernel(
    pos_ref, w_ref, dext_ref, fext_ref, xu_ref, xd_ref, s_in_ref, g_in_ref, sums_ref, rwt_ref,
    g_ref, coef_ref, mom_ref,
    d2_ref, f2_ref, s2_ref, g2_ref,
):
    gx, gy = pos_ref[0], pos_ref[1]
    lane = lane_iota(ROWS)
    iy = grid_y(gy)
    d2_ref[0, 0:4] = xd_ref[0:4]
    d2_ref[0, 4:6] = dext_ref[0:2]
    d2_ref[1, 0:2] = dext_ref[14:16]
    d2_ref[1, 2:6] = xu_ref[0:4]
    s2_ref[0, 4:7] = s_in_ref[0:3]
    s2_ref[1, 0:3] = s_in_ref[11:14]
    for c in range(3):
        f2_ref[c, 0, 0:3] = xd_ref[4 + 3 * c : 7 + 3 * c]
        f2_ref[c, 0, 3:6] = fext_ref[c, 0:3]
        f2_ref[c, 1, 0:3] = fext_ref[c, 13:16]
        f2_ref[c, 1, 3:6] = xu_ref[4 + 3 * c : 7 + 3 * c]
        g2_ref[c, 0, 4:6] = g_in_ref[c, 0:2]
        g2_ref[c, 1, 0:2] = g_in_ref[c, 10:12]

    def smooth_step(i, _):
        side, m = lax.shift_right_logical(i, 2), lax.bitwise_and(i, 3)
        planes = [d2_ref[side, m + k] for k in range(3)]
        flags = brick_flags(f2_ref[1, side, m + 2 * side, 11:13], f2_ref[0, side, m + 2 * side, 11:13])
        s2_ref[side, m + 3 * side], coef_ref[side, m] = stiffness_plane(
            planes, flags, gx * CX + m - 3 + 18 * side, iy[0], rwt_ref, w_ref, lane
        )
        return 0

    lax.fori_loop(0, 8, smooth_step, 0, unroll=UNROLL[3])

    def image_step(i, _):
        side, m = lax.shift_right_logical(i, 2), lax.bitwise_and(i, 3)
        n = m + side
        outs = image_plane(
            lambda c, k: f2_ref[c, side, m + 1 + k],
            s2_ref[side, n], s2_ref[side, n + 1], s2_ref[side, n + 2], lane,
        )
        inside = iy[0] * on_grid(gx * CX + m - 2 + 16 * side)
        for c in range(3):
            g = outs[c] * inside
            g_ref[c, side, m] = g
            g2_ref[c, side, m + 2 * side] = g
        return 0

    lax.fori_loop(0, 8, image_step, 0, unroll=UNROLL[4])

    def moment_step(m, sums):
        for side in range(2):
            q = m + 2 - side
            n = m + 3 - 2 * side
            outs = image_plane(
                lambda c, k: g2_ref[c, side, q + k],
                s2_ref[side, n - 1], s2_ref[side, n], s2_ref[side, n + 1], lane,
            )
            fs = [f2_ref[c, side, m + 3 - 3 * side] for c in range(3)]
            sums = add_moments(sums, fs, [g2_ref[c, side, q] for c in range(3)], outs)
        return sums

    sums = lax.fori_loop(0, 3, moment_step, tuple(sums_ref[k] for k in range(4)), unroll=UNROLL[5])
    at = lax.broadcasted_iota(jnp.int32, (1, 128), 1)
    line = jnp.zeros((1, 128), F32)
    for k in range(4):
        total = jnp.sum(jnp.sum(sums[k], axis=0, keepdims=True), axis=1, keepdims=True)
        line = jnp.where(at == k, total, line)
    mom_ref[...] = line


def last_kernel(
    w_ref, fext_ref, xu_ref, xd_ref, g_in_ref, g_rim_ref, coef_in_ref, coef_rim_ref, mom_ref,
    u_hbm, sens_hbm,
    u_ref, sh_ref, coef_ref, own_ref, sens_ref, sem,
):
    lane = lane_iota(ROWS)
    line = jnp.sum(mom_ref[...], axis=0, keepdims=True)
    at = lax.broadcasted_iota(jnp.int32, (1, 128), 1)
    m0, m1, m2, m3 = (
        jnp.sum(jnp.where(at == k, line, 0.0), axis=1, keepdims=True) for k in range(4)
    )
    s1 = m0 / m1
    rr = m0 - 2.0 * s1 * m1 + s1 * s1 * m2
    grow = 1.0 + rr / m0
    s2 = rr / (grow * grow * m1 - 2.0 * grow * s1 * m2 + s1 * s1 * m3)
    alpha = jnp.broadcast_to(s1 + s2 * grow, (ROWS, CZ))
    beta = jnp.broadcast_to(-s1 * s2, (ROWS, CZ))

    def u_plane(q, fs, gs):
        us = [alpha * f + beta * g for f, g in zip(fs, gs)]
        for c in range(3):
            u_ref[c, q] = us[c]
        return us

    def u_step(k, _):
        us = u_plane(k + 4, [fext_ref[c, k + 2] for c in range(3)], [g_in_ref[c, k] for c in range(3)])
        for c in range(3):
            own_ref[c, k + 2] = us[c][0:8]
        return 0

    lax.fori_loop(0, CX - 4, u_step, 0, unroll=4)
    for x in (0, 1, 14, 15):
        side, m = (0, x + 2) if x < 8 else (1, x - 14)
        us = u_plane(
            x + 2, [fext_ref[c, x] for c in range(3)], [g_rim_ref[c, side, m] for c in range(3)]
        )
        for c in range(3):
            own_ref[c, x] = us[c][0:8]
    u_copy = pltpu.make_async_copy(own_ref, u_hbm, sem.at[0])
    u_copy.start()
    for q, slab, i, side, m in ((0, xd_ref, 1, 0, 0), (1, xd_ref, 2, 0, 1), (18, xu_ref, 0, 1, 2), (19, xu_ref, 1, 1, 3)):
        u_plane(q, [slab[4 + 3 * c + i] for c in range(3)], [g_rim_ref[c, side, m] for c in range(3)])
    coef_ref[0:2] = coef_rim_ref[0, 2:4]
    coef_ref[2:16] = coef_in_ref[...]
    coef_ref[16:18] = coef_rim_ref[1, 0:2]

    def share_step(r, _):
        ex = ey = ez = e0 = None
        for c in range(3):
            v = u_ref[c, r + 1]
            ax, bx = v - u_ref[c, r + 2], v - u_ref[c, r]
            ay, az = v - yp(v), v - zp(v, lane)
            tx, ty, tz, t0 = ax * ax + bx * bx, ay * ay, az * az, v * v
            if c == 0:
                tx = tx + tx
            elif c == 1:
                ty = ty + ty
            else:
                tz, t0 = tz + tz, t0 + t0
            ex = tx if ex is None else ex + tx
            ey = ty if ey is None else ey + ty
            ez = tz if ez is None else ez + tz
            e0 = t0 if e0 is None else e0 + t0
        energy = 0.5 * (ex + (ey + ym(ey)) + (ez + zm(ez, lane, e0)))
        sh_ref[r] = coef_ref[r] * energy
        return 0

    lax.fori_loop(0, CX + 2, share_step, 0, unroll=UNROLL[6])

    def out_step(x, _):
        planes = [sh_ref[x], sh_ref[x + 1], sh_ref[x + 2]]
        sens_ref[x] = filter_plane(planes, w_ref, lane, -1)[0:8]
        return 0

    half = CX // 2
    copies = [u_copy]
    for k in range(2):
        lax.fori_loop(k * half, (k + 1) * half, out_step, 0, unroll=UNROLL[7])
        part = pl.ds(k * half, half)
        copies.append(pltpu.make_async_copy(sens_ref.at[part], sens_hbm.at[part], sem.at[1 + k]))
        copies[-1].start()
    for copy in copies:
        copy.wait()


VMEM = pl.BlockSpec(memory_space=pltpu.VMEM)
SMEM = pl.BlockSpec(memory_space=pltpu.SMEM)


def f32(*shape):
    return jax.ShapeDtypeStruct(shape, F32)


HBM = pl.BlockSpec(memory_space=pltpu.HBM)


def call(kernel, outs, ins, out_specs, scratch, cost=None):
    return pl.pallas_call(
        kernel,
        out_shape=outs,
        in_specs=ins,
        out_specs=out_specs,
        scratch_shapes=scratch,
        cost_estimate=cost,
        compiler_params=pltpu.CompilerParams(vmem_limit_bytes=24 * 1024 * 1024),
    )


def swap(lo, hi, axes, count):
    up = lax.ppermute(lo, axes, [(i + 1, i) for i in range(count - 1)])
    down = lax.ppermute(hi, axes, [(i, i + 1) for i in range(count - 1)])
    return up, down


def spread_sum(line, axes, count):
    lines = jnp.broadcast_to(line, (count, 128))
    return lax.all_to_all(lines, axes, 0, 0, tiled=True)


def body(density, force, brick_ids, offsets):
    gx, gy = ("zl", "x"), ("zh", "y", "c")
    pos = jnp.stack([lax.axis_index(gx), lax.axis_index(gy)]).astype(jnp.int32)
    ins = (offsets.T, density, force, brick_ids.reshape(1, 512))
    plane = (ROWS, CZ)
    slab_y, slab_x = f32(216, CZ), f32(13, *plane)
    den, f, mask, w, lo, hi = call(
        pack_y_kernel,
        (f32(CX, CY, CZ), f32(3, CX, CY, CZ), f32(8, CZ), f32(27), slab_y, slab_y),
        [SMEM, HBM, HBM, HBM],
        (VMEM, VMEM, VMEM, SMEM, VMEM, VMEM),
        [pltpu.VMEM((1, 512), jnp.int32), pltpu.SemaphoreType.DMA((3,))],
    )(*(pltpu.with_memory_space_constraint(a, pltpu.HBM) for a in ins))
    up, down = swap(lo, hi, gy, DEV_Y)
    dext, fext, lo, hi = call(
        pack_x_kernel,
        (f32(CX, *plane), f32(3, CX, *plane), slab_x, slab_x),
        [VMEM] * 5,
        (VMEM,) * 4,
        [],
    )(den, f, mask, up, down)
    up, down = swap(lo, hi, gx, DEV_X)
    stiff, coef, image, sums, rwt = call(
        inner_kernel,
        (f32(14, *plane), f32(14, *plane), f32(3, 12, *plane), f32(4, 8, CZ), f32(3, *plane)),
        [SMEM, SMEM, VMEM, VMEM],
        (VMEM,) * 5,
        [],
        pl.CostEstimate(flops=8_000_000, bytes_accessed=8_000_000, transcendentals=0),
    )(pos, w, dext, fext)
    image_rim, coef_rim, line = call(
        rim_kernel,
        (f32(3, 2, 4, *plane), f32(2, 4, *plane), f32(1, 128)),
        [SMEM, SMEM] + [VMEM] * 8,
        (VMEM,) * 3,
        [
            pltpu.VMEM((2, 6, *plane), F32),
            pltpu.VMEM((3, 2, 6, *plane), F32),
            pltpu.VMEM((2, 7, *plane), F32),
            pltpu.VMEM((3, 2, 6, *plane), F32),
        ],
    )(pos, w, dext, fext, up, down, stiff, image, sums, rwt)
    lines = spread_sum(line, ("x", "y"), 32)
    lines = spread_sum(jnp.sum(lines, axis=0, keepdims=True), ("zl", "zh", "c"), 24)
    return call(
        last_kernel,
        (f32(3, CX, CY, CZ), f32(CX, CY, CZ)),
        [SMEM] + [VMEM] * 8,
        (HBM, HBM),
        [
            pltpu.VMEM((3, CX + 4, *plane), F32),
            pltpu.VMEM((CX + 2, *plane), F32),
            pltpu.VMEM((CX + 2, *plane), F32),
            pltpu.VMEM((3, CX, CY, CZ), F32),
            pltpu.VMEM((CX, CY, CZ), F32),
            pltpu.SemaphoreType.DMA((3,)),
        ],
    )(w, fext, up, down, image, image_rim, coef, coef_rim, lines)


def solution(mesh):
    fine = Mesh(mesh.devices.reshape(3, 4, 4, 8, 2), ("zl", "x", "zh", "y", "c"))
    gx, gy = ("zl", "x"), ("zh", "y", "c")
    return jax.shard_map(
        body,
        mesh=fine,
        in_specs=(P(gx, gy, None), P(None, gx, gy, None), P(gx, gy, None), P()),
        out_specs=(P(None, gx, gy, None), P(gx, gy, None)),
        check_vma=False,
    )
```

time: 103 us -> 82 us (0.80)
  starting transfers between devices: 33.1 us -> 19.6 us
  local copies, waits for them, and re-layouts: 6.02 us -> 0.02 us
  blocking collectives: 52.5 us -> 46.6 us
  waiting for transfers between devices: 1.25 us -> 4.78 us
    ppermute x8 -> x4, starting transfers between devices: 33.1 us -> 19.6 us  [the longest x2 13.7 us: swap(): up = lax.ppermute(lo, axes, [(i + 1, i) for i in range(count - 1)])]
    unnamed x16 -> x0, local copies, waits for them, and re-layouts: 5.99 us -> none
    all_to_all x2, blocking collectives: 52.5 us -> 46.6 us  [spread_sum(): return lax.all_to_all(lines, axes, 0, 0, tiled=True)]
    ppermute x8 -> x4, waiting for transfers between devices: 1.25 us -> 4.78 us  [the longest x2 4.6 us: swap(): down = lax.ppermute(hi, axes, [(i, i + 1) for i in range(count - 1)])]
    pallas_call x2 -> x4, Pallas kernels: 6.25 us -> 7.02 us  [the longest x1 2.48 us: body(): call(inner_kernel, (f32(14, *plane), f32(14, *plane), f32(3, 12, *plane),...]
  transfers between devices with their start and end apart: 8 -> 4, of which waited for: 1 -> 3; matrix products, arithmetic and copies ran while one was open for 0% -> 0% of each run, Pallas kernels for 0% -> 3%
where the time goes in v3:
time: 82 us; the launch traced here: 81.7 us
  blocking collectives  46.6 us (57%)
  starting transfers between devices  19.6 us (24%)
  Pallas kernels  9.82 us (12%)
  waiting for transfers between devices  4.78 us (6%)
    all_to_all x2, blocking collectives, spread_sum(): return lax.all_to_all(lines, axes, 0, 0, tiled=True)  46.6 us
    ppermute x2, starting transfers between devices, swap(): up = lax.ppermute(lo, axes, [(i + 1, i) for i in range(count - 1)])  13.7 us
    ppermute x2, starting transfers between devices, swap(): down = lax.ppermute(hi, axes, [(i, i + 1) for i in range(count - 1)])  5.92 us
    ppermute x2, waiting for transfers between devices, swap(): down = lax.ppermute(hi, axes, [(i, i + 1) for i in range(count - 1)])  4.6 us
    pallas_call x1, Pallas kernels, body(): call(last_kernel, (f32(3, CX, CY, CZ), f32(CX, CY, CZ)), [SMEM] + [VMEM]...  2.81 us
    pallas_call x1, Pallas kernels, body(): call(inner_kernel, (f32(14, *plane), f32(14, *plane), f32(3, 12, *plane),...  2.48 us
    pallas_call x1, Pallas kernels, body(): call(pack_y_kernel, (f32(CX, CY, CZ), f32(3, CX, CY, CZ), f32(8, CZ), f32...  2.39 us
    pallas_call x1, Pallas kernels, body(): call(rim_kernel, (f32(3, 2, 4, *plane), f32(2, 4, *plane), f32(1, 128)),...  2.02 us
  transfers between devices with their start and end apart: 4, of which 3 were waited for; matrix products, arithmetic and copies ran while one was open for 0% of the time, Pallas kernels for 3%

profile of v3, /device:TPU:1, one launch (start us, length us, event | category | flops | bytes accessed | tf_op | source)
XLA Modules:
  0.0 81.7 jit_solution(7798302318866452295)
XLA Ops:
  0.6 2.4 %shard_map.59 = (f32[16,8,256]{2,1,0:T(8,128)S(1)}, f32[3,16,8,256]{3,2,1,0:T(8,128)S(1)}, f32[8,256]{1,0:T(8,128)S(1)}, f32[27]{0:T(128)S(1)}, f32[216,256]{1,0:T(8,128)S(1)}, /*index=5*/f32[216,256]{1,0:T(8,128)S(1)}) custom-call(s32[3,14]{1,0:T(4,128)} %bitcast.10, f32[16,8,256]{2,1,0:T(8,128)} %den_hbm.1, f32[3,16,8,256]{3,2,1,0:T(8,128)} %f_hbm.1, ...), custom_call_target="tpu_custom_call" | custom-call | tf_op jit(solution)/shard_map/pallas_call | solution.py:462
  3.0 12.4 %collective-permute-start = (f32[216,256]{1,0:T(8,128)S(1)}, f32[216,256]{1,0:T(8,128)S(1)}, u32[]{:S(2)}, u32[]{:S(2)}) collective-permute-start(f32[216,256]{1,0:T(8,128)S(1)} %get-tuple-element.24), channel_id=1, source_target_pairs={{1,0},{2,1},{3,2},{4,3},{5,4},{6,5},{7,6},{8,7},{9,8},{10,9},{11,1... | collective-permute-start | bytes 663560 | tf_op jit(solution)/shard_map/ppermute | solution.py:446
  15.5 1.9 %collective-permute-start.1 = (f32[216,256]{1,0:T(8,128)S(1)}, f32[216,256]{1,0:T(8,128)S(1)}, u32[]{:S(2)}, u32[]{:S(2)}) collective-permute-start(f32[216,256]{1,0:T(8,128)S(1)} %get-tuple-element.25), channel_id=1, source_target_pairs={{0,1},{1,2},{2,3},{3,4},{4,5},{5,6},{6,7},{7,8},{8,9},{9,10},{10,1... | collective-permute-start | bytes 663560 | tf_op jit(solution)/shard_map/ppermute | solution.py:447
  17.4 0.0 collective-permute-done.up_ref
  17.4 2.8 %collective-permute-done.1.dn_ref = f32[216,256]{1,0:T(8,128)S(1)} collective-permute-done((f32[216,256]{1,0:T(8,128)S(1)}, f32[216,256]{1,0:T(8,128)S(1)}, u32[]{:S(2)}, u32[]{:S(2)}) %collective-permute-start.1) | collective-permute-done | bytes 221216 | tf_op jit(solution)/shard_map/ppermute | solution.py:447
  20.2 0.1 shard_map.60
  20.4 1.3 %collective-permute-start.2 = (f32[13,16,256]{2,1,0:T(8,128)S(1)}, f32[13,16,256]{2,1,0:T(8,128)S(1)}, u32[]{:S(2)}, u32[]{:S(2)}) collective-permute-start(f32[13,16,256]{2,1,0:T(8,128)S(1)} %get-tuple-element.27), channel_id=1, source_target_pairs={{64,0},{128,64},{192,128},{256,192},{320,256},{384,320},{448,384},... | collective-permute-start | bytes 638984 | tf_op jit(solution)/shard_map/ppermute | solution.py:446
  21.7 4.0 %collective-permute-start.3 = (f32[13,16,256]{2,1,0:T(8,128)S(1)}, f32[13,16,256]{2,1,0:T(8,128)S(1)}, u32[]{:S(2)}, u32[]{:S(2)}) collective-permute-start(f32[13,16,256]{2,1,0:T(8,128)S(1)} %get-tuple-element.28), channel_id=1, source_target_pairs={{0,64},{64,128},{128,192},{192,256},{256,320},{320,384},{384,448},... | collective-permute-start | bytes 638984 | tf_op jit(solution)/shard_map/ppermute | solution.py:447
  25.7 0.1 pad_add_fusion.pos_ref
  25.8 2.5 %shard_map.61 = (f32[14,16,256]{2,1,0:T(8,128)S(1)}, f32[14,16,256]{2,1,0:T(8,128)S(1)}, f32[3,12,16,256]{3,2,1,0:T(8,128)S(1)}, f32[4,8,256]{2,1,0:T(8,128)S(1)}, f32[3,16,256]{2,1,0:T(8,128)S(1)}) custom-call(s32[2]{0:T(128)S(1)} %pad_add_fusion.pos_ref, f32[27]{0:T(128)S(1)} %get-tuple-element.20.w_ref, f32[16,16,256]{2,1,0:T(8,128)S(1)} %get-tuple-element.29.dext_ref, ...), custom_call_target="tpu_custom_call" | custom-call | flops 8000000 | bytes 8000000 | tf_op jit(solution)/shard_map/pallas_call | solution.py:478
  28.3 0.2 collective-permute-done.2.xu_ref
  28.4 1.8 %collective-permute-done.3.xd_ref = f32[13,16,256]{2,1,0:T(8,128)S(1)} collective-permute-done((f32[13,16,256]{2,1,0:T(8,128)S(1)}, f32[13,16,256]{2,1,0:T(8,128)S(1)}, u32[]{:S(2)}, u32[]{:S(2)}) %collective-permute-start.3) | collective-permute-done | bytes 213024 | tf_op jit(solution)/shard_map/ppermute | solution.py:447
  30.2 2.0 %shard_map.62 = (f32[3,2,4,16,256]{4,3,2,1,0:T(8,128)S(1)}, f32[2,4,16,256]{3,2,1,0:T(8,128)S(1)}, f32[1,128]{1,0:T(1,128)S(1)}) custom-call(s32[2]{0:T(128)S(1)} %pad_add_fusion.pos_ref, f32[27]{0:T(128)S(1)} %get-tuple-element.20.w_ref, f32[16,16,256]{2,1,0:T(8,128)S(1)} %get-tuple-element.29.dext_ref, f32[3,16,16,256]{3,2,1,0:T(8,128)S(1)} %get-tuple-element.26.fext_ref, ...), custom_call_target="tpu_custom_call" | custom-call | tf_op jit(solution)/shard_map/pallas_call | solution.py:486
  32.2 14.1 %all_to_all.14 = f32[32,1,128]{2,1,0:T(1,128)S(1)} all-to-all(f32[32,1,128]{2,1,0:T(1,128)S(1)} %broadcast_in_dim.4), channel_id=1, replica_groups=mesh['zl'=3,'x'=4,'zh'=4,'y'=8,'c'=2] {'x','y'}, dimensions={0} | all-to-all | bytes 32768 | tf_op jit(solution)/shard_map/all_to_all | solution.py:453
  46.4 32.5 %all_to_all.15 = f32[24,1,128]{2,1,0:T(1,128)S(1)} all-to-all(f32[24,1,128]{2,1,0:T(1,128)S(1)} %broadcast_in_dim.5), channel_id=1, replica_groups=mesh['zl'=3,'x'=4,'zh'=4,'y'=8,'c'=2] {'zl','zh','c'}, dimensions={0} | all-to-all | bytes 24576 | tf_op jit(solution)/shard_map/all_to_all | solution.py:453
  78.9 2.8 %shard_map.63 = (f32[3,16,8,256]{3,2,1,0:T(8,128)}, f32[16,8,256]{2,1,0:T(8,128)}) custom-call(f32[27]{0:T(128)S(1)} %get-tuple-element.20.w_ref, f32[3,16,16,256]{3,2,1,0:T(8,128)S(1)} %get-tuple-element.26.fext_ref, f32[13,16,256]{2,1,0:T(8,128)S(1)} %collective-permute-done.2.xu_ref, f32[13,16,256]{2,1,0:T(8,128)S(1)} %collective-permute-done.3.xd_ref, ...), custom_call_target="tpu_custom_call" | custom-call | tf_op jit(solution)/shard_map/pallas_call | solution.py:500
  (3 shorter events, 0.0 us)
Async XLA Ops:
  3.0 14.4 %collective-permute-start = (f32[216,256]{1,0:T(8,128)S(1)}, f32[216,256]{1,0:T(8,128)S(1)}, u32[]{:S(2)}, u32[]{:S(2)}) collective-permute-start(f32[216,256]{1,0:T(8,128)S(1)} %get-tuple-element.24), channel_id=1, source_target_pairs={{1,0},{2,1},{3,2},{4,3},{5,4},{6,5},{7,6},{8,7},{9,8},{10,9},{11,1... | collective-permute-start | bytes 663560 | tf_op jit(solution)/shard_map/ppermute | solution.py:446
  15.5 4.8 %collective-permute-start.1 = (f32[216,256]{1,0:T(8,128)S(1)}, f32[216,256]{1,0:T(8,128)S(1)}, u32[]{:S(2)}, u32[]{:S(2)}) collective-permute-start(f32[216,256]{1,0:T(8,128)S(1)} %get-tuple-element.25), channel_id=1, source_target_pairs={{0,1},{1,2},{2,3},{3,4},{4,5},{5,6},{6,7},{7,8},{8,9},{9,10},{10,1... | collective-permute-start | bytes 663560 | tf_op jit(solution)/shard_map/ppermute | solution.py:447
  20.4 8.1 %collective-permute-start.2 = (f32[13,16,256]{2,1,0:T(8,128)S(1)}, f32[13,16,256]{2,1,0:T(8,128)S(1)}, u32[]{:S(2)}, u32[]{:S(2)}) collective-permute-start(f32[13,16,256]{2,1,0:T(8,128)S(1)} %get-tuple-element.27), channel_id=1, source_target_pairs={{64,0},{128,64},{192,128},{256,192},{320,256},{384,320},{448,384},... | collective-permute-start | bytes 638984 | tf_op jit(solution)/shard_map/ppermute | solution.py:446
  21.7 8.5 %collective-permute-start.3 = (f32[13,16,256]{2,1,0:T(8,128)S(1)}, f32[13,16,256]{2,1,0:T(8,128)S(1)}, u32[]{:S(2)}, u32[]{:S(2)}) collective-permute-start(f32[13,16,256]{2,1,0:T(8,128)S(1)} %get-tuple-element.28), channel_id=1, source_target_pairs={{0,64},{64,128},{128,192},{192,256},{256,320},{320,384},{384,448},... | collective-permute-start | bytes 638984 | tf_op jit(solution)/shard_map/ppermute | solution.py:447

commit v4 on v3

--- a/solution.py
+++ b/solution.py
@@ -16,6 +16,7 @@
 CX, CY, CZ = 16, 8, 256
 NX, NY = 192, 512
 DEV_X, DEV_Y = 12, 64
+GX, GY = ("zl", "x"), ("zh", "y", "c")
 ROWS = 16
 F32 = jnp.float32
 UNROLL = (7, 4, 5, 8, 4, 1, 6, 4)
@@ -47,6 +48,10 @@
 
 def zm(v, lane, fill=0.0):
     return jnp.where(lane == 0, fill, roll(v, 1, 1))
+
+
+def is_odd(at):
+    return lax.bitwise_and(at, 1)
 
 
 def store_weights(off_ref, w_ref):
@@ -68,7 +73,7 @@
 
 
 def pack_y_kernel(
-    off_ref, den_hbm, f_hbm, ids_hbm, den_ref, f_ref, m_ref, w_ref, lo_ref, hi_ref, ids_ref, sem
+    den_hbm, f_hbm, ids_hbm, den_ref, f_ref, m_ref, first_ref, second_ref, ids_ref, sem
 ):
     copies = [
         pltpu.make_async_copy(src, dst, sem.at[i])
@@ -76,7 +81,6 @@
     ]
     for copy in copies:
         copy.start()
-    store_weights(off_ref, w_ref)
     copies[0].wait()
     ids = ids_ref[...]
     row = lax.shift_right_logical(ids, 6)
@@ -87,25 +91,39 @@
     ).astype(jnp.bfloat16)
     flags = lax.dot_general(p, q, (((1,), (1,)), ((), ())), preferred_element_type=F32)
     m_ref[...] = flags
-    lo_ref[208:216] = flags
-    hi_ref[208:216] = flags
     copies[1].wait()
+    copies[2].wait()
     den = jnp.swapaxes(den_ref[...], 0, 1)
+    fs = [jnp.swapaxes(f_ref[c], 0, 1) for c in range(3)]
+
+    odd = jnp.full((CX, CZ), is_odd(lax.axis_index(GY)), jnp.int32) == 1
+
+    def fill(at, lo, hi):
+        first_ref[at : at + 16] = jnp.where(odd, hi, lo)
+        second_ref[at : at + 16] = jnp.where(odd, lo, hi)
+
+    first_ref[208:216] = flags
+    second_ref[208:216] = flags
     for j in range(4):
-        lo_ref[16 * j : 16 * j + 16] = den[j]
-        hi_ref[16 * j : 16 * j + 16] = den[4 + j]
-    copies[2].wait()
+        fill(16 * j, den[j], den[4 + j])
     for c in range(3):
-        f = jnp.swapaxes(f_ref[c], 0, 1)
         for j in range(3):
-            at = 64 + 16 * (3 * c + j)
-            lo_ref[at : at + 16] = f[j]
-            hi_ref[at : at + 16] = f[5 + j]
-
-
-def pack_x_kernel(den_ref, f_ref, m_ref, up_ref, dn_ref, dext_ref, fext_ref, lo_ref, hi_ref):
-    def spread_flags(ref, first, by):
-        rows = [ref[first + 2 * bx + by : first + 2 * bx + by + 1] for bx in range(4)]
+            fill(64 + 16 * (3 * c + j), fs[c][j], fs[c][5 + j])
+
+
+def pack_x_kernel(
+    den_ref, f_ref, m_ref, first_in, second_in, dext_ref, fext_ref, first_ref, second_ref
+):
+    odd_y = jnp.full((CX, CZ), is_odd(lax.axis_index(GY)), jnp.int32) == 1
+
+    def below(first, count):
+        return jnp.where(odd_y[0:count], second_in[first : first + count], first_in[first : first + count])
+
+    def above(first, count):
+        return jnp.where(odd_y[0:count], first_in[first : first + count], second_in[first : first + count])
+
+    def spread_flags(flags, by):
+        rows = [flags[2 * bx + by : 2 * bx + by + 1] for bx in range(4)]
         return jnp.concatenate([jnp.broadcast_to(r, (4, CZ)) for r in rows], axis=0)
 
     def halo_rows(planes):
@@ -113,23 +131,25 @@
 
     dext_ref[:, 0:8] = den_ref[...]
     dext_ref[:, 8:16] = halo_rows(
-        [up_ref[16 * j : 16 * j + 16] for j in range(4)] + [dn_ref[16 * j : 16 * j + 16] for j in range(4)]
+        [above(16 * j, 16) for j in range(4)] + [below(16 * j, 16) for j in range(4)]
     )
+    own = m_ref[...]
     flags = (
-        [spread_flags(up_ref, 208, 0), spread_flags(dn_ref, 208, 1)],
-        [spread_flags(m_ref, 0, 0), spread_flags(m_ref, 0, 1)],
+        [spread_flags(above(208, 8), 0), spread_flags(below(208, 8), 1)],
+        [spread_flags(own, 0), spread_flags(own, 1)],
         [jnp.zeros((CX, CZ), F32)] * 2,
     )
     for c in range(3):
         at = [64 + 16 * (3 * c + j) for j in range(3)]
         fext_ref[c, :, 0:8] = f_ref[c]
         fext_ref[c, :, 8:16] = halo_rows(
-            [up_ref[i : i + 16] for i in at] + flags[c] + [dn_ref[i : i + 16] for i in at]
-        )
-    for slab, dx0, fx0 in ((lo_ref, 0, 0), (hi_ref, 12, 13)):
-        slab[0:4] = dext_ref[dx0 : dx0 + 4]
-        for c in range(3):
-            slab[4 + 3 * c : 7 + 3 * c] = fext_ref[c, fx0 : fx0 + 3]
+            [above(i, 16) for i in at] + flags[c] + [below(i, 16) for i in at]
+        )
+    odd_x = is_odd(lax.axis_index(GX))
+    for slab, top in ((first_ref, odd_x), (second_ref, 1 - odd_x)):
+        slab[0:4] = dext_ref[pl.ds(12 * top, 4)]
+        for c in range(3):
+            slab[4 + 3 * c : 7 + 3 * c] = fext_ref[c, pl.ds(13 * top, 3)]
 
 
 def filter_plane(planes, w_ref, lane, sign):
@@ -223,11 +243,12 @@
 
 
 def inner_kernel(
-    pos_ref, w_ref, dext_ref, fext_ref, s_ref, coef_ref, g_ref, sums_ref, rwt_ref
+    off_ref, dext_ref, fext_ref, w_ref, s_ref, coef_ref, g_ref, sums_ref, rwt_ref
 ):
-    gx, gy = pos_ref[0], pos_ref[1]
+    gx, gy = lax.axis_index(GX), lax.axis_index(GY)
     lane = lane_iota(ROWS)
     iy = grid_y(gy)
+    store_weights(off_ref, w_ref)
     store_reciprocals(rwt_ref, w_ref, iy)
 
     def smooth_step(p, _):
@@ -265,26 +286,42 @@
 
 
 def rim_kernel(
-    pos_ref, w_ref, dext_ref, fext_ref, xu_ref, xd_ref, s_in_ref, g_in_ref, sums_ref, rwt_ref,
-    g_ref, coef_ref, mom_ref,
-    d2_ref, f2_ref, s2_ref, g2_ref,
+    w_in, dext_ref, fext_ref, first_in, second_in, s_in_ref, g_in_ref, sums_ref, rwt_ref,
+    g_ref, coef_ref, f_rim_ref, mom_ref,
+    d2_ref, f2_ref, s2_ref, g2_ref, w_ref, sem,
 ):
-    gx, gy = pos_ref[0], pos_ref[1]
+    w_copy = pltpu.make_async_copy(w_in, w_ref, sem)
+    w_copy.start()
+    gx, gy = lax.axis_index(GX), lax.axis_index(GY)
     lane = lane_iota(ROWS)
     iy = grid_y(gy)
-    d2_ref[0, 0:4] = xd_ref[0:4]
     d2_ref[0, 4:6] = dext_ref[0:2]
     d2_ref[1, 0:2] = dext_ref[14:16]
-    d2_ref[1, 2:6] = xu_ref[0:4]
     s2_ref[0, 4:7] = s_in_ref[0:3]
     s2_ref[1, 0:3] = s_in_ref[11:14]
     for c in range(3):
-        f2_ref[c, 0, 0:3] = xd_ref[4 + 3 * c : 7 + 3 * c]
         f2_ref[c, 0, 3:6] = fext_ref[c, 0:3]
         f2_ref[c, 1, 0:3] = fext_ref[c, 13:16]
-        f2_ref[c, 1, 3:6] = xu_ref[4 + 3 * c : 7 + 3 * c]
         g2_ref[c, 0, 4:6] = g_in_ref[c, 0:2]
         g2_ref[c, 1, 0:2] = g_in_ref[c, 10:12]
+
+    odd = jnp.full((ROWS, CZ), is_odd(gx), jnp.int32) == 1
+    for k in range(13):
+        one, two = first_in[k], second_in[k]
+        below, above = jnp.where(odd, two, one), jnp.where(odd, one, two)
+        if k < 4:
+            d2_ref[0, k] = below
+            d2_ref[1, 2 + k] = above
+            continue
+        c, i = (k - 4) // 3, (k - 4) % 3
+        f2_ref[c, 0, i] = below
+        f2_ref[c, 1, 3 + i] = above
+        if i >= 1:
+            f_rim_ref[c, 0, i - 1] = below
+        if i <= 1:
+            f_rim_ref[c, 1, i] = above
+
+    w_copy.wait()
 
     def smooth_step(i, _):
         side, m = lax.shift_right_logical(i, 2), lax.bitwise_and(i, 3)
@@ -335,10 +372,12 @@
 
 
 def last_kernel(
-    w_ref, fext_ref, xu_ref, xd_ref, g_in_ref, g_rim_ref, coef_in_ref, coef_rim_ref, mom_ref,
+    w_in, fext_ref, f_rim_ref, g_in_ref, g_rim_ref, coef_in_ref, coef_rim_ref, mom_ref,
     u_hbm, sens_hbm,
-    u_ref, sh_ref, coef_ref, own_ref, sens_ref, sem,
+    u_ref, sh_ref, coef_ref, own_ref, sens_ref, w_ref, sem,
 ):
+    w_copy = pltpu.make_async_copy(w_in, w_ref, sem.at[3])
+    w_copy.start()
     lane = lane_iota(ROWS)
     line = jnp.sum(mom_ref[...], axis=0, keepdims=True)
     at = lax.broadcasted_iota(jnp.int32, (1, 128), 1)
@@ -374,8 +413,12 @@
             own_ref[c, x] = us[c][0:8]
     u_copy = pltpu.make_async_copy(own_ref, u_hbm, sem.at[0])
     u_copy.start()
-    for q, slab, i, side, m in ((0, xd_ref, 1, 0, 0), (1, xd_ref, 2, 0, 1), (18, xu_ref, 0, 1, 2), (19, xu_ref, 1, 1, 3)):
-        u_plane(q, [slab[4 + 3 * c + i] for c in range(3)], [g_rim_ref[c, side, m] for c in range(3)])
+    for q, side, i in ((0, 0, 0), (1, 0, 1), (18, 1, 0), (19, 1, 1)):
+        u_plane(
+            q,
+            [f_rim_ref[c, side, i] for c in range(3)],
+            [g_rim_ref[c, side, i + 2 * side] for c in range(3)],
+        )
     coef_ref[0:2] = coef_rim_ref[0, 2:4]
     coef_ref[2:16] = coef_in_ref[...]
     coef_ref[16:18] = coef_rim_ref[1, 0:2]
@@ -408,6 +451,7 @@
         sens_ref[x] = filter_plane(planes, w_ref, lane, -1)[0:8]
         return 0
 
+    w_copy.wait()
     half = CX // 2
     copies = [u_copy]
     for k in range(2):
@@ -428,6 +472,7 @@
 
 
 HBM = pl.BlockSpec(memory_space=pltpu.HBM)
+ANY = pl.BlockSpec(memory_space=pl.ANY)
 
 
 def call(kernel, outs, ins, out_specs, scratch, cost=None):
@@ -442,10 +487,12 @@
     )
 
 
-def swap(lo, hi, axes, count):
-    up = lax.ppermute(lo, axes, [(i + 1, i) for i in range(count - 1)])
-    down = lax.ppermute(hi, axes, [(i, i + 1) for i in range(count - 1)])
-    return up, down
+def swap(first, second, axes, count):
+    got = []
+    for slab, start in ((first, 1), (second, 0)):
+        pairs = [(i, i + 1) for i in range(start, count - 1, 2)]
+        got.append(lax.ppermute(slab, axes, pairs + [(b, a) for a, b in pairs]))
+    return got
 
 
 def spread_sum(line, axes, count):
@@ -454,53 +501,53 @@
 
 
 def body(density, force, brick_ids, offsets):
-    gx, gy = ("zl", "x"), ("zh", "y", "c")
-    pos = jnp.stack([lax.axis_index(gx), lax.axis_index(gy)]).astype(jnp.int32)
-    ins = (offsets.T, density, force, brick_ids.reshape(1, 512))
+    ins = (density, force, brick_ids.reshape(1, 512))
     plane = (ROWS, CZ)
     slab_y, slab_x = f32(216, CZ), f32(13, *plane)
-    den, f, mask, w, lo, hi = call(
+    den, f, mask, first, second = call(
         pack_y_kernel,
-        (f32(CX, CY, CZ), f32(3, CX, CY, CZ), f32(8, CZ), f32(27), slab_y, slab_y),
-        [SMEM, HBM, HBM, HBM],
-        (VMEM, VMEM, VMEM, SMEM, VMEM, VMEM),
+        (f32(CX, CY, CZ), f32(3, CX, CY, CZ), f32(8, CZ), slab_y, slab_y),
+        [HBM, HBM, HBM],
+        (VMEM,) * 5,
         [pltpu.VMEM((1, 512), jnp.int32), pltpu.SemaphoreType.DMA((3,))],
     )(*(pltpu.with_memory_space_constraint(a, pltpu.HBM) for a in ins))
-    up, down = swap(lo, hi, gy, DEV_Y)
-    dext, fext, lo, hi = call(
+    first, second = swap(first, second, GY, DEV_Y)
+    dext, fext, first, second = call(
         pack_x_kernel,
         (f32(CX, *plane), f32(3, CX, *plane), slab_x, slab_x),
         [VMEM] * 5,
         (VMEM,) * 4,
         [],
-    )(den, f, mask, up, down)
-    up, down = swap(lo, hi, gx, DEV_X)
-    stiff, coef, image, sums, rwt = call(
+    )(den, f, mask, first, second)
+    first, second = swap(first, second, GX, DEV_X)
+    w, stiff, coef, image, sums, rwt = call(
         inner_kernel,
-        (f32(14, *plane), f32(14, *plane), f32(3, 12, *plane), f32(4, 8, CZ), f32(3, *plane)),
-        [SMEM, SMEM, VMEM, VMEM],
-        (VMEM,) * 5,
+        (f32(128), f32(14, *plane), f32(14, *plane), f32(3, 12, *plane), f32(4, 8, CZ), f32(3, *plane)),
+        [SMEM, VMEM, VMEM],
+        (SMEM,) + (VMEM,) * 5,
         [],
         pl.CostEstimate(flops=8_000_000, bytes_accessed=8_000_000, transcendentals=0),
-    )(pos, w, dext, fext)
-    image_rim, coef_rim, line = call(
+    )(pltpu.with_memory_space_constraint(offsets.T, pltpu.HBM), dext, fext)
+    image_rim, coef_rim, f_rim, line = call(
         rim_kernel,
-        (f32(3, 2, 4, *plane), f32(2, 4, *plane), f32(1, 128)),
-        [SMEM, SMEM] + [VMEM] * 8,
-        (VMEM,) * 3,
+        (f32(3, 2, 4, *plane), f32(2, 4, *plane), f32(3, 2, 2, *plane), f32(1, 128)),
+        [ANY] + [VMEM] * 8,
+        (VMEM,) * 4,
         [
             pltpu.VMEM((2, 6, *plane), F32),
             pltpu.VMEM((3, 2, 6, *plane), F32),
             pltpu.VMEM((2, 7, *plane), F32),
             pltpu.VMEM((3, 2, 6, *plane), F32),
+            pltpu.SMEM((128,), F32),
+            pltpu.SemaphoreType.DMA(()),
         ],
-    )(pos, w, dext, fext, up, down, stiff, image, sums, rwt)
+    )(w, dext, fext, first, second, stiff, image, sums, rwt)
     lines = spread_sum(line, ("x", "y"), 32)
     lines = spread_sum(jnp.sum(lines, axis=0, keepdims=True), ("zl", "zh", "c"), 24)
     return call(
         last_kernel,
         (f32(3, CX, CY, CZ), f32(CX, CY, CZ)),
-        [SMEM] + [VMEM] * 8,
+        [ANY] + [VMEM] * 7,
         (HBM, HBM),
         [
             pltpu.VMEM((3, CX + 4, *plane), F32),
@@ -508,18 +555,18 @@
             pltpu.VMEM((CX + 2, *plane), F32),
             pltpu.VMEM((3, CX, CY, CZ), F32),
             pltpu.VMEM((CX, CY, CZ), F32),
-            pltpu.SemaphoreType.DMA((3,)),
+            pltpu.SMEM((128,), F32),
+            pltpu.SemaphoreType.DMA((4,)),
         ],
-    )(w, fext, up, down, image, image_rim, coef, coef_rim, lines)
+    )(w, fext, f_rim, image, image_rim, coef, coef_rim, lines)
 
 
 def solution(mesh):
     fine = Mesh(mesh.devices.reshape(3, 4, 4, 8, 2), ("zl", "x", "zh", "y", "c"))
-    gx, gy = ("zl", "x"), ("zh", "y", "c")
     return jax.shard_map(
         body,
         mesh=fine,
-        in_specs=(P(gx, gy, None), P(None, gx, gy, None), P(gx, gy, None), P()),
-        out_specs=(P(None, gx, gy, None), P(gx, gy, None)),
+        in_specs=(P(GX, GY, None), P(None, GX, GY, None), P(GX, GY, None), P()),
+        out_specs=(P(None, GX, GY, None), P(GX, GY, None)),
         check_vma=False,
     )

time: 82 us -> 73.8 us (0.90)
  starting transfers between devices: 19.6 us -> 15.7 us
  blocking collectives: 46.6 us -> 43.8 us
  Pallas kernels: 9.82 us -> 8.99 us
    ppermute x4, starting transfers between devices: 19.6 us -> 15.7 us  [swap(): got.append(lax.ppermute(slab, axes, pairs + [(b, a) for a, b in pairs]))]
    all_to_all x2, blocking collectives: 46.6 us -> 43.8 us  [spread_sum(): return lax.all_to_all(lines, axes, 0, 0, tiled=True)]
    pallas_call x4, Pallas kernels: 9.69 us -> 8.82 us  [the longest x1 3.32 us: body(): call(inner_kernel, (f32(128), f32(14, *plane), f32(14, *plane), f32(3, 12...]
  transfers between devices with their start and end apart: 4 -> 4, of which waited for: 3 -> 2; matrix products, arithmetic and copies ran while one was open for 0% -> 0% of each run, Pallas kernels for 3% -> 5%
where the time goes in v4:
time: 73.8 us; the launch traced here: 73.4 us
  blocking collectives  43.8 us (59%)
  starting transfers between devices  15.7 us (21%)
  Pallas kernels  8.99 us (12%)
  waiting for transfers between devices  4.17 us (6%)
    all_to_all x2, blocking collectives, spread_sum(): return lax.all_to_all(lines, axes, 0, 0, tiled=True)  43.8 us
    ppermute x4, starting transfers between devices, swap(): got.append(lax.ppermute(slab, axes, pairs + [(b, a) for a, b in pairs]))  15.7 us
    ppermute x4, waiting for transfers between devices, swap(): got.append(lax.ppermute(slab, axes, pairs + [(b, a) for a, b in pairs]))  4.17 us
    pallas_call x1, Pallas kernels, body(): call(inner_kernel, (f32(128), f32(14, *plane), f32(14, *plane), f32(3, 12...  3.32 us
    pallas_call x1, Pallas kernels, body(): call(last_kernel, (f32(3, CX, CY, CZ), f32(CX, CY, CZ)), [ANY] + [VMEM] *...  2.29 us
    pallas_call x1, Pallas kernels, body(): call(rim_kernel, (f32(3, 2, 4, *plane), f32(2, 4, *plane), f32(3, 2, 2, *...  2 us
  transfers between devices with their start and end apart: 4, of which 2 were waited for; matrix products, arithmetic and copies ran while one was open for 0% of the time, Pallas kernels for 5%

profile of v4, /device:TPU:1, one launch (start us, length us, event | category | flops | bytes accessed | tf_op | source)
XLA Modules:
  0.0 73.4 jit_solution(11792620950456536038)
XLA Ops:
  0.6 1.2 %shard_map.59 = (f32[16,8,256]{2,1,0:T(8,128)S(1)}, f32[3,16,8,256]{3,2,1,0:T(8,128)S(1)}, f32[8,256]{1,0:T(8,128)S(1)}, f32[216,256]{1,0:T(8,128)S(1)}, f32[216,256]{1,0:T(8,128)S(1)}) custom-call(f32[16,8,256]{2,1,0:T(8,128)} %den_hbm.1, f32[3,16,8,256]{3,2,1,0:T(8,128)} %f_hbm.1, s32[1,512]{1,0:T(1,128)} %bitcast.8), custom_call_target="tpu_custom_call" | custom-call | tf_op jit(solution)/shard_map/pallas_call | solution.py:507
  1.8 4.6 %collective-permute-start = (f32[216,256]{1,0:T(8,128)S(1)}, f32[216,256]{1,0:T(8,128)S(1)}, u32[]{:S(2)}, u32[]{:S(2)}) collective-permute-start(f32[216,256]{1,0:T(8,128)S(1)} %get-tuple-element.24), channel_id=1, source_target_pairs={{1,2},{3,4},{5,6},{7,8},{9,10},{11,12},{13,14},{15,16},{17,18},{19... | collective-permute-start | bytes 663560 | tf_op jit(solution)/shard_map/ppermute | solution.py:494
  6.5 8.5 %collective-permute-start.1 = (f32[216,256]{1,0:T(8,128)S(1)}, f32[216,256]{1,0:T(8,128)S(1)}, u32[]{:S(2)}, u32[]{:S(2)}) collective-permute-start(f32[216,256]{1,0:T(8,128)S(1)} %get-tuple-element.25), channel_id=1, source_target_pairs={{0,1},{2,3},{4,5},{6,7},{8,9},{10,11},{12,13},{14,15},{16,17},{18,... | collective-permute-start | bytes 663560 | tf_op jit(solution)/shard_map/ppermute | solution.py:494
  15.0 0.0 collective-permute-done.first_in
  15.0 1.1 %collective-permute-done.1.second_in = f32[216,256]{1,0:T(8,128)S(1)} collective-permute-done((f32[216,256]{1,0:T(8,128)S(1)}, f32[216,256]{1,0:T(8,128)S(1)}, u32[]{:S(2)}, u32[]{:S(2)}) %collective-permute-start.1) | collective-permute-done | bytes 221216 | tf_op jit(solution)/shard_map/ppermute | solution.py:494
  16.0 0.2 shard_map.60
  16.2 0.7 collective-permute-start.2
  16.9 1.9 %collective-permute-start.3 = (f32[13,16,256]{2,1,0:T(8,128)S(1)}, f32[13,16,256]{2,1,0:T(8,128)S(1)}, u32[]{:S(2)}, u32[]{:S(2)}) collective-permute-start(f32[13,16,256]{2,1,0:T(8,128)S(1)} %get-tuple-element.30), channel_id=1, source_target_pairs={{0,64},{128,192},{256,320},{384,448},{512,576},{640,704},{64,0},{1... | collective-permute-start | bytes 638984 | tf_op jit(solution)/shard_map/ppermute | solution.py:494
  18.8 3.3 %shard_map.61 = (f32[128]{0:T(128)S(1)}, f32[14,16,256]{2,1,0:T(8,128)S(1)}, f32[14,16,256]{2,1,0:T(8,128)S(1)}, f32[3,12,16,256]{3,2,1,0:T(8,128)S(1)}, f32[4,8...) custom-call(s32[3,14]{1,0:T(4,128)} %bitcast.9, f32[16,16,256]{2,1,0:T(8,128)S(1)} %get-tuple-element.26.dext_ref, ...), custom_call_target="tpu_custom_call" | custom-call | flops 8000000 | bytes 8000000 | tf_op jit(solution)/shard_map/pallas_call | solution.py:523
  22.2 0.0 collective-permute-done.2.first_in
  22.2 3.1 %collective-permute-done.3.second_in = f32[13,16,256]{2,1,0:T(8,128)S(1)} collective-permute-done((f32[13,16,256]{2,1,0:T(8,128)S(1)}, f32[13,16,256]{2,1,0:T(8,128)S(1)}, u32[]{:S(2)}, u32[]{:S(2)}) %collective-permute-start.3) | collective-permute-done | bytes 213024 | tf_op jit(solution)/shard_map/ppermute | solution.py:494
  25.3 2.0 %shard_map.62 = (f32[3,2,4,16,256]{4,3,2,1,0:T(8,128)S(1)}, f32[2,4,16,256]{3,2,1,0:T(8,128)S(1)}, f32[3,2,2,16,256]{4,3,2,1,0:T(8,128)S(1)}, f32[1,128]{1,0:T(1,128)S(1)}) custom-call(f32[128]{0:T(128)S(1)} %get-tuple-element.28.w_in, f32[16,16,256]{2,1,0:T(8,128)S(1)} %get-tuple-element.26.dext_ref, f32[3,16,16,256]{3,2,1,0:T(8,128)S(1)} %get-tuple-element.27.fext_ref, ...), custom_call_target="tpu_custom_call" | custom-call | tf_op jit(solution)/shard_map/pallas_call | solution.py:531
  27.3 19.8 %all_to_all.14 = f32[32,1,128]{2,1,0:T(1,128)S(1)} all-to-all(f32[32,1,128]{2,1,0:T(1,128)S(1)} %broadcast_in_dim.4), channel_id=1, replica_groups=mesh['zl'=3,'x'=4,'zh'=4,'y'=8,'c'=2] {'x','y'}, dimensions={0} | all-to-all | bytes 32768 | tf_op jit(solution)/shard_map/all_to_all | solution.py:500
  47.1 24.0 %all_to_all.15 = f32[24,1,128]{2,1,0:T(1,128)S(1)} all-to-all(f32[24,1,128]{2,1,0:T(1,128)S(1)} %broadcast_in_dim.5), channel_id=1, replica_groups=mesh['zl'=3,'x'=4,'zh'=4,'y'=8,'c'=2] {'zl','zh','c'}, dimensions={0} | all-to-all | bytes 24576 | tf_op jit(solution)/shard_map/all_to_all | solution.py:500
  71.1 2.3 %shard_map.63 = (f32[3,16,8,256]{3,2,1,0:T(8,128)}, f32[16,8,256]{2,1,0:T(8,128)}) custom-call(f32[128]{0:T(128)S(1)} %get-tuple-element.28.w_in, f32[3,16,16,256]{3,2,1,0:T(8,128)S(1)} %get-tuple-element.27.fext_ref, f32[3,2,2,16,256]{4,3,2,1,0:T(8,128)S(1)} %get-tuple-element.35.f_rim_ref, f32[3,12,16,256]{3,2,1,0:T(8,128)S(1)} %get-tuple-element.32.g_in_ref, ...), custom_call_target="tpu_custom_call" | custom-call | tf_op jit(solution)/shard_map/pallas_call | solution.py:547
  (3 shorter events, 0.0 us)
Async XLA Ops:
  1.8 13.1 %collective-permute-start = (f32[216,256]{1,0:T(8,128)S(1)}, f32[216,256]{1,0:T(8,128)S(1)}, u32[]{:S(2)}, u32[]{:S(2)}) collective-permute-start(f32[216,256]{1,0:T(8,128)S(1)} %get-tuple-element.24), channel_id=1, source_target_pairs={{1,2},{3,4},{5,6},{7,8},{9,10},{11,12},{13,14},{15,16},{17,18},{19... | collective-permute-start | bytes 663560 | tf_op jit(solution)/shard_map/ppermute | solution.py:494
  6.5 9.6 %collective-permute-start.1 = (f32[216,256]{1,0:T(8,128)S(1)}, f32[216,256]{1,0:T(8,128)S(1)}, u32[]{:S(2)}, u32[]{:S(2)}) collective-permute-start(f32[216,256]{1,0:T(8,128)S(1)} %get-tuple-element.25), channel_id=1, source_target_pairs={{0,1},{2,3},{4,5},{6,7},{8,9},{10,11},{12,13},{14,15},{16,17},{18,... | collective-permute-start | bytes 663560 | tf_op jit(solution)/shard_map/ppermute | solution.py:494
  16.2 5.9 %collective-permute-start.2 = (f32[13,16,256]{2,1,0:T(8,128)S(1)}, f32[13,16,256]{2,1,0:T(8,128)S(1)}, u32[]{:S(2)}, u32[]{:S(2)}) collective-permute-start(f32[13,16,256]{2,1,0:T(8,128)S(1)} %get-tuple-element.29), channel_id=1, source_target_pairs={{64,128},{192,256},{320,384},{448,512},{576,640},{128,64},{256,192... | collective-permute-start | bytes 638984 | tf_op jit(solution)/shard_map/ppermute | solution.py:494
  16.9 8.4 %collective-permute-start.3 = (f32[13,16,256]{2,1,0:T(8,128)S(1)}, f32[13,16,256]{2,1,0:T(8,128)S(1)}, u32[]{:S(2)}, u32[]{:S(2)}) collective-permute-start(f32[13,16,256]{2,1,0:T(8,128)S(1)} %get-tuple-element.30), channel_id=1, source_target_pairs={{0,64},{128,192},{256,320},{384,448},{512,576},{640,704},{64,0},{1... | collective-permute-start | bytes 638984 | tf_op jit(solution)/shard_map/ppermute | solution.py:494

commit v5 on v4

--- a/solution.py
+++ b/solution.py
@@ -19,7 +19,7 @@
 GX, GY = ("zl", "x"), ("zh", "y", "c")
 ROWS = 16
 F32 = jnp.float32
-UNROLL = (7, 4, 5, 8, 4, 1, 6, 4)
+UNROLL = (7, 4, 5, 8, 4, 3, 9, 8)
 
 
 def sub_iota(rows):
@@ -146,13 +146,20 @@
             [above(i, 16) for i in at] + flags[c] + [below(i, 16) for i in at]
         )
     odd_x = is_odd(lax.axis_index(GX))
+    sub = sub_iota(8)
+    spare = (sub == 2) | (sub == 3)
     for slab, top in ((first_ref, odd_x), (second_ref, 1 - odd_x)):
-        slab[0:4] = dext_ref[pl.ds(12 * top, 4)]
-        for c in range(3):
-            slab[4 + 3 * c : 7 + 3 * c] = fext_ref[c, pl.ds(13 * top, 3)]
-
-
-def filter_plane(planes, w_ref, lane, sign):
+        near, deep = 13 * top, 2 + 11 * top
+        slab[0:4] = dext_ref[pl.ds(12 * top, 4), 0:8]
+        slab[13:17] = dext_ref[pl.ds(12 * top, 4), 8:16]
+        for c in range(3):
+            slab[4 + 3 * c : 7 + 3 * c] = fext_ref[c, pl.ds(near, 3), 0:8]
+            slab[17 + 2 * c] = fext_ref[c, 15 * top, 8:16]
+            deepest = roll(fext_ref[c, deep, 8:16], 3, 0)
+            slab[18 + 2 * c] = jnp.where(spare, deepest, fext_ref[c, 1 + 13 * top, 8:16])
+
+
+def filter_plane(planes, w_ref, lane, sign, rows=ROWS):
     out = None
     for dz in (-1, 0, 1):
         acc = None
@@ -160,12 +167,13 @@
             t = None
             for dx in (-1, 0, 1):
                 w = w_ref[(sign * dx + 1) * 9 + (sign * dy + 1) * 3 + sign * dz + 1]
-                term = planes[dx + 1] * w
+                term = planes[dx + 1][0 : rows if dy == 0 else ROWS] * w
                 t = term if t is None else t + term
             if dy == 1:
                 t = yp(t)
             elif dy == -1:
                 t = ym(t)
+            t = t[0:rows]
             acc = t if acc is None else acc + t
         if dz == 1:
             acc = zp(acc, lane)
@@ -175,17 +183,19 @@
     return out
 
 
-def image_plane(load, s_m, s_0, s_p, lane):
+def image_plane(load, s_m, s_0, s_p, lane, rows=ROWS):
+    py = 0.5 * (s_0 + yp(s_0))
+    s_m, s_0, s_p, lane = s_m[0:rows], s_0[0:rows], s_p[0:rows], lane[0:rows]
     px, mx = 0.5 * (s_0 + s_p), 0.5 * (s_0 + s_m)
-    py = 0.5 * (s_0 + yp(s_0))
     pz = 0.5 * (s_0 + zp(s_0, lane))
     half = -0.5 * s_0
     outs = []
     for c in range(3):
         v = load(c, 0)
-        fx = px * (v - load(c, 1)) + mx * (v - load(c, -1))
         fy = py * (v - yp(v))
-        fy = fy - ym(fy)
+        fy = fy[0:rows] - ym(fy)[0:rows]
+        v = v[0:rows]
+        fx = px * (v - load(c, 1)[0:rows]) + mx * (v - load(c, -1)[0:rows])
         fz = pz * (v - zp(v, lane))
         fz = fz - zm(fz, lane, half * v)
         outs.append(fx + fy + fz + (fx, fy, fz)[c])
@@ -274,7 +284,7 @@
 
     def moment_step(t, sums):
         outs = image_plane(
-            lambda c, k: g_ref[c, t + 1 + k], s_ref[t + 1], s_ref[t + 2], s_ref[t + 3], lane
+            lambda c, k: g_ref[c, t + 1 + k], s_ref[t + 1], s_ref[t + 2], s_ref[t + 3], lane, 8
         )
         fs = [fext_ref[c, t + 3] for c in range(3)]
         return add_moments(sums, fs, [g_ref[c, t + 1] for c in range(3)], outs)
@@ -305,28 +315,39 @@
         g2_ref[c, 0, 4:6] = g_in_ref[c, 0:2]
         g2_ref[c, 1, 0:2] = g_in_ref[c, 10:12]
 
-    odd = jnp.full((ROWS, CZ), is_odd(gx), jnp.int32) == 1
-    for k in range(13):
+    odd = jnp.full((8, CZ), is_odd(gx), jnp.int32) == 1
+    own_rows, halo_rows = slice(0, 8), slice(8, 16)
+    for k in range(23):
         one, two = first_in[k], second_in[k]
-        below, above = jnp.where(odd, two, one), jnp.where(odd, one, two)
-        if k < 4:
-            d2_ref[0, k] = below
-            d2_ref[1, 2 + k] = above
+        sides = jnp.where(odd, two, one), jnp.where(odd, one, two)
+        if k < 4 or 13 <= k < 17:
+            rows, i = (own_rows, k) if k < 4 else (halo_rows, k - 13)
+            for side in range(2):
+                d2_ref[side, i + 2 * side, rows] = sides[side]
             continue
-        c, i = (k - 4) // 3, (k - 4) % 3
-        f2_ref[c, 0, i] = below
-        f2_ref[c, 1, 3 + i] = above
-        if i >= 1:
-            f_rim_ref[c, 0, i - 1] = below
-        if i <= 1:
-            f_rim_ref[c, 1, i] = above
+        for side in range(2):
+            if k < 13:
+                c, rows = (k - 4) // 3, own_rows
+                parts = (((k - 4) % 3, sides[side]),)
+            else:
+                c, rows = (k - 17) // 2, halo_rows
+                order = (0, 1, 2) if side else (2, 1, 0)
+                if (k - 17) % 2 == 0:
+                    parts = ((order[0], sides[side]),)
+                else:
+                    parts = ((order[1], sides[side]), (order[2], roll(sides[side], -3, 0)))
+            for i, part in parts:
+                f2_ref[c, side, i + 3 * side, rows] = part
+                if i + side in (1, 2) and i - 1 + side >= 0:
+                    f_rim_ref[c, side, i - 1 + side, rows] = part
 
     w_copy.wait()
 
     def smooth_step(i, _):
         side, m = lax.shift_right_logical(i, 2), lax.bitwise_and(i, 3)
         planes = [d2_ref[side, m + k] for k in range(3)]
-        flags = brick_flags(f2_ref[1, side, m + 2 * side, 11:13], f2_ref[0, side, m + 2 * side, 11:13])
+        at = jnp.where(side == 0, jnp.maximum(m, 2), jnp.minimum(m + 2, 3))
+        flags = brick_flags(f2_ref[1, side, at, 11:13], f2_ref[0, side, at, 11:13])
         s2_ref[side, m + 3 * side], coef_ref[side, m] = stiffness_plane(
             planes, flags, gx * CX + m - 3 + 18 * side, iy[0], rwt_ref, w_ref, lane
         )
@@ -356,7 +377,7 @@
             n = m + 3 - 2 * side
             outs = image_plane(
                 lambda c, k: g2_ref[c, side, q + k],
-                s2_ref[side, n - 1], s2_ref[side, n], s2_ref[side, n + 1], lane,
+                s2_ref[side, n - 1], s2_ref[side, n], s2_ref[side, n + 1], lane, 8,
             )
             fs = [f2_ref[c, side, m + 3 - 3 * side] for c in range(3)]
             sums = add_moments(sums, fs, [g2_ref[c, side, q] for c in range(3)], outs)
@@ -384,9 +405,10 @@
     m0, m1, m2, m3 = (
         jnp.sum(jnp.where(at == k, line, 0.0), axis=1, keepdims=True) for k in range(4)
     )
-    s1 = m0 / m1
-    rr = m0 - 2.0 * s1 * m1 + s1 * s1 * m2
-    grow = 1.0 + rr / m0
+    inverse = 1.0 / m1
+    s1 = m0 * inverse
+    grow = s1 * m2 * inverse
+    rr = m0 * (grow - 1.0)
     s2 = rr / (grow * grow * m1 - 2.0 * grow * s1 * m2 + s1 * s1 * m3)
     alpha = jnp.broadcast_to(s1 + s2 * grow, (ROWS, CZ))
     beta = jnp.broadcast_to(-s1 * s2, (ROWS, CZ))
@@ -448,7 +470,7 @@
 
     def out_step(x, _):
         planes = [sh_ref[x], sh_ref[x + 1], sh_ref[x + 2]]
-        sens_ref[x] = filter_plane(planes, w_ref, lane, -1)[0:8]
+        sens_ref[x] = filter_plane(planes, w_ref, lane[0:8], -1, 8)
         return 0
 
     w_copy.wait()
@@ -503,7 +525,7 @@
 def body(density, force, brick_ids, offsets):
     ins = (density, force, brick_ids.reshape(1, 512))
     plane = (ROWS, CZ)
-    slab_y, slab_x = f32(216, CZ), f32(13, *plane)
+    slab_y, slab_x = f32(216, CZ), f32(23, 8, CZ)
     den, f, mask, first, second = call(
         pack_y_kernel,
         (f32(CX, CY, CZ), f32(3, CX, CY, CZ), f32(8, CZ), slab_y, slab_y),
@@ -542,8 +564,8 @@
             pltpu.SemaphoreType.DMA(()),
         ],
     )(w, dext, fext, first, second, stiff, image, sums, rwt)
-    lines = spread_sum(line, ("x", "y"), 32)
-    lines = spread_sum(jnp.sum(lines, axis=0, keepdims=True), ("zl", "zh", "c"), 24)
+    lines = spread_sum(line, ("zl", "zh", "c"), 24)
+    lines = spread_sum(jnp.sum(lines, axis=0, keepdims=True), ("x", "y"), 32)
     return call(
         last_kernel,
         (f32(3, CX, CY, CZ), f32(CX, CY, CZ)),

time: 73.8 us -> 72.4 us (0.981)
  no operation moved by 1% of the time
where the time goes in v5:
time: 72.4 us; the launch traced here: 72.1 us
  blocking collectives  43.4 us (60%)
  starting transfers between devices  15.7 us (22%)
  Pallas kernels  8.63 us (12%)
  waiting for transfers between devices  3.64 us (5%)
    all_to_all x2, blocking collectives, spread_sum(): return lax.all_to_all(lines, axes, 0, 0, tiled=True)  43.4 us
    ppermute x4, starting transfers between devices, swap(): got.append(lax.ppermute(slab, axes, pairs + [(b, a) for a, b in pairs]))  15.7 us
    ppermute x4, waiting for transfers between devices, swap(): got.append(lax.ppermute(slab, axes, pairs + [(b, a) for a, b in pairs]))  3.64 us
    pallas_call x1, Pallas kernels, body(): call(inner_kernel, (f32(128), f32(14, *plane), f32(14, *plane), f32(3, 12...  3.32 us
    pallas_call x1, Pallas kernels, body(): call(last_kernel, (f32(3, CX, CY, CZ), f32(CX, CY, CZ)), [ANY] + [VMEM] *...  2.11 us
    pallas_call x1, Pallas kernels, body(): call(rim_kernel, (f32(3, 2, 4, *plane), f32(2, 4, *plane), f32(3, 2, 2, *...  1.81 us
  transfers between devices with their start and end apart: 4, of which 2 were waited for; matrix products, arithmetic and copies ran while one was open for 0% of the time, Pallas kernels for 5%

profile of v5, /device:TPU:1, one launch (start us, length us, event | category | flops | bytes accessed | tf_op | source)
XLA Modules:
  0.0 72.1 jit_solution(8312279838493061693)
XLA Ops:
  0.6 1.2 %shard_map.59 = (f32[16,8,256]{2,1,0:T(8,128)S(1)}, f32[3,16,8,256]{3,2,1,0:T(8,128)S(1)}, f32[8,256]{1,0:T(8,128)S(1)}, f32[216,256]{1,0:T(8,128)S(1)}, f32[216,256]{1,0:T(8,128)S(1)}) custom-call(f32[16,8,256]{2,1,0:T(8,128)} %den_hbm.1, f32[3,16,8,256]{3,2,1,0:T(8,128)} %f_hbm.1, s32[1,512]{1,0:T(1,128)} %bitcast.8), custom_call_target="tpu_custom_call" | custom-call | tf_op jit(solution)/shard_map/pallas_call | solution.py:529
  1.8 4.6 %collective-permute-start = (f32[216,256]{1,0:T(8,128)S(1)}, f32[216,256]{1,0:T(8,128)S(1)}, u32[]{:S(2)}, u32[]{:S(2)}) collective-permute-start(f32[216,256]{1,0:T(8,128)S(1)} %get-tuple-element.24), channel_id=1, source_target_pairs={{1,2},{3,4},{5,6},{7,8},{9,10},{11,12},{13,14},{15,16},{17,18},{19... | collective-permute-start | bytes 663560 | tf_op jit(solution)/shard_map/ppermute | solution.py:516
  6.5 8.5 %collective-permute-start.1 = (f32[216,256]{1,0:T(8,128)S(1)}, f32[216,256]{1,0:T(8,128)S(1)}, u32[]{:S(2)}, u32[]{:S(2)}) collective-permute-start(f32[216,256]{1,0:T(8,128)S(1)} %get-tuple-element.25), channel_id=1, source_target_pairs={{0,1},{2,3},{4,5},{6,7},{8,9},{10,11},{12,13},{14,15},{16,17},{18,... | collective-permute-start | bytes 663560 | tf_op jit(solution)/shard_map/ppermute | solution.py:516
  15.0 0.0 collective-permute-done.first_in
  15.0 1.1 %collective-permute-done.1.second_in = f32[216,256]{1,0:T(8,128)S(1)} collective-permute-done((f32[216,256]{1,0:T(8,128)S(1)}, f32[216,256]{1,0:T(8,128)S(1)}, u32[]{:S(2)}, u32[]{:S(2)}) %collective-permute-start.1) | collective-permute-done | bytes 221216 | tf_op jit(solution)/shard_map/ppermute | solution.py:516
  16.0 0.2 shard_map.60
  16.2 0.7 collective-permute-start.2
  16.9 1.9 %collective-permute-start.3 = (f32[23,8,256]{2,1,0:T(8,128)S(1)}, f32[23,8,256]{2,1,0:T(8,128)S(1)}, u32[]{:S(2)}, u32[]{:S(2)}) collective-permute-start(f32[23,8,256]{2,1,0:T(8,128)S(1)} %get-tuple-element.30), channel_id=1, source_target_pairs={{0,64},{128,192},{256,320},{384,448},{512,576},{640,704},{64,0},{1... | collective-permute-start | bytes 565256 | tf_op jit(solution)/shard_map/ppermute | solution.py:516
  18.8 3.3 %shard_map.61 = (f32[128]{0:T(128)S(1)}, f32[14,16,256]{2,1,0:T(8,128)S(1)}, f32[14,16,256]{2,1,0:T(8,128)S(1)}, f32[3,12,16,256]{3,2,1,0:T(8,128)S(1)}, f32[4,8...) custom-call(s32[3,14]{1,0:T(4,128)} %bitcast.9, f32[16,16,256]{2,1,0:T(8,128)S(1)} %get-tuple-element.26.dext_ref, ...), custom_call_target="tpu_custom_call" | custom-call | flops 8000000 | bytes 8000000 | tf_op jit(solution)/shard_map/pallas_call | solution.py:545
  22.2 0.0 collective-permute-done.2.first_in
  22.2 2.6 %collective-permute-done.3.second_in = f32[23,8,256]{2,1,0:T(8,128)S(1)} collective-permute-done((f32[23,8,256]{2,1,0:T(8,128)S(1)}, f32[23,8,256]{2,1,0:T(8,128)S(1)}, u32[]{:S(2)}, u32[]{:S(2)}) %collective-permute-start.3) | collective-permute-done | bytes 188448 | tf_op jit(solution)/shard_map/ppermute | solution.py:516
  24.7 1.8 %shard_map.62 = (f32[3,2,4,16,256]{4,3,2,1,0:T(8,128)S(1)}, f32[2,4,16,256]{3,2,1,0:T(8,128)S(1)}, f32[3,2,2,16,256]{4,3,2,1,0:T(8,128)S(1)}, f32[1,128]{1,0:T(1,128)S(1)}) custom-call(f32[128]{0:T(128)S(1)} %get-tuple-element.28.w_in, f32[16,16,256]{2,1,0:T(8,128)S(1)} %get-tuple-element.26.dext_ref, f32[3,16,16,256]{3,2,1,0:T(8,128)S(1)} %get-tuple-element.27.fext_ref, ...), custom_call_target="tpu_custom_call" | custom-call | tf_op jit(solution)/shard_map/pallas_call | solution.py:553
  26.6 31.3 %all_to_all.14 = f32[24,1,128]{2,1,0:T(1,128)S(1)} all-to-all(f32[24,1,128]{2,1,0:T(1,128)S(1)} %broadcast_in_dim.4), channel_id=1, replica_groups=mesh['zl'=3,'x'=4,'zh'=4,'y'=8,'c'=2] {'zl','zh','c'}, dimensions={0} | all-to-all | bytes 24576 | tf_op jit(solution)/shard_map/all_to_all | solution.py:522
  58.0 12.1 %all_to_all.15 = f32[32,1,128]{2,1,0:T(1,128)S(1)} all-to-all(f32[32,1,128]{2,1,0:T(1,128)S(1)} %broadcast_in_dim.5), channel_id=1, replica_groups=mesh['zl'=3,'x'=4,'zh'=4,'y'=8,'c'=2] {'x','y'}, dimensions={0} | all-to-all | bytes 32768 | tf_op jit(solution)/shard_map/all_to_all | solution.py:522
  70.0 2.1 %shard_map.63 = (f32[3,16,8,256]{3,2,1,0:T(8,128)}, f32[16,8,256]{2,1,0:T(8,128)}) custom-call(f32[128]{0:T(128)S(1)} %get-tuple-element.28.w_in, f32[3,16,16,256]{3,2,1,0:T(8,128)S(1)} %get-tuple-element.27.fext_ref, f32[3,2,2,16,256]{4,3,2,1,0:T(8,128)S(1)} %get-tuple-element.35.f_rim_ref, f32[3,12,16,256]{3,2,1,0:T(8,128)S(1)} %get-tuple-element.32.g_in_ref, ...), custom_call_target="tpu_custom_call" | custom-call | tf_op jit(solution)/shard_map/pallas_call | solution.py:569
  (3 shorter events, 0.0 us)
Async XLA Ops:
  1.8 13.1 %collective-permute-start = (f32[216,256]{1,0:T(8,128)S(1)}, f32[216,256]{1,0:T(8,128)S(1)}, u32[]{:S(2)}, u32[]{:S(2)}) collective-permute-start(f32[216,256]{1,0:T(8,128)S(1)} %get-tuple-element.24), channel_id=1, source_target_pairs={{1,2},{3,4},{5,6},{7,8},{9,10},{11,12},{13,14},{15,16},{17,18},{19... | collective-permute-start | bytes 663560 | tf_op jit(solution)/shard_map/ppermute | solution.py:516
  6.5 9.6 %collective-permute-start.1 = (f32[216,256]{1,0:T(8,128)S(1)}, f32[216,256]{1,0:T(8,128)S(1)}, u32[]{:S(2)}, u32[]{:S(2)}) collective-permute-start(f32[216,256]{1,0:T(8,128)S(1)} %get-tuple-element.25), channel_id=1, source_target_pairs={{0,1},{2,3},{4,5},{6,7},{8,9},{10,11},{12,13},{14,15},{16,17},{18,... | collective-permute-start | bytes 663560 | tf_op jit(solution)/shard_map/ppermute | solution.py:516
  16.2 5.9 %collective-permute-start.2 = (f32[23,8,256]{2,1,0:T(8,128)S(1)}, f32[23,8,256]{2,1,0:T(8,128)S(1)}, u32[]{:S(2)}, u32[]{:S(2)}) collective-permute-start(f32[23,8,256]{2,1,0:T(8,128)S(1)} %get-tuple-element.29), channel_id=1, source_target_pairs={{64,128},{192,256},{320,384},{448,512},{576,640},{128,64},{256,192... | collective-permute-start | bytes 565256 | tf_op jit(solution)/shard_map/ppermute | solution.py:516
  16.9 7.8 %collective-permute-start.3 = (f32[23,8,256]{2,1,0:T(8,128)S(1)}, f32[23,8,256]{2,1,0:T(8,128)S(1)}, u32[]{:S(2)}, u32[]{:S(2)}) collective-permute-start(f32[23,8,256]{2,1,0:T(8,128)S(1)} %get-tuple-element.30), channel_id=1, source_target_pairs={{0,64},{128,192},{256,320},{384,448},{512,576},{640,704},{64,0},{1... | collective-permute-start | bytes 565256 | tf_op jit(solution)/shard_map/ppermute | solution.py:516

commit v6 on v5

--- a/solution.py
+++ b/solution.py
@@ -19,7 +19,7 @@
 GX, GY = ("zl", "x"), ("zh", "y", "c")
 ROWS = 16
 F32 = jnp.float32
-UNROLL = (7, 4, 5, 8, 4, 3, 9, 8)
+UNROLL = (7, 4, 5, 4, 4, 3, 9, 8)
 
 
 def sub_iota(rows):
@@ -52,6 +52,10 @@
 
 def is_odd(at):
     return lax.bitwise_and(at, 1)
+
+
+def partner_side(at, second):
+    return 1 - is_odd(at) if second else is_odd(at)
 
 
 def store_weights(off_ref, w_ref):
@@ -112,7 +116,7 @@
 
 
 def pack_x_kernel(
-    den_ref, f_ref, m_ref, first_in, second_in, dext_ref, fext_ref, first_ref, second_ref
+    den_ref, f_ref, m_ref, first_in, second_in, _, dext_ref, fext_ref, first_ref, second_ref
 ):
     odd_y = jnp.full((CX, CZ), is_odd(lax.axis_index(GY)), jnp.int32) == 1
 
@@ -252,14 +256,17 @@
     return m0, m1, m2, m3
 
 
+def table_kernel(off_ref, _, w_ref, rwt_ref):
+    store_weights(off_ref, w_ref)
+    store_reciprocals(rwt_ref, w_ref, grid_y(lax.axis_index(GY)))
+
+
 def inner_kernel(
-    off_ref, dext_ref, fext_ref, w_ref, s_ref, coef_ref, g_ref, sums_ref, rwt_ref
+    w_ref, rwt_ref, dext_ref, fext_ref, s_ref, coef_ref, g_ref, sums_ref
 ):
     gx, gy = lax.axis_index(GX), lax.axis_index(GY)
     lane = lane_iota(ROWS)
     iy = grid_y(gy)
-    store_weights(off_ref, w_ref)
-    store_reciprocals(rwt_ref, w_ref, iy)
 
     def smooth_step(p, _):
         x = p + 1
@@ -296,94 +303,70 @@
 
 
 def rim_kernel(
-    w_in, dext_ref, fext_ref, first_in, second_in, s_in_ref, g_in_ref, sums_ref, rwt_ref,
+    second, w_in, dext_ref, fext_ref, slab_ref, s_in_ref, g_in_ref, sums_ref, rwt_ref,
     g_ref, coef_ref, f_rim_ref, mom_ref,
     d2_ref, f2_ref, s2_ref, g2_ref, w_ref, sem,
 ):
     w_copy = pltpu.make_async_copy(w_in, w_ref, sem)
     w_copy.start()
     gx, gy = lax.axis_index(GX), lax.axis_index(GY)
+    side = partner_side(gx, second)
     lane = lane_iota(ROWS)
     iy = grid_y(gy)
-    d2_ref[0, 4:6] = dext_ref[0:2]
-    d2_ref[1, 0:2] = dext_ref[14:16]
-    s2_ref[0, 4:7] = s_in_ref[0:3]
-    s2_ref[1, 0:3] = s_in_ref[11:14]
+    d2_ref[pl.ds(4 - 4 * side, 2)] = dext_ref[pl.ds(14 * side, 2)]
+    d2_ref[pl.ds(2 * side, 4), 0:8] = slab_ref[0:4]
+    d2_ref[pl.ds(2 * side, 4), 8:16] = slab_ref[13:17]
+    s2_ref[pl.ds(4 - 4 * side, 3)] = s_in_ref[pl.ds(11 * side, 3)]
     for c in range(3):
-        f2_ref[c, 0, 3:6] = fext_ref[c, 0:3]
-        f2_ref[c, 1, 0:3] = fext_ref[c, 13:16]
-        g2_ref[c, 0, 4:6] = g_in_ref[c, 0:2]
-        g2_ref[c, 1, 0:2] = g_in_ref[c, 10:12]
-
-    odd = jnp.full((8, CZ), is_odd(gx), jnp.int32) == 1
-    own_rows, halo_rows = slice(0, 8), slice(8, 16)
-    for k in range(23):
-        one, two = first_in[k], second_in[k]
-        sides = jnp.where(odd, two, one), jnp.where(odd, one, two)
-        if k < 4 or 13 <= k < 17:
-            rows, i = (own_rows, k) if k < 4 else (halo_rows, k - 13)
-            for side in range(2):
-                d2_ref[side, i + 2 * side, rows] = sides[side]
-            continue
-        for side in range(2):
-            if k < 13:
-                c, rows = (k - 4) // 3, own_rows
-                parts = (((k - 4) % 3, sides[side]),)
-            else:
-                c, rows = (k - 17) // 2, halo_rows
-                order = (0, 1, 2) if side else (2, 1, 0)
-                if (k - 17) % 2 == 0:
-                    parts = ((order[0], sides[side]),)
-                else:
-                    parts = ((order[1], sides[side]), (order[2], roll(sides[side], -3, 0)))
-            for i, part in parts:
-                f2_ref[c, side, i + 3 * side, rows] = part
-                if i + side in (1, 2) and i - 1 + side >= 0:
-                    f_rim_ref[c, side, i - 1 + side, rows] = part
-
+        f2_ref[c, pl.ds(3 - 3 * side, 3)] = fext_ref[c, pl.ds(13 * side, 3)]
+        f2_ref[c, pl.ds(3 * side, 3), 0:8] = slab_ref[4 + 3 * c : 7 + 3 * c]
+        deep = slab_ref[18 + 2 * c]
+        f2_ref[c, 2 + side, 8:16] = slab_ref[17 + 2 * c]
+        f2_ref[c, 1 + 3 * side, 8:16] = deep
+        f2_ref[c, 5 * side, 8:16] = roll(deep, -3, 0)
+        f_rim_ref[c] = f2_ref[c, pl.ds(1 + 2 * side, 2)]
+        g2_ref[c, pl.ds(4 - 4 * side, 2)] = g_in_ref[c, pl.ds(10 * side, 2)]
     w_copy.wait()
 
-    def smooth_step(i, _):
-        side, m = lax.shift_right_logical(i, 2), lax.bitwise_and(i, 3)
-        planes = [d2_ref[side, m + k] for k in range(3)]
+    def smooth_step(m, _):
+        planes = [d2_ref[m + k] for k in range(3)]
         at = jnp.where(side == 0, jnp.maximum(m, 2), jnp.minimum(m + 2, 3))
-        flags = brick_flags(f2_ref[1, side, at, 11:13], f2_ref[0, side, at, 11:13])
-        s2_ref[side, m + 3 * side], coef_ref[side, m] = stiffness_plane(
+        flags = brick_flags(f2_ref[1, at, 11:13], f2_ref[0, at, 11:13])
+        s2_ref[m + 3 * side], coef_ref[m] = stiffness_plane(
             planes, flags, gx * CX + m - 3 + 18 * side, iy[0], rwt_ref, w_ref, lane
         )
         return 0
 
-    lax.fori_loop(0, 8, smooth_step, 0, unroll=UNROLL[3])
-
-    def image_step(i, _):
-        side, m = lax.shift_right_logical(i, 2), lax.bitwise_and(i, 3)
+    lax.fori_loop(0, 4, smooth_step, 0, unroll=UNROLL[3])
+
+    def image_step(m, _):
         n = m + side
         outs = image_plane(
-            lambda c, k: f2_ref[c, side, m + 1 + k],
-            s2_ref[side, n], s2_ref[side, n + 1], s2_ref[side, n + 2], lane,
+            lambda c, k: f2_ref[c, m + 1 + k], s2_ref[n], s2_ref[n + 1], s2_ref[n + 2], lane
         )
         inside = iy[0] * on_grid(gx * CX + m - 2 + 16 * side)
         for c in range(3):
             g = outs[c] * inside
-            g_ref[c, side, m] = g
-            g2_ref[c, side, m + 2 * side] = g
-        return 0
-
-    lax.fori_loop(0, 8, image_step, 0, unroll=UNROLL[4])
+            g_ref[c, m] = g
+            g2_ref[c, m + 2 * side] = g
+        return 0
+
+    lax.fori_loop(0, 4, image_step, 0, unroll=UNROLL[4])
 
     def moment_step(m, sums):
-        for side in range(2):
-            q = m + 2 - side
-            n = m + 3 - 2 * side
-            outs = image_plane(
-                lambda c, k: g2_ref[c, side, q + k],
-                s2_ref[side, n - 1], s2_ref[side, n], s2_ref[side, n + 1], lane, 8,
-            )
-            fs = [f2_ref[c, side, m + 3 - 3 * side] for c in range(3)]
-            sums = add_moments(sums, fs, [g2_ref[c, side, q] for c in range(3)], outs)
-        return sums
+        q = m + 2 - side
+        n = m + 3 - 2 * side
+        outs = image_plane(
+            lambda c, k: g2_ref[c, q + k], s2_ref[n - 1], s2_ref[n], s2_ref[n + 1], lane, 8
+        )
+        fs = [f2_ref[c, m + 3 - 3 * side] for c in range(3)]
+        return add_moments(sums, fs, [g2_ref[c, q] for c in range(3)], outs)
 
     sums = lax.fori_loop(0, 3, moment_step, tuple(sums_ref[k] for k in range(4)), unroll=UNROLL[5])
+    if not second:
+        for k in range(4):
+            mom_ref[k] = sums[k]
+        return
     at = lax.broadcasted_iota(jnp.int32, (1, 128), 1)
     line = jnp.zeros((1, 128), F32)
     for k in range(4):
@@ -393,7 +376,7 @@
 
 
 def last_kernel(
-    w_in, fext_ref, f_rim_ref, g_in_ref, g_rim_ref, coef_in_ref, coef_rim_ref, mom_ref,
+    w_in, fext_ref, g_in_ref, coef_in_ref, g1_ref, coef1_ref, f1_ref, g2_ref, coef2_ref, f2_ref, mom_ref,
     u_hbm, sens_hbm,
     u_ref, sh_ref, coef_ref, own_ref, sens_ref, w_ref, sem,
 ):
@@ -426,24 +409,26 @@
         return 0
 
     lax.fori_loop(0, CX - 4, u_step, 0, unroll=4)
-    for x in (0, 1, 14, 15):
-        side, m = (0, x + 2) if x < 8 else (1, x - 14)
-        us = u_plane(
-            x + 2, [fext_ref[c, x] for c in range(3)], [g_rim_ref[c, side, m] for c in range(3)]
-        )
-        for c in range(3):
-            own_ref[c, x] = us[c][0:8]
+    coef_ref[2:16] = coef_in_ref[...]
+    sides = []
+    for second, rim_f_ref, g_ref, rim_ref in ((0, f1_ref, g1_ref, coef1_ref), (1, f2_ref, g2_ref, coef2_ref)):
+        side = partner_side(lax.axis_index(GX), second)
+        coef_ref[pl.ds(16 * side, 2)] = rim_ref[pl.ds(2 - 2 * side, 2)]
+        sides.append((side, rim_f_ref, g_ref))
+        for i in range(2):
+            x, m = 14 * side + i, 2 - 2 * side + i
+            us = u_plane(x + 2, [fext_ref[c, x] for c in range(3)], [g_ref[c, m] for c in range(3)])
+            for c in range(3):
+                own_ref[c, x] = us[c][0:8]
     u_copy = pltpu.make_async_copy(own_ref, u_hbm, sem.at[0])
     u_copy.start()
-    for q, side, i in ((0, 0, 0), (1, 0, 1), (18, 1, 0), (19, 1, 1)):
-        u_plane(
-            q,
-            [f_rim_ref[c, side, i] for c in range(3)],
-            [g_rim_ref[c, side, i + 2 * side] for c in range(3)],
-        )
-    coef_ref[0:2] = coef_rim_ref[0, 2:4]
-    coef_ref[2:16] = coef_in_ref[...]
-    coef_ref[16:18] = coef_rim_ref[1, 0:2]
+    for side, rim_f_ref, g_ref in sides:
+        for i in range(2):
+            u_plane(
+                18 * side + i,
+                [rim_f_ref[c, i] for c in range(3)],
+                [g_ref[c, 2 * side + i] for c in range(3)],
+            )
 
     def share_step(r, _):
         ex = ey = ez = e0 = None
@@ -534,42 +519,53 @@
         [pltpu.VMEM((1, 512), jnp.int32), pltpu.SemaphoreType.DMA((3,))],
     )(*(pltpu.with_memory_space_constraint(a, pltpu.HBM) for a in ins))
     first, second = swap(first, second, GY, DEV_Y)
+    w, rwt = call(
+        table_kernel,
+        (f32(128), f32(3, *plane)),
+        [SMEM, ANY],
+        (SMEM, VMEM),
+        [],
+        pl.CostEstimate(flops=1_000_000, bytes_accessed=1_000_000, transcendentals=0),
+    )(pltpu.with_memory_space_constraint(offsets.T, pltpu.HBM), mask)
     dext, fext, first, second = call(
         pack_x_kernel,
         (f32(CX, *plane), f32(3, CX, *plane), slab_x, slab_x),
-        [VMEM] * 5,
+        [VMEM] * 5 + [ANY],
         (VMEM,) * 4,
         [],
-    )(den, f, mask, first, second)
+    )(den, f, mask, first, second, w)
     first, second = swap(first, second, GX, DEV_X)
-    w, stiff, coef, image, sums, rwt = call(
+    stiff, coef, image, sums = call(
         inner_kernel,
-        (f32(128), f32(14, *plane), f32(14, *plane), f32(3, 12, *plane), f32(4, 8, CZ), f32(3, *plane)),
-        [SMEM, VMEM, VMEM],
-        (SMEM,) + (VMEM,) * 5,
+        (f32(14, *plane), f32(14, *plane), f32(3, 12, *plane), f32(4, 8, CZ)),
+        [SMEM, VMEM, VMEM, VMEM],
+        (VMEM,) * 4,
         [],
         pl.CostEstimate(flops=8_000_000, bytes_accessed=8_000_000, transcendentals=0),
-    )(pltpu.with_memory_space_constraint(offsets.T, pltpu.HBM), dext, fext)
-    image_rim, coef_rim, f_rim, line = call(
-        rim_kernel,
-        (f32(3, 2, 4, *plane), f32(2, 4, *plane), f32(3, 2, 2, *plane), f32(1, 128)),
-        [ANY] + [VMEM] * 8,
-        (VMEM,) * 4,
-        [
-            pltpu.VMEM((2, 6, *plane), F32),
-            pltpu.VMEM((3, 2, 6, *plane), F32),
-            pltpu.VMEM((2, 7, *plane), F32),
-            pltpu.VMEM((3, 2, 6, *plane), F32),
-            pltpu.SMEM((128,), F32),
-            pltpu.SemaphoreType.DMA(()),
-        ],
-    )(w, dext, fext, first, second, stiff, image, sums, rwt)
-    lines = spread_sum(line, ("zl", "zh", "c"), 24)
+    )(w, rwt, dext, fext)
+    rims = []
+    for k, slab in enumerate((first, second)):
+        image_rim, coef_rim, f_rim, sums = call(
+            functools.partial(rim_kernel, k),
+            (f32(3, 4, *plane), f32(4, *plane), f32(3, 2, *plane), f32(1, 128) if k else f32(4, 8, CZ)),
+            [ANY] + [VMEM] * 7,
+            (VMEM,) * 4,
+            [
+                pltpu.VMEM((6, *plane), F32),
+                pltpu.VMEM((3, 6, *plane), F32),
+                pltpu.VMEM((7, *plane), F32),
+                pltpu.VMEM((3, 6, *plane), F32),
+                pltpu.SMEM((128,), F32),
+                pltpu.SemaphoreType.DMA(()),
+            ],
+        )(w, dext, fext, slab, stiff, image, sums, rwt)
+        rims += [image_rim, coef_rim, f_rim]
+    lines = spread_sum(sums, ("zl", "zh", "c"), 24)
     lines = spread_sum(jnp.sum(lines, axis=0, keepdims=True), ("x", "y"), 32)
     return call(
         last_kernel,
         (f32(3, CX, CY, CZ), f32(CX, CY, CZ)),
-        [ANY] + [VMEM] * 7,
+        [ANY] + [VMEM] * 10,
         (HBM, HBM),
         [
             pltpu.VMEM((3, CX + 4, *plane), F32),
@@ -580,7 +576,7 @@
             pltpu.SMEM((128,), F32),
             pltpu.SemaphoreType.DMA((4,)),
         ],
-    )(w, fext, f_rim, image, image_rim, coef, coef_rim, lines)
+    )(w, fext, image, coef, *rims, lines)
 
 
 def solution(mesh):

time: 72.4 us -> 72.6 us (level)
  Pallas kernels: 8.63 us -> 9.67 us
  waiting for transfers between devices: 3.64 us -> 2.71 us
    pallas_call x2 -> x4, Pallas kernels: 5.13 us -> 6.16 us  [the longest x1 2.46 us: body(): call(inner_kernel, (f32(14, *plane), f32(14, *plane), f32(3, 12, *plane),...]
    ppermute x4, waiting for transfers between devices: 3.64 us -> 2.71 us  [swap(): got.append(lax.ppermute(slab, axes, pairs + [(b, a) for a, b in pairs]))]
  transfers between devices with their start and end apart: 4 -> 4, of which waited for: 2 -> 1; matrix products, arithmetic and copies ran while one was open for 0% -> 0% of each run, Pallas kernels for 5% -> 7%
where the time goes in v6:
time: 72.6 us; the launch traced here: 72.3 us
  blocking collectives  43.4 us (60%)
  starting transfers between devices  15.7 us (22%)
  Pallas kernels  9.67 us (13%)
  waiting for transfers between devices  2.71 us (4%)
  between operations  0.74 us (1%)
    all_to_all x2, blocking collectives, spread_sum(): return lax.all_to_all(lines, axes, 0, 0, tiled=True)  43.4 us
    ppermute x4, starting transfers between devices, swap(): got.append(lax.ppermute(slab, axes, pairs + [(b, a) for a, b in pairs]))  15.7 us
    ppermute x4, waiting for transfers between devices, swap(): got.append(lax.ppermute(slab, axes, pairs + [(b, a) for a, b in pairs]))  2.71 us
    pallas_call x1, Pallas kernels, body(): call(inner_kernel, (f32(14, *plane), f32(14, *plane), f32(3, 12, *plane),...  2.46 us
    pallas_call x2, Pallas kernels, body(): call(functools.partial(rim_kernel, k), (f32(3, 4, *plane), f32(4, *plane)...  2.3 us
    pallas_call x1, Pallas kernels, body(): call(last_kernel, (f32(3, CX, CY, CZ), f32(CX, CY, CZ)), [ANY] + [VMEM] *...  2.11 us
  transfers between devices with their start and end apart: 4, of which 1 were waited for; matrix products, arithmetic and copies ran while one was open for 0% of the time, Pallas kernels for 7%

profile of v6, /device:TPU:1, one launch (start us, length us, event | category | flops | bytes accessed | tf_op | source)
XLA Modules:
  0.0 72.3 jit_solution(11202688536913814062)
XLA Ops:
  0.6 1.2 %shard_map.59 = (f32[16,8,256]{2,1,0:T(8,128)S(1)}, f32[3,16,8,256]{3,2,1,0:T(8,128)S(1)}, f32[8,256]{1,0:T(8,128)S(1)}, f32[216,256]{1,0:T(8,128)S(1)}, f32[216,256]{1,0:T(8,128)S(1)}) custom-call(f32[16,8,256]{2,1,0:T(8,128)} %den_hbm.1, f32[3,16,8,256]{3,2,1,0:T(8,128)} %f_hbm.1, s32[1,512]{1,0:T(1,128)} %bitcast.8), custom_call_target="tpu_custom_call" | custom-call | tf_op jit(solution)/shard_map/pallas_call | solution.py:514
  1.8 4.6 %collective-permute-start = (f32[216,256]{1,0:T(8,128)S(1)}, f32[216,256]{1,0:T(8,128)S(1)}, u32[]{:S(2)}, u32[]{:S(2)}) collective-permute-start(f32[216,256]{1,0:T(8,128)S(1)} %get-tuple-element.29), channel_id=1, source_target_pairs={{1,2},{3,4},{5,6},{7,8},{9,10},{11,12},{13,14},{15,16},{17,18},{19... | collective-permute-start | bytes 663560 | tf_op jit(solution)/shard_map/ppermute | solution.py:501
  6.5 8.5 %collective-permute-start.1 = (f32[216,256]{1,0:T(8,128)S(1)}, f32[216,256]{1,0:T(8,128)S(1)}, u32[]{:S(2)}, u32[]{:S(2)}) collective-permute-start(f32[216,256]{1,0:T(8,128)S(1)} %get-tuple-element.30), channel_id=1, source_target_pairs={{0,1},{2,3},{4,5},{6,7},{8,9},{10,11},{12,13},{14,15},{16,17},{18,... | collective-permute-start | bytes 663560 | tf_op jit(solution)/shard_map/ppermute | solution.py:501
  15.0 1.4 %shard_map.60 = (f32[128]{0:T(128)S(1)}, f32[3,16,256]{2,1,0:T(8,128)S(1)}) custom-call(s32[3,14]{1,0:T(4,128)} %bitcast.9, f32[8,256]{1,0:T(8,128)S(1)} %get-tuple-element.25._.m_ref), custom_call_target="tpu_custom_call" | custom-call | flops 1000000 | bytes 1000000 | tf_op jit(solution)/shard_map/pallas_call | solution.py:522
  16.4 0.0 collective-permute-done.first_in
  16.4 0.0 collective-permute-done.1.second_in
  16.4 0.2 shard_map.61
  16.6 0.7 collective-permute-start.2
  17.3 1.9 %collective-permute-start.3 = (f32[23,8,256]{2,1,0:T(8,128)S(1)}, f32[23,8,256]{2,1,0:T(8,128)S(1)}, u32[]{:S(2)}, u32[]{:S(2)}) collective-permute-start(f32[23,8,256]{2,1,0:T(8,128)S(1)} %get-tuple-element.42), channel_id=1, source_target_pairs={{0,64},{128,192},{256,320},{384,448},{512,576},{640,704},{64,0},{1... | collective-permute-start | bytes 565256 | tf_op jit(solution)/shard_map/ppermute | solution.py:501
  19.2 2.5 %shard_map.62 = (f32[14,16,256]{2,1,0:T(8,128)S(1)}, f32[14,16,256]{2,1,0:T(8,128)S(1)}, f32[3,12,16,256]{3,2,1,0:T(8,128)S(1)}, f32[4,8,256]{2,1,0:T(8,128)S(1)}) custom-call(f32[128]{0:T(128)S(1)} %get-tuple-element.26._.w_ref.w_in, f32[3,16,256]{2,1,0:T(8,128)S(1)} %get-tuple-element.32.rwt_ref, f32[16,16,256]{2,1,0:T(8,128)S(1)} %get-tuple-element.33.dext_ref, ...), custom_call_target="tpu_custom_call" | custom-call | flops 8000000 | bytes 8000000 | tf_op jit(solution)/shard_map/pallas_call | solution.py:538
  21.7 0.0 collective-permute-done.2.slab_ref
  21.7 1.1 %shard_map.63 = (f32[3,4,16,256]{3,2,1,0:T(8,128)S(1)}, f32[4,16,256]{2,1,0:T(8,128)S(1)}, f32[3,2,16,256]{3,2,1,0:T(8,128)S(1)}, f32[4,8,256]{2,1,0:T(8,128)S(1)}) custom-call(f32[128]{0:T(128)S(1)} %get-tuple-element.26._.w_ref.w_in, f32[16,16,256]{2,1,0:T(8,128)S(1)} %get-tuple-element.33.dext_ref, f32[3,16,16,256]{3,2,1,0:T(8,128)S(1)} %get-tuple-element.31.fext_ref, ...), custom_call_target="tpu_custom_call" | custom-call | tf_op jit(solution)/shard_map/pallas_call | solution.py:548
  22.8 2.7 %collective-permute-done.3.slab_ref = f32[23,8,256]{2,1,0:T(8,128)S(1)} collective-permute-done((f32[23,8,256]{2,1,0:T(8,128)S(1)}, f32[23,8,256]{2,1,0:T(8,128)S(1)}, u32[]{:S(2)}, u32[]{:S(2)}) %collective-permute-start.3) | collective-permute-done | bytes 188448 | tf_op jit(solution)/shard_map/ppermute | solution.py:501
  25.5 1.2 %shard_map.64 = (f32[3,4,16,256]{3,2,1,0:T(8,128)S(1)}, f32[4,16,256]{2,1,0:T(8,128)S(1)}, f32[3,2,16,256]{3,2,1,0:T(8,128)S(1)}, f32[1,128]{1,0:T(1,128)S(1)}) custom-call(f32[128]{0:T(128)S(1)} %get-tuple-element.26._.w_ref.w_in, f32[16,16,256]{2,1,0:T(8,128)S(1)} %get-tuple-element.33.dext_ref, f32[3,16,16,256]{3,2,1,0:T(8,128)S(1)} %get-tuple-element.31.fext_ref, ...), custom_call_target="tpu_custom_call" | custom-call | tf_op jit(solution)/shard_map/pallas_call | solution.py:548
  26.7 30.6 %all_to_all.14 = f32[24,1,128]{2,1,0:T(1,128)S(1)} all-to-all(f32[24,1,128]{2,1,0:T(1,128)S(1)} %broadcast_in_dim.4), channel_id=1, replica_groups=mesh['zl'=3,'x'=4,'zh'=4,'y'=8,'c'=2] {'zl','zh','c'}, dimensions={0} | all-to-all | bytes 24576 | tf_op jit(solution)/shard_map/all_to_all | solution.py:507
  57.3 12.9 %all_to_all.15 = f32[32,1,128]{2,1,0:T(1,128)S(1)} all-to-all(f32[32,1,128]{2,1,0:T(1,128)S(1)} %broadcast_in_dim.5), channel_id=1, replica_groups=mesh['zl'=3,'x'=4,'zh'=4,'y'=8,'c'=2] {'x','y'}, dimensions={0} | all-to-all | bytes 32768 | tf_op jit(solution)/shard_map/all_to_all | solution.py:507
  70.2 2.1 %shard_map.65 = (f32[3,16,8,256]{3,2,1,0:T(8,128)}, f32[16,8,256]{2,1,0:T(8,128)}) custom-call(f32[128]{0:T(128)S(1)} %get-tuple-element.26._.w_ref.w_in, f32[3,16,16,256]{3,2,1,0:T(8,128)S(1)} %get-tuple-element.31.fext_ref, f32[3,12,16,256]{3,2,1,0:T(8,128)S(1)} %get-tuple-element.34.g_in_ref, f32[14,16,256]{2,1,0:T(8,128)S(1)} %get-tuple-element.35.coef_in_ref, ...), custom_call_target="tpu_custom_call" | custom-call | tf_op jit(solution)/shard_map/pallas_call | solution.py:565
  (3 shorter events, 0.0 us)
Async XLA Ops:
  1.8 14.5 %collective-permute-start = (f32[216,256]{1,0:T(8,128)S(1)}, f32[216,256]{1,0:T(8,128)S(1)}, u32[]{:S(2)}, u32[]{:S(2)}) collective-permute-start(f32[216,256]{1,0:T(8,128)S(1)} %get-tuple-element.29), channel_id=1, source_target_pairs={{1,2},{3,4},{5,6},{7,8},{9,10},{11,12},{13,14},{15,16},{17,18},{19... | collective-permute-start | bytes 663560 | tf_op jit(solution)/shard_map/ppermute | solution.py:501
  6.5 9.9 %collective-permute-start.1 = (f32[216,256]{1,0:T(8,128)S(1)}, f32[216,256]{1,0:T(8,128)S(1)}, u32[]{:S(2)}, u32[]{:S(2)}) collective-permute-start(f32[216,256]{1,0:T(8,128)S(1)} %get-tuple-element.30), channel_id=1, source_target_pairs={{0,1},{2,3},{4,5},{6,7},{8,9},{10,11},{12,13},{14,15},{16,17},{18,... | collective-permute-start | bytes 663560 | tf_op jit(solution)/shard_map/ppermute | solution.py:501
  16.6 5.1 %collective-permute-start.2 = (f32[23,8,256]{2,1,0:T(8,128)S(1)}, f32[23,8,256]{2,1,0:T(8,128)S(1)}, u32[]{:S(2)}, u32[]{:S(2)}) collective-permute-start(f32[23,8,256]{2,1,0:T(8,128)S(1)} %get-tuple-element.36), channel_id=1, source_target_pairs={{64,128},{192,256},{320,384},{448,512},{576,640},{128,64},{256,192... | collective-permute-start | bytes 565256 | tf_op jit(solution)/shard_map/ppermute | solution.py:501
  17.3 8.2 %collective-permute-start.3 = (f32[23,8,256]{2,1,0:T(8,128)S(1)}, f32[23,8,256]{2,1,0:T(8,128)S(1)}, u32[]{:S(2)}, u32[]{:S(2)}) collective-permute-start(f32[23,8,256]{2,1,0:T(8,128)S(1)} %get-tuple-element.42), channel_id=1, source_target_pairs={{0,64},{128,192},{256,320},{384,448},{512,576},{640,704},{64,0},{1... | collective-permute-start | bytes 565256 | tf_op jit(solution)/shard_map/ppermute | solution.py:501

commit v7 on v6

--- a/solution.py
+++ b/solution.py
@@ -116,7 +116,7 @@
 
 
 def pack_x_kernel(
-    den_ref, f_ref, m_ref, first_in, second_in, _, dext_ref, fext_ref, first_ref, second_ref
+    den_ref, f_ref, m_ref, first_in, second_in, dext_ref, fext_ref, first_ref, second_ref
 ):
     odd_y = jnp.full((CX, CZ), is_odd(lax.axis_index(GY)), jnp.int32) == 1
 
@@ -256,17 +256,14 @@
     return m0, m1, m2, m3
 
 
-def table_kernel(off_ref, _, w_ref, rwt_ref):
-    store_weights(off_ref, w_ref)
-    store_reciprocals(rwt_ref, w_ref, grid_y(lax.axis_index(GY)))
-
-
 def inner_kernel(
-    w_ref, rwt_ref, dext_ref, fext_ref, s_ref, coef_ref, g_ref, sums_ref
+    off_ref, dext_ref, fext_ref, w_ref, s_ref, coef_ref, g_ref, sums_ref, rwt_ref
 ):
     gx, gy = lax.axis_index(GX), lax.axis_index(GY)
     lane = lane_iota(ROWS)
     iy = grid_y(gy)
+    store_weights(off_ref, w_ref)
+    store_reciprocals(rwt_ref, w_ref, iy)
 
     def smooth_step(p, _):
         x = p + 1
@@ -519,30 +516,22 @@
         [pltpu.VMEM((1, 512), jnp.int32), pltpu.SemaphoreType.DMA((3,))],
     )(*(pltpu.with_memory_space_constraint(a, pltpu.HBM) for a in ins))
     first, second = swap(first, second, GY, DEV_Y)
-    w, rwt = call(
-        table_kernel,
-        (f32(128), f32(3, *plane)),
-        [SMEM, ANY],
-        (SMEM, VMEM),
-        [],
-        pl.CostEstimate(flops=1_000_000, bytes_accessed=1_000_000, transcendentals=0),
-    )(pltpu.with_memory_space_constraint(offsets.T, pltpu.HBM), mask)
     dext, fext, first, second = call(
         pack_x_kernel,
         (f32(CX, *plane), f32(3, CX, *plane), slab_x, slab_x),
-        [VMEM] * 5 + [ANY],
+        [VMEM] * 5,
         (VMEM,) * 4,
         [],
-    )(den, f, mask, first, second, w)
+    )(den, f, mask, first, second)
     first, second = swap(first, second, GX, DEV_X)
-    stiff, coef, image, sums = call(
+    w, stiff, coef, image, sums, rwt = call(
         inner_kernel,
-        (f32(14, *plane), f32(14, *plane), f32(3, 12, *plane), f32(4, 8, CZ)),
-        [SMEM, VMEM, VMEM, VMEM],
-        (VMEM,) * 4,
+        (f32(128), f32(14, *plane), f32(14, *plane), f32(3, 12, *plane), f32(4, 8, CZ), f32(3, *plane)),
+        [SMEM, VMEM, VMEM],
+        (SMEM,) + (VMEM,) * 5,
         [],
         pl.CostEstimate(flops=8_000_000, bytes_accessed=8_000_000, transcendentals=0),
-    )(w, rwt, dext, fext)
+    )(pltpu.with_memory_space_constraint(offsets.T, pltpu.HBM), dext, fext)
     rims = []
     for k, slab in enumerate((first, second)):
         image_rim, coef_rim, f_rim, sums = call(

time: 72.6 us -> 72.8 us (level)
  blocking collectives: 43.4 us -> 44.4 us
    all_to_all x2, blocking collectives: 43.4 us -> 44.4 us  [spread_sum(): return lax.all_to_all(lines, axes, 0, 0, tiled=True)]
    pallas_call x2 -> x1, Pallas kernels: 3.86 us -> 3.3 us  [body(): call(inner_kernel, (f32(128), f32(14, *plane), f32(14, *plane), f32(3, 12...]
  transfers between devices with their start and end apart: 4 -> 4, of which waited for: 1 -> 2; matrix products, arithmetic and copies ran while one was open for 0% -> 0% of each run, Pallas kernels for 7% -> 6%
where the time goes in v7:
time: 72.8 us; the launch traced here: 72.5 us
  blocking collectives  44.4 us (61%)
  starting transfers between devices  15.7 us (22%)
  Pallas kernels  9.11 us (13%)
  waiting for transfers between devices  2.54 us (3%)
  between operations  0.73 us (1%)
    all_to_all x2, blocking collectives, spread_sum(): return lax.all_to_all(lines, axes, 0, 0, tiled=True)  44.4 us
    ppermute x4, starting transfers between devices, swap(): got.append(lax.ppermute(slab, axes, pairs + [(b, a) for a, b in pairs]))  15.7 us
    pallas_call x1, Pallas kernels, body(): call(inner_kernel, (f32(128), f32(14, *plane), f32(14, *plane), f32(3, 12...  3.3 us
    ppermute x4, waiting for transfers between devices, swap(): got.append(lax.ppermute(slab, axes, pairs + [(b, a) for a, b in pairs]))  2.54 us
    pallas_call x2, Pallas kernels, body(): call(functools.partial(rim_kernel, k), (f32(3, 4, *plane), f32(4, *plane)...  2.3 us
    pallas_call x1, Pallas kernels, body(): call(last_kernel, (f32(3, CX, CY, CZ), f32(CX, CY, CZ)), [ANY] + [VMEM] *...  2.11 us
  transfers between devices with their start and end apart: 4, of which 2 were waited for; matrix products, arithmetic and copies ran while one was open for 0% of the time, Pallas kernels for 6%

profile of v7, /device:TPU:1, one launch (start us, length us, event | category | flops | bytes accessed | tf_op | source)
XLA Modules:
  0.0 72.5 jit_solution(12319274036604905451)
XLA Ops:
  0.6 1.2 %shard_map.59 = (f32[16,8,256]{2,1,0:T(8,128)S(1)}, f32[3,16,8,256]{3,2,1,0:T(8,128)S(1)}, f32[8,256]{1,0:T(8,128)S(1)}, f32[216,256]{1,0:T(8,128)S(1)}, f32[216,256]{1,0:T(8,128)S(1)}) custom-call(f32[16,8,256]{2,1,0:T(8,128)} %den_hbm.1, f32[3,16,8,256]{3,2,1,0:T(8,128)} %f_hbm.1, s32[1,512]{1,0:T(1,128)} %bitcast.8), custom_call_target="tpu_custom_call" | custom-call | tf_op jit(solution)/shard_map/pallas_call | solution.py:511
  1.8 4.6 %collective-permute-start = (f32[216,256]{1,0:T(8,128)S(1)}, f32[216,256]{1,0:T(8,128)S(1)}, u32[]{:S(2)}, u32[]{:S(2)}) collective-permute-start(f32[216,256]{1,0:T(8,128)S(1)} %get-tuple-element.28), channel_id=1, source_target_pairs={{1,2},{3,4},{5,6},{7,8},{9,10},{11,12},{13,14},{15,16},{17,18},{19... | collective-permute-start | bytes 663560 | tf_op jit(solution)/shard_map/ppermute | solution.py:498
  6.5 8.5 %collective-permute-start.1 = (f32[216,256]{1,0:T(8,128)S(1)}, f32[216,256]{1,0:T(8,128)S(1)}, u32[]{:S(2)}, u32[]{:S(2)}) collective-permute-start(f32[216,256]{1,0:T(8,128)S(1)} %get-tuple-element.29), channel_id=1, source_target_pairs={{0,1},{2,3},{4,5},{6,7},{8,9},{10,11},{12,13},{14,15},{16,17},{18,... | collective-permute-start | bytes 663560 | tf_op jit(solution)/shard_map/ppermute | solution.py:498
  15.0 0.0 collective-permute-done.first_in
  15.0 1.1 %collective-permute-done.1.second_in = f32[216,256]{1,0:T(8,128)S(1)} collective-permute-done((f32[216,256]{1,0:T(8,128)S(1)}, f32[216,256]{1,0:T(8,128)S(1)}, u32[]{:S(2)}, u32[]{:S(2)}) %collective-permute-start.1) | collective-permute-done | bytes 221216 | tf_op jit(solution)/shard_map/ppermute | solution.py:498
  16.0 0.2 shard_map.60
  16.2 0.7 collective-permute-start.2
  16.9 1.9 %collective-permute-start.3 = (f32[23,8,256]{2,1,0:T(8,128)S(1)}, f32[23,8,256]{2,1,0:T(8,128)S(1)}, u32[]{:S(2)}, u32[]{:S(2)}) collective-permute-start(f32[23,8,256]{2,1,0:T(8,128)S(1)} %get-tuple-element.42), channel_id=1, source_target_pairs={{0,64},{128,192},{256,320},{384,448},{512,576},{640,704},{64,0},{1... | collective-permute-start | bytes 565256 | tf_op jit(solution)/shard_map/ppermute | solution.py:498
  18.8 3.3 %shard_map.61 = (f32[128]{0:T(128)S(1)}, f32[14,16,256]{2,1,0:T(8,128)S(1)}, f32[14,16,256]{2,1,0:T(8,128)S(1)}, f32[3,12,16,256]{3,2,1,0:T(8,128)S(1)}, f32[4,8...) custom-call(s32[3,14]{1,0:T(4,128)} %bitcast.9, f32[16,16,256]{2,1,0:T(8,128)S(1)} %get-tuple-element.30.dext_ref, ...), custom_call_target="tpu_custom_call" | custom-call | flops 8000000 | bytes 8000000 | tf_op jit(solution)/shard_map/pallas_call | solution.py:527
  22.2 0.0 collective-permute-done.2.slab_ref
  22.2 1.1 %shard_map.62 = (f32[3,4,16,256]{3,2,1,0:T(8,128)S(1)}, f32[4,16,256]{2,1,0:T(8,128)S(1)}, f32[3,2,16,256]{3,2,1,0:T(8,128)S(1)}, f32[4,8,256]{2,1,0:T(8,128)S(1)}) custom-call(f32[128]{0:T(128)S(1)} %get-tuple-element.32.w_in, f32[16,16,256]{2,1,0:T(8,128)S(1)} %get-tuple-element.30.dext_ref, f32[3,16,16,256]{3,2,1,0:T(8,128)S(1)} %get-tuple-element.31.fext_ref, ...), custom_call_target="tpu_custom_call" | custom-call | tf_op jit(solution)/shard_map/pallas_call | solution.py:537
  23.3 1.5 %collective-permute-done.3.slab_ref = f32[23,8,256]{2,1,0:T(8,128)S(1)} collective-permute-done((f32[23,8,256]{2,1,0:T(8,128)S(1)}, f32[23,8,256]{2,1,0:T(8,128)S(1)}, u32[]{:S(2)}, u32[]{:S(2)}) %collective-permute-start.3) | collective-permute-done | bytes 188448 | tf_op jit(solution)/shard_map/ppermute | solution.py:498
  24.7 1.2 %shard_map.63 = (f32[3,4,16,256]{3,2,1,0:T(8,128)S(1)}, f32[4,16,256]{2,1,0:T(8,128)S(1)}, f32[3,2,16,256]{3,2,1,0:T(8,128)S(1)}, f32[1,128]{1,0:T(1,128)S(1)}) custom-call(f32[128]{0:T(128)S(1)} %get-tuple-element.32.w_in, f32[16,16,256]{2,1,0:T(8,128)S(1)} %get-tuple-element.30.dext_ref, f32[3,16,16,256]{3,2,1,0:T(8,128)S(1)} %get-tuple-element.31.fext_ref, ...), custom_call_target="tpu_custom_call" | custom-call | tf_op jit(solution)/shard_map/pallas_call | solution.py:537
  26.0 31.3 %all_to_all.14 = f32[24,1,128]{2,1,0:T(1,128)S(1)} all-to-all(f32[24,1,128]{2,1,0:T(1,128)S(1)} %broadcast_in_dim.4), channel_id=1, replica_groups=mesh['zl'=3,'x'=4,'zh'=4,'y'=8,'c'=2] {'zl','zh','c'}, dimensions={0} | all-to-all | bytes 24576 | tf_op jit(solution)/shard_map/all_to_all | solution.py:504
  57.3 13.0 %all_to_all.15 = f32[32,1,128]{2,1,0:T(1,128)S(1)} all-to-all(f32[32,1,128]{2,1,0:T(1,128)S(1)} %broadcast_in_dim.5), channel_id=1, replica_groups=mesh['zl'=3,'x'=4,'zh'=4,'y'=8,'c'=2] {'x','y'}, dimensions={0} | all-to-all | bytes 32768 | tf_op jit(solution)/shard_map/all_to_all | solution.py:504
  70.4 2.1 %shard_map.64 = (f32[3,16,8,256]{3,2,1,0:T(8,128)}, f32[16,8,256]{2,1,0:T(8,128)}) custom-call(f32[128]{0:T(128)S(1)} %get-tuple-element.32.w_in, f32[3,16,16,256]{3,2,1,0:T(8,128)S(1)} %get-tuple-element.31.fext_ref, f32[3,12,16,256]{3,2,1,0:T(8,128)S(1)} %get-tuple-element.33.g_in_ref, f32[14,16,256]{2,1,0:T(8,128)S(1)} %get-tuple-element.34.coef_in_ref, ...), custom_call_target="tpu_custom_call" | custom-call | tf_op jit(solution)/shard_map/pallas_call | solution.py:554
  (3 shorter events, 0.0 us)
Async XLA Ops:
  1.8 13.1 %collective-permute-start = (f32[216,256]{1,0:T(8,128)S(1)}, f32[216,256]{1,0:T(8,128)S(1)}, u32[]{:S(2)}, u32[]{:S(2)}) collective-permute-start(f32[216,256]{1,0:T(8,128)S(1)} %get-tuple-element.28), channel_id=1, source_target_pairs={{1,2},{3,4},{5,6},{7,8},{9,10},{11,12},{13,14},{15,16},{17,18},{19... | collective-permute-start | bytes 663560 | tf_op jit(solution)/shard_map/ppermute | solution.py:498
  6.5 9.6 %collective-permute-start.1 = (f32[216,256]{1,0:T(8,128)S(1)}, f32[216,256]{1,0:T(8,128)S(1)}, u32[]{:S(2)}, u32[]{:S(2)}) collective-permute-start(f32[216,256]{1,0:T(8,128)S(1)} %get-tuple-element.29), channel_id=1, source_target_pairs={{0,1},{2,3},{4,5},{6,7},{8,9},{10,11},{12,13},{14,15},{16,17},{18,... | collective-permute-start | bytes 663560 | tf_op jit(solution)/shard_map/ppermute | solution.py:498
  16.2 5.9 %collective-permute-start.2 = (f32[23,8,256]{2,1,0:T(8,128)S(1)}, f32[23,8,256]{2,1,0:T(8,128)S(1)}, u32[]{:S(2)}, u32[]{:S(2)}) collective-permute-start(f32[23,8,256]{2,1,0:T(8,128)S(1)} %get-tuple-element.35), channel_id=1, source_target_pairs={{64,128},{192,256},{320,384},{448,512},{576,640},{128,64},{256,192... | collective-permute-start | bytes 565256 | tf_op jit(solution)/shard_map/ppermute | solution.py:498
  16.9 7.8 %collective-permute-start.3 = (f32[23,8,256]{2,1,0:T(8,128)S(1)}, f32[23,8,256]{2,1,0:T(8,128)S(1)}, u32[]{:S(2)}, u32[]{:S(2)}) collective-permute-start(f32[23,8,256]{2,1,0:T(8,128)S(1)} %get-tuple-element.42), channel_id=1, source_target_pairs={{0,64},{128,192},{256,320},{384,448},{512,576},{640,704},{64,0},{1... | collective-permute-start | bytes 565256 | tf_op jit(solution)/shard_map/ppermute | solution.py:498
